TPU v7x, 32 devices: a whole 2x2x4 slice. The times are simulated.
32 devices in a mesh: groups: 2 (over x), loop: 16 (over z, y, core).
Axes of the slice: x: 2, y: 2, z: 4, core: 2. Of those that a mesh axis runs over, the one named last changes fastest.
Arguments:
- activations: bfloat16 [5120, 4096], P('loop', 'groups'), parts along dimension 1, may hold values from -6 to 6
- out_grads: bfloat16 [20480, 4096], P('loop', 'groups'), parts along dimension 1, may hold values from -6 to 6
- left_factors: bfloat16 [256, 5120], P('loop'), may hold values from -0.078125 to 0.078125
- right_factors: bfloat16 [256, 20480], P('loop'), may hold values from -0.0390625 to 0.0390625
- token_ids: int32 [4096], P(('groups', 'loop')), parts along dimension 0, may hold values from 0 to 50687
- doc_starts: int32 [4096], P(('groups', 'loop')), parts along dimension 0, may hold values 0 or 1
- token_weights: float32 [50688], replicated, may hold values from 0.25 to 4
Outputs:
- scores: float32 [4096, 8], P(('groups', 'loop')), parts along dimension 0
- doc_influence: float32 [4096, 8], P(('groups', 'loop')), parts along dimension 0
There are 2 independent parts, one for each index of `groups`. A program takes and returns all parts, laid end to end along the dimension named above; an argument that names none is the same for every part. Nothing has to cross between parts.
All inputs are finite; a program needn't handle non-finite values. No bound on the sum of `doc_starts` on one device may be relied on, other than what follows from the above.
Results may differ from a plain program's by a relative error of at most 0.0003.
Values may be sent and summed in bfloat16 or wider, within the bound.
No kernel may reach another device: no remote copies, remote signals or barrier semaphores. Data moves between devices by JAX's collectives and lax.ppermute only.
A program may use at most 128 MiB of HBM per device.

v0:
```python
import jax
import jax.numpy as jnp
from jax import lax
from jax.sharding import PartitionSpec as P

RANK = 32


def carried_in(array, axis, combine, identity):
    devices, index = (lax.axis_size(axis), lax.axis_index(axis))
    everything = jax.tree.map(lambda part: lax.all_gather(part, axis), array)
    start = jax.tree.map(
        lambda part, zero: jnp.broadcast_to(jnp.asarray(zero, part.dtype), part.shape),
        array,
        identity,
    )

    def lap(k, before):
        reached = k < index
        new = combine(before, jax.tree.map(lambda part: part[k], everything))
        return jax.tree.map(lambda a, b: jnp.where(reached, a, b), new, before)

    return lax.fori_loop(0, devices, lap, start)


def merge_docs(earlier, later):
    taken = later[2] > 0
    return (
        jnp.where(taken, later[0], earlier[0] + later[0]),
        jnp.where(taken, later[1], earlier[1] + later[1]),
        jnp.maximum(earlier[2], later[2]),
    )


def project(columns, factors):
    return lax.dot_general(
        columns, factors, (((0,), (1,)), ((), ())), preferred_element_type=jnp.float32
    )


def local(
    activations, out_grads, left_factors, right_factors, token_ids, doc_starts, token_weights
):
    shards = lax.axis_size("loop")
    tok_rows = activations.shape[1] // shards
    left_all, right_all = (
        lax.all_gather(left_factors, "loop", axis=0, tiled=True),
        lax.all_gather(right_factors, "loop", axis=0, tiled=True),
    )
    query_count = left_all.shape[0] // RANK
    act_cols, grad_cols = (
        lax.all_to_all(activations, "loop", split_axis=1, concat_axis=0, tiled=True),
        lax.all_to_all(out_grads, "loop", split_axis=1, concat_axis=0, tiled=True),
    )
    left_proj = project(act_cols, left_all)
    right_proj = project(grad_cols, right_all)
    products = (left_proj * right_proj).reshape(tok_rows, query_count, RANK).sum(axis=-1)
    weights = jnp.take(token_weights, token_ids)
    scores = products * (weights * RANK ** (-0.5))[:, None]
    segment = jnp.cumsum(doc_starts)
    positions = jnp.arange(tok_rows)
    same_doc = (positions[None, :] <= positions[:, None]) & (segment[None, :] == segment[:, None])
    matrix = same_doc.astype(jnp.float32)
    local_sum = jnp.dot(matrix, scores, precision=lax.Precision.HIGHEST)
    local_count = jnp.sum(matrix, axis=1)
    tail_sum = local_sum[-1]
    tail_count = local_count[-1]
    tail_flag = jnp.max(doc_starts).astype(jnp.float32)
    identity = (jnp.zeros_like(tail_sum), jnp.zeros((), jnp.float32), jnp.zeros((), jnp.float32))
    carry_sum, carry_count, carry_flag = carried_in(
        (tail_sum, tail_count, tail_flag), "loop", merge_docs, identity
    )
    leading = (segment == 0).astype(jnp.float32)
    doc_sum = local_sum + leading[:, None] * carry_sum[None, :]
    doc_count = local_count + leading * carry_count
    return (scores, doc_sum / jnp.sqrt(doc_count)[:, None])


def solution(mesh):
    return jax.shard_map(
        local,
        mesh=mesh,
        in_specs=(
            P("loop", "groups"),
            P("loop", "groups"),
            P("loop", None),
            P("loop", None),
            P(("groups", "loop")),
            P(("groups", "loop")),
            P(),
        ),
        out_specs=(P(("groups", "loop"), None), P(("groups", "loop"), None)),
        check_vma=False,
    )
```

profile of v0, /device:TPU:0, one launch (start us, length us, event | category | flops | bytes accessed | tf_op | source)
XLA Modules:
  0.0 351.8 jit_solution(3540749496277134327)
XLA Ops:
  7.2 0.0 copy-start
  7.2 0.0 all-gather.4.cloned.1.call-start
  7.2 0.7 all-gather.4.cloned.1.call-update
  7.9 0.0 all-gather.6.cloned.1.call-start
  8.0 0.7 all-gather.6.cloned.1.call-update
  8.7 1.4 copy_bitcast_fusion
  10.1 7.4 %all-to-all-start = ((bf16[320,16,128]{2,0,1:T(8,128)(2,1)}), bf16[320,16,128]{2,0,1:T(8,128)(2,1)S(1)}, u32[]{:S(2)}, u32[]{:S(2)}) async-start(bf16[320,16,128]{2,0,1:T(8,128)(2,1)} %copy_bitcast_fusion), calls=%async_computation | async-start | bytes 2621440 | tf_op jit(solution)/shard_map/all_to_all | solution.py:52
  17.5 8.0 %copy.31 = bf16[1280,2048]{0,1:T(8,128)(2,1)} copy(bf16[1280,2048]{1,0:T(8,128)(2,1)} %param.10) | data formatting | bytes 10485760 | tf_op args[1]
  25.4 24.7 %all-to-all-done = bf16[320,16,128]{2,0,1:T(8,128)(2,1)S(1)} async-done(((bf16[320,16,128]{2,0,1:T(8,128)(2,1)}), bf16[320,16,128]{2,0,1:T(8,128)(2,1)S(1)}, u32[]{:S(2)}, u32[]{:S(2)}) %all-to-all-start) | async-done | bytes 1310752 | tf_op jit(solution)/shard_map/all_to_all | solution.py:52
  50.1 8.2 %all-to-all-start.1 = ((bf16[1280,16,128]{0,2,1:T(8,128)(2,1)}), bf16[1280,16,128]{0,2,1:T(8,128)(2,1)}, u32[]{:S(2)}, u32[]{:S(2)}) async-start(bf16[1280,16,128]{0,2,1:T(8,128)(2,1)} %bitcast.33), calls=%async_computation.1 | async-start | bytes 10485760 | tf_op jit(solution)/shard_map/all_to_all | solution.py:53
  58.4 0.1 copy.34
  58.5 0.2 reduce-window.7
  58.6 0.1 reduce
  58.7 0.6 reduce_max.9
  60.1 0.6 dynamic-slice
  60.6 0.2 convert_reduce_fusion
  60.8 0.8 slice_dynamic-update-slice_fusion
  61.6 0.8 dynamic-update-slice
  62.4 135.6 %all-reduce.2 = (f32[16]{0:T(128)S(1)}, f32[16]{0:T(128)S(1)}) all-reduce(f32[16]{0:T(128)S(1)} %dynamic-update-slice, f32[16]{0:T(128)S(1)} %slice_dynamic-update-slice_fusion), channel_id=1, replica_groups=mesh['groups'=2,'loop'=16] {'loop'}, use_global_device_ids=true, to_apply=%add | all-reduce | flops 32 | bytes 256
  198.1 1.1 gather_fusion
  199.2 0.0 all-gather.4.cloned.1.call-done
  199.3 2.7 fusion.8
  202.0 7.8 %copy.32 = bf16[16,1280,128]{2,1,0:T(8,128)(2,1)} copy(bf16[16,1280,128]{1,2,0:T(8,128)(2,1)} %bitcast.3) | data formatting | bytes 10485760 | tf_op jit(solution)/shard_map/all_to_all | solution.py:53
  209.9 35.2 %all-gather.6.cloned.1.call-done = bf16[256,20480]{1,0:T(8,128)(2,1)} async-done(((bf16[16,20480]{1,0:T(8,128)(2,1)}), bf16[256,20480]{1,0:T(8,128)(2,1)}) %all-gather.6.cloned.1.call-update) | async-done | bytes 10485776 | tf_op jit(solution)/shard_map/all_gather | solution.py:48
  245.0 9.1 %convolution_multiply_fusion = f32[128,256]{1,0:T(8,128)S(1)} fusion(f32[128,256]{1,0:T(8,128)S(1)} %fusion.8, bf16[20480,128]{1,0:T(8,128)(2,1)} %bitcast.34, bf16[256,20480]{1,0:T(8,128)(2,1)} %all-gather.6.cloned.1.call-done), kind=kOutput, calls=%fused_computation.5 | convolution fusion | flops 1342210048 | bytes 15990784 | tf_op jit(solution)/shard_map/dot_general | solution.py:36
  254.1 0.1 copy.33
  254.2 0.0 copy-start.2
  254.3 0.2 fusion.1
  254.4 0.2 slice_reduce_fusion
  254.7 43.2 %all-gather = f32[16,1,8]{2,1,0:T(1,128)S(1)} all-gather(f32[1,1,8]{2,1,0:T(1,128)S(1)} %bitcast.37), channel_id=1, replica_groups=mesh['groups'=2,'loop'=16] {'loop'}, dimensions={0}, use_global_device_ids=true | all-gather | bytes 544 | tf_op jit(solution)/shard_map/all_gather | solution.py:11
  297.9 46.4 %while.16 = (s32[]{:T(128)}, f32[8]{0:T(128)S(1)}, f32[]{:T(128)}, s32[]{:T(128)}, f32[16]{0:T(128)S(1)}, /*index=5*/f32[16,8]{1,0:T(8,128)S(1)}, f32[16]{0:T(128)S(1)}, s32[]{:T(128)}, f32[1]{0:T(128)}, s32[]{:T(128)}) while((s32[]{:T(128)}, f32[8]{0:T(128)S(1)}, f32[]{:T(128)}, s32[]{:T(128)}, f32[16]{0:T(128)S(1)}, ...), condition=%wide.region_5.6_spmd.clone, body=%wide.region_4.5_spmd.clone.sunk | while | flops 40 | bytes 301 | solution.py:23
  297.9 0.6 dynamic_slice.29
  299.0 0.6 dynamic_slice.30
  300.8 0.6 dynamic_slice.29
  302.0 0.6 dynamic_slice.30
  303.7 0.6 dynamic_slice.29
  304.9 0.6 dynamic_slice.30
  306.6 0.6 dynamic_slice.29
  307.8 0.6 dynamic_slice.30
  309.5 0.6 dynamic_slice.29
  310.7 0.6 dynamic_slice.30
  312.4 0.6 dynamic_slice.29
  313.6 0.6 dynamic_slice.30
  315.3 0.6 dynamic_slice.29
  316.5 0.6 dynamic_slice.30
  318.2 0.6 dynamic_slice.29
  319.4 0.6 dynamic_slice.30
  321.1 0.6 dynamic_slice.29
  322.3 0.6 dynamic_slice.30
  324.0 0.6 dynamic_slice.29
  325.2 0.6 dynamic_slice.30
  326.9 0.6 dynamic_slice.29
  328.1 0.6 dynamic_slice.30
  329.8 0.6 dynamic_slice.29
  331.0 0.6 dynamic_slice.30
  332.7 0.6 dynamic_slice.29
  333.9 0.6 dynamic_slice.30
  335.6 0.6 dynamic_slice.29
  336.8 0.6 dynamic_slice.30
  338.5 0.6 dynamic_slice.29
  339.7 0.6 dynamic_slice.30
  341.4 0.6 dynamic_slice.29
  342.6 0.6 dynamic_slice.30
  344.3 0.7 add_divide_fusion
  (37 shorter events, 0.4 us)
Async XLA Ops:
  7.2 1.5 copy-start
  7.2 192.1 %all-gather.4.cloned.1.call-start = ((), (), s32[]{:S(2)}) async-start(), calls=%async_computation.2 | async-start | bytes 2785280 | tf_op jit(solution)/shard_map/all_gather | solution.py:47
  7.9 237.1 %all-gather.6.cloned.1.call-start = ((), (), s32[]{:S(2)}) async-start(), calls=%async_computation.3 | async-start | bytes 11141120 | tf_op jit(solution)/shard_map/all_gather | solution.py:48
  10.1 40.0 %all-to-all-start = ((bf16[320,16,128]{2,0,1:T(8,128)(2,1)}), bf16[320,16,128]{2,0,1:T(8,128)(2,1)S(1)}, u32[]{:S(2)}, u32[]{:S(2)}) async-start(bf16[320,16,128]{2,0,1:T(8,128)(2,1)} %copy_bitcast_fusion), calls=%async_computation | async-start | bytes 2621440 | tf_op jit(solution)/shard_map/all_to_all | solution.py:52
  50.1 8.2 %copy-start.3 = (s32[128]{0:T(128)S(1)}, s32[128]{0:T(128)}, u32[]{:S(2)}) copy-start(s32[128]{0:T(128)} %param.14) | copy-start | bytes 1540
  50.1 9.9 %copy-start.5 = (u32[32]{0:T(128)S(1)}, u32[32]{0:T(128)}, u32[]{:S(2)}) copy-start(u32[32]{0:T(128)} %constant.64) | copy-start | bytes 388
  50.1 147.9 %copy-start.4 = (s32[128]{0:T(128)S(1)}, s32[128]{0:T(128)}, u32[]{:S(2)}) copy-start(s32[128]{0:T(128)} %param.13) | copy-start | bytes 1540
  50.1 147.9 %copy-start.1 = (f32[50688]{0:T(1024)S(1)}, f32[50688]{0:T(1024)}, u32[]{:S(2)}) copy-start(f32[50688]{0:T(1024)} %param.15) | copy-start | bytes 608260
  50.1 151.9 %all-to-all-start.1 = ((bf16[1280,16,128]{0,2,1:T(8,128)(2,1)}), bf16[1280,16,128]{0,2,1:T(8,128)(2,1)}, u32[]{:S(2)}, u32[]{:S(2)}) async-start(bf16[1280,16,128]{0,2,1:T(8,128)(2,1)} %bitcast.33), calls=%async_computation.1 | async-start | bytes 10485760 | tf_op jit(solution)/shard_map/all_to_all | solution.py:53
  254.2 90.8 %copy-start.2 = (f32[128,8]{0,1:T(8,128)}, f32[128,8]{0,1:T(8,128)S(1)}, u32[]{:S(2)}) copy-start(f32[128,8]{0,1:T(8,128)S(1)} %broadcast_multiply_fusion) | copy-start | bytes 12292
Sparse Core Ops, SparseCore 0:
  10.3 89.4 all-gather.3
  102.0 142.9 all-gather.5
where the time goes:
time: 353 us; the launch traced here: 352 us
  blocking collectives  179 us (51%)
  waiting for transfers between devices  61.2 us (17%)
  local copies, waits for them, and re-layouts  39.6 us (11%)
  loops' own time  27.6 us (8%)
  starting transfers between devices  15.7 us (4%)
  between operations  14.9 us (4%)
  matrix products  12 us (3%)
    unnamed x1, blocking collectives  136 us
    all_gather x1, blocking collectives, carried_in(): everything = jax.tree.map(lambda part: lax.all_gather(part, axis), array)  43.2 us
    all_gather x1, waiting for transfers between devices, local(): lax.all_gather(right_factors, 'loop', axis=0, tiled=True)  35.2 us
    another operation x1, loops' own time, carried_in(): return lax.fori_loop(0, devices, lap, start)  27.6 us
    all_to_all x1, waiting for transfers between devices, local(): lax.all_to_all(activations, 'loop', split_axis=1, concat_axis=0, tiled=True)  24.7 us
    dynamic_slice x32, local copies, waits for them, and re-layouts, lap(): new = combine(before, jax.tree.map(lambda part: part[k], everything))  18.6 us
    dot_general x2, matrix products, project(): lax.dot_general(columns, factors, (((0,), (1,)), ((), ())), preferred_ele...  11.8 us
    unnamed x18, local copies, waits for them, and re-layouts  10.1 us
  transfers between devices with their start and end apart: 4, of which 2 were waited for; matrix products, arithmetic and copies ran while one was open for 7% of the time, Pallas kernels for 0%

commit v1 on v0

v1 whole, which is shorter than its diff:
```python
import functools
import jax
import jax.numpy as jnp
from jax import lax
from jax.experimental import pallas as pl
from jax.experimental.pallas import tpu as pltpu
from jax.sharding import PartitionSpec as P

RANK = 32
LANES = 128
F32 = jnp.float32


def swap(value, axis, offset):
    size = lax.axis_size(axis)
    return lax.ppermute(value, axis, [(i, i ^ offset) for i in range(size)])


def stage_bits(size):
    bits = []
    bit = 4
    while bit < size:
        bits.append(bit)
        bit *= 2
    pairs = [bits[i : i + 2] for i in range(0, len(bits), 2)]
    stages = []
    for pair in pairs:
        offsets = [0]
        for one in pair:
            offsets = offsets + [one | other for other in offsets]
        stages.append(offsets)
    return stages


def block_order(stages):
    order = [0]
    for offsets in stages:
        order = [high | low for high in offsets for low in order]
    return order


def project_kernel(halves, with_add, ids, left, right, acts, grads, *rest):
    outs = rest[1:] if with_add else rest
    a = jnp.dot(left[...], acts[...], preferred_element_type=F32)
    b = jnp.dot(right[...], grads[...], preferred_element_type=F32)
    rows = a.shape[0] // halves
    pieces = []
    for h in range(halves):
        pieces.append(a[h * rows : (h + 1) * rows])
        pieces.append(b[h * rows : (h + 1) * rows])
    for h, piece in enumerate(pieces):
        if with_add:
            piece = piece + rest[0][0, h * rows : (h + 1) * rows, :]
        if len(outs) == 1:
            outs[0][0, h * rows : (h + 1) * rows, :] = piece
        else:
            outs[h // 2][0, (h % 2) * rows : (h % 2 + 1) * rows, :] = piece


def project(ids, left, right, acts, grads, halves, add=None, skip=0, split=False):
    blocks = ids.shape[0]
    rows, left_depth = left.shape
    right_depth = right.shape[1]
    total = 2 * rows
    in_specs = [
        pl.BlockSpec((rows, left_depth), lambda i, ids: (0, 0)),
        pl.BlockSpec((rows, right_depth), lambda i, ids: (0, 0)),
        pl.BlockSpec((left_depth, LANES), lambda i, ids: (0, ids[i])),
        pl.BlockSpec((right_depth, LANES), lambda i, ids: (0, ids[i])),
    ]
    args = [left, right, acts, grads]
    if add is not None:
        in_specs.append(pl.BlockSpec((1, total, LANES), lambda i, ids: (i + skip, 0, 0)))
        args.append(add)
    parts = halves if split else 1
    shape = jax.ShapeDtypeStruct((blocks, total // parts, LANES), F32)
    spec = pl.BlockSpec((1, total // parts, LANES), lambda i, ids: (i, 0, 0))
    return pl.pallas_call(
        functools.partial(project_kernel, halves, add is not None),
        grid_spec=pltpu.PrefetchScalarGridSpec(
            num_scalar_prefetch=1,
            grid=(blocks,),
            in_specs=in_specs,
            out_specs=[spec] * parts,
        ),
        out_shape=[shape] * parts,
        cost_estimate=pl.CostEstimate(
            flops=2 * blocks * LANES * rows * (left_depth + right_depth),
            bytes_accessed=2 * blocks * LANES * (left_depth + right_depth)
            + 4 * blocks * total * LANES,
            transcendentals=0,
        ),
        name="project",
    )(ids, *args)


def merge_kernel(count, *refs):
    ins, outs = refs[:count], refs[count:]
    size = outs[0].shape[0]
    for p, out in enumerate(outs):
        value = ins[0][p * size : (p + 1) * size]
        for other in ins[1:]:
            value = value + other[p * size : (p + 1) * size]
        out[...] = value


def merge(parts, pieces):
    blocks, rows, lanes = parts[0].shape
    shape = jax.ShapeDtypeStruct((blocks // pieces, rows, lanes), F32)
    nbytes = 4 * blocks * rows * lanes * (len(parts) + 1)
    return pl.pallas_call(
        functools.partial(merge_kernel, len(parts)),
        out_shape=[shape] * pieces,
        cost_estimate=pl.CostEstimate(
            flops=nbytes // 4, bytes_accessed=nbytes, transcendentals=0
        ),
        name="merge",
    )(*parts)


def score_kernel(count, queries, *refs):
    ins, out = refs[:count], refs[count]
    value = ins[0][0]
    for other in ins[1:]:
        value = value + other[0]
    half = value.shape[0] // 2
    product = value[:half] * value[half:]
    out[...] = product.reshape(queries, half // queries, LANES).sum(axis=1)


def partial_scores(parts, queries):
    return pl.pallas_call(
        functools.partial(score_kernel, len(parts), queries),
        out_shape=jax.ShapeDtypeStruct((queries, LANES), F32),
        name="partial_scores",
    )(*parts)


def tail_kernel(count, *refs):
    ins = refs[:count]
    weights, same_doc, counts, flag, scores, local, message = refs[count:]
    half = count // 2
    rows = [ins[i][...] + ins[i + half][...] for i in range(half)]
    value = jnp.concatenate(rows, axis=0) * weights[...]
    scores[...] = value
    total = jnp.dot(
        value, same_doc[...], precision=lax.Precision.HIGHEST, preferred_element_type=F32
    )
    local[...] = total
    queries = total.shape[0]
    message[0:queries, :] = total
    message[queries : queries + 1, :] = counts[...]
    message[queries + 1 : queries + 2, :] = flag[...]
    message[queries + 2 :, :] = jnp.zeros_like(message[queries + 2 :, :])


def fold_members(queries, me, refs, shift):
    members = len(refs)
    lane = LANES - 1
    tails = [ref[:, lane : lane + 1] for ref in refs]
    mine = lax.rem(lax.shift_right_logical(me, shift), members)
    before = jnp.zeros_like(tails[0])
    running = jnp.zeros_like(tails[0])
    flag_row = lax.broadcasted_iota(jnp.int32, tails[0].shape, 0) == queries + 1
    for j in range(members):
        before = jnp.where(mine == j, running, before)
        value = tails[0]
        for k in range(1, members):
            value = jnp.where((mine ^ k) == j, tails[k], value)
        flag = value[queries + 1 : queries + 2, :]
        kept = jnp.where(flag > 0, value, value + running)
        running = jnp.where(flag_row, jnp.maximum(value, running), kept)
    return before, running


def group_kernel(queries, shift, count, me, *refs):
    before, running = fold_members(queries, me[0], refs[:count], shift)
    refs[count][...] = jnp.broadcast_to(before, refs[count].shape)
    refs[count + 1][...] = jnp.broadcast_to(running, refs[count + 1].shape)


def fold_group(me, messages, queries, shift):
    shape = jax.ShapeDtypeStruct(messages[0].shape, F32)
    return pl.pallas_call(
        functools.partial(group_kernel, queries, shift, len(messages)),
        in_specs=[pl.BlockSpec(memory_space=pltpu.SMEM)]
        + [pl.BlockSpec(memory_space=pltpu.VMEM)] * len(messages),
        out_shape=[shape] * 2,
        name="fold_group",
    )(me, *messages)


def finish_kernel(queries, count, *refs):
    befores = refs[:count]
    local, counts, leading, out = refs[count:]
    carry = jnp.zeros_like(befores[0][...])
    for ref in befores:
        value = ref[...]
        flag = value[queries + 1 : queries + 2, :]
        carry = jnp.where(flag > 0, value, value + carry)
    lead = leading[...]
    total = local[...] + lead * carry[0:queries, :]
    number = counts[...] + lead * carry[queries : queries + 1, :]
    out[...] = total / jnp.sqrt(number)


def local(
    activations, out_grads, left_factors, right_factors, token_ids, doc_starts, token_weights
):
    size, groups = lax.axis_size("loop"), lax.axis_size("groups")
    me = lax.axis_index("loop").astype(jnp.int32)
    rows = left_factors.shape[0]
    queries = rows * size // RANK
    part = rows // groups
    group = lax.axis_index("groups")
    depths = (left_factors.shape[1] // size, right_factors.shape[1] // size)

    def cut(factors, depth):
        mine = lax.dynamic_slice_in_dim(factors, group * part, part, axis=0)
        return mine.reshape(part, size, depth).swapaxes(0, 1)

    outgoing = jnp.concatenate(
        [cut(left_factors, depths[0]), cut(right_factors, depths[1])], axis=2
    )
    arrived = lax.all_to_all(outgoing, "loop", split_axis=0, concat_axis=0, tiled=True)
    own = arrived.reshape(size * part, sum(depths))
    other = lax.ppermute(own, "groups", [(i, i ^ 1) for i in range(groups)])

    stages = stage_bits(size)
    order = jnp.array(block_order(stages), jnp.int32)
    count = len(block_order(stages))
    ids_core = jnp.concatenate([order ^ 2 ^ 1, order ^ 1]) ^ me
    ids_y = (order ^ 2) ^ me
    ids_own = order ^ me

    halves = 2
    partials = []
    for factors in (own, other):
        left, right = factors[:, : depths[0]], factors[:, depths[0] :]
        (send,) = project(ids_core, left, right, activations, out_grads, halves)
        from_core = swap(send, "loop", 1)
        to_y = project(
            ids_y, left, right, activations, out_grads, halves, add=from_core, split=True
        )
        kept = project(
            ids_own,
            left,
            right,
            activations,
            out_grads,
            halves,
            add=from_core,
            skip=count,
            split=True,
        )
        for h in range(halves):
            values = [kept[h], swap(to_y[h], "loop", 2)]
            for offsets in reversed(stages):
                pieces = merge(values, len(offsets))
                values = [pieces[0]] + [
                    swap(piece, "loop", offset) for piece, offset in zip(pieces[1:], offsets[1:])
                ]
            partials.append(partial_scores(values, queries // halves))

    positions = jnp.arange(LANES)
    segment = jnp.cumsum(doc_starts)
    same_doc = (
        (positions[:, None] <= positions[None, :]) & (segment[:, None] == segment[None, :])
    ).astype(F32)
    local_count = jnp.sum(same_doc, axis=0)[None, :]
    leading = (segment == 0).astype(F32)[None, :]
    flag = jnp.broadcast_to((segment[-1] > 0).astype(F32), (1, LANES))
    weights = (jnp.take(token_weights, token_ids) * RANK ** (-0.5))[None, :]

    tile = jax.ShapeDtypeStruct((queries, LANES), F32)
    scores, local_sum, message = pl.pallas_call(
        functools.partial(tail_kernel, len(partials)),
        out_shape=[tile, tile, jax.ShapeDtypeStruct((2 * queries, LANES), F32)],
        name="tails",
    )(*partials, weights, same_doc, local_count, flag)

    befores = []
    shift = 0
    for offsets in [[0, 1, 2, 3]] + stages:
        messages = [message] + [swap(message, "loop", offset) for offset in offsets[1:]]
        before, message = fold_group(me.reshape(1), messages, queries, shift)
        befores.insert(0, before)
        shift += len(offsets).bit_length() - 1
    influence = pl.pallas_call(
        functools.partial(finish_kernel, queries, len(befores)),
        out_shape=tile,
        name="finish",
    )(*befores, local_sum, local_count, leading)
    return (scores.T, influence.T)


def solution(mesh):
    return jax.shard_map(
        local,
        mesh=mesh,
        in_specs=(
            P("loop", "groups"),
            P("loop", "groups"),
            P("loop", None),
            P("loop", None),
            P(("groups", "loop")),
            P(("groups", "loop")),
            P(),
        ),
        out_specs=(P(("groups", "loop"), None), P(("groups", "loop"), None)),
        check_vma=False,
    )
```

time: 353 us -> 130 us (0.37)
  blocking collectives: 179 us -> 19.9 us
  waiting for transfers between devices: 61.2 us -> 6.47 us
  Pallas kernels: 0 us -> 53.7 us
  loops' own time: 27.6 us -> 0 us
  local copies, waits for them, and re-layouts: 39.6 us -> 13 us
  starting transfers between devices: 15.7 us -> 29.5 us
  between operations: 14.9 us -> 1.52 us
  matrix products: 12 us -> 0 us
    unnamed x1 -> x0, blocking collectives: 136 us -> none
    pallas_call x0 -> x18, Pallas kernels: none -> 53.7 us  [the longest x6 34.7 us: project(): pl.pallas_call(functools.partial(project_kernel, halves, add is not None)...]
    all_gather x1 -> x0, blocking collectives: 43.2 us -> none  [carried_in(): everything = jax.tree.map(lambda part: lax.all_gather(part, axis), array)]
    all_gather x2 -> x0, waiting for transfers between devices: 35.2 us -> none  [the longest x1 35.2 us: local(): lax.all_gather(right_factors, 'loop', axis=0, tiled=True)]
    ppermute x0 -> x25, starting transfers between devices: none -> 29.5 us  [the longest x24 28 us: swap(): return lax.ppermute(value, axis, [(i, i ^ offset) for i in range(size)])]
    another operation x1 -> x0, loops' own time: 27.6 us -> none  [carried_in(): return lax.fori_loop(0, devices, lap, start)]
    all_to_all x2 -> x0, waiting for transfers between devices: 24.7 us -> none  [the longest x1 24.7 us: local(): lax.all_to_all(activations, 'loop', split_axis=1, concat_axis=0, tiled=True)]
    all_to_all x0 -> x1, blocking collectives: none -> 19.9 us  [local(): lax.all_to_all(outgoing, 'loop', split_axis=0, concat_axis=0, tiled=True)]
  transfers between devices with their start and end apart: 4 -> 25, of which waited for: 2 -> 4; matrix products, arithmetic and copies ran while one was open for 7% -> 7% of each run, Pallas kernels for 0% -> 36%
where the time goes in v1:
time: 130 us; the launch traced here: 128 us
  Pallas kernels  53.7 us (41%)
  starting transfers between devices  29.5 us (23%)
  blocking collectives  19.9 us (15%)
  local copies, waits for them, and re-layouts  13 us (10%)
  waiting for transfers between devices  6.47 us (5%)
  other arithmetic  4.19 us (3%)
  between operations  1.52 us (1%)
    pallas_call x6, Pallas kernels, project(): pl.pallas_call(functools.partial(project_kernel, halves, add is not None)...  34.7 us
    ppermute x24, starting transfers between devices, swap(): return lax.ppermute(value, axis, [(i, i ^ offset) for i in range(size)])  28 us
    all_to_all x1, blocking collectives, local(): lax.all_to_all(outgoing, 'loop', split_axis=0, concat_axis=0, tiled=True)  19.9 us
    pallas_call x4, Pallas kernels, merge(): pl.pallas_call(functools.partial(merge_kernel, len(parts)), out_shape=[sh...  6.98 us
    unnamed x62, local copies, waits for them, and re-layouts  6.5 us
    pallas_call x4, Pallas kernels, partial_scores(): pl.pallas_call(functools.partial(score_kernel, len(parts), queries), out_...  6.14 us
    ppermute x24, waiting for transfers between devices, swap(): return lax.ppermute(value, axis, [(i, i ^ offset) for i in range(size)])  5.7 us
    slice x4, local copies, waits for them, and re-layouts, local(): left, right = (factors[:, :depths[0]], factors[:, depths[0]:])  3.06 us
  transfers between devices with their start and end apart: 25, of which 4 were waited for; matrix products, arithmetic and copies ran while one was open for 7% of the time, Pallas kernels for 36%

profile of v1, /device:TPU:0, one launch (start us, length us, event | category | flops | bytes accessed | tf_op | source)
XLA Modules:
  0.0 128.3 jit_solution(18311217837001930631)
XLA Ops:
  0.7 1.1 copy-done
  1.7 0.9 constant_dynamic-slice_fusion.1
  3.0 19.9 %all_to_all.5 = bf16[16,8,1600]{2,1,0:T(8,128)(2,1)S(1)} all-to-all(bf16[16,8,1600]{2,1,0:T(8,128)(2,1)S(1)} %pad_maximum_fusion), channel_id=1, replica_groups=mesh['groups'=2,'loop'=16] {'loop'}, dimensions={0} | all-to-all | bytes 819200 | tf_op jit(solution)/shard_map/all_to_all | solution.py:225
  22.9 1.5 %collective-permute-start.9 = (bf16[128,1600]{1,0:T(8,128)(2,1)S(1)}, bf16[128,1600]{1,0:T(8,128)(2,1)S(1)}, u32[]{:S(2)}, u32[]{:S(2)}) collective-permute-start(bf16[128,1600]{1,0:T(8,128)(2,1)S(1)} %bitcast.14), channel_id=1, source_target_pairs={{0,16},{16,0},{1,17},{17,1},{2,18},{18,2},{3,19},{19,3},{4,20},{20... | collective-permute-start | bytes 1228808 | tf_op jit(solution)/shard_map/ppermute | solution.py:227
  24.4 0.6 add_xor_fusion.ids
  25.0 0.9 slice.24.right
  25.9 0.6 slice.23.left
  26.5 7.5 %project.6 = f32[8,256,128]{2,1,0:T(8,128)} custom-call(s32[8]{0:T(128)} %add_xor_fusion.ids, bf16[128,320]{1,0:T(8,128)(2,1)} %slice.23.left, bf16[128,1280]{1,0:T(8,128)(2,1)} %slice.24.right, bf16[320,2048]{1,0:T(8,128)(2,1)} %acts.11, bf16[1280,2048]{1,0:T(8,128)(2,1)} %grads.11), custom_call_target="tpu_custom_call" | custom-call | flops 419430400 | bytes 4325376 | tf_op jit(solution)/shard_map/project/pallas_call | solution.py:78
  34.0 0.8 collective-permute-done.9
  34.7 0.9 slice.26.right
  35.6 0.6 slice.25.left
  36.3 7.5 %project.9 = f32[8,256,128]{2,1,0:T(8,128)} custom-call(s32[8]{0:T(128)} %add_xor_fusion.ids, bf16[128,320]{1,0:T(8,128)(2,1)} %slice.25.left, bf16[128,1280]{1,0:T(8,128)(2,1)} %slice.26.right, bf16[320,2048]{1,0:T(8,128)(2,1)} %acts.11, bf16[1280,2048]{1,0:T(8,128)(2,1)} %grads.11), custom_call_target="tpu_custom_call" | custom-call | flops 419430400 | bytes 4325376 | tf_op jit(solution)/shard_map/project/pallas_call | solution.py:78
  44.2 0.5 fusion.3
  44.7 0.7 fusion.1.refs_5_
  45.4 1.0 copy-done.2
  46.4 4.9 %project.8 = (f32[4,128,128]{2,1,0:T(8,128)}, f32[4,128,128]{2,1,0:T(8,128)}) custom-call(s32[4]{0:T(128)} %get-tuple-element.63.ids, bf16[128,320]{1,0:T(8,128)(2,1)} %slice.23.left, bf16[128,1280]{1,0:T(8,128)(2,1)} %slice.24.right, bf16[320,2048]{1,0:T(8,128)(2,1)} %acts.11, bf16[1280,2048]{1,0:T(8,128)(2,1)} %grads.11, f32[8,256,128]{2,1,0:T(8,128)} %copy-done.2), custom_call_target="tpu_custom_call" | custom-call | flops 209715200 | bytes 2162688 | tf_op jit(solution)/shard_map/project/pallas_call | solution.py:78
  51.3 1.0 collective-permute-start.5
  52.2 1.1 collective-permute-start.1
  53.4 1.0 copy-done.1
  54.4 4.9 %project.11 = (f32[4,128,128]{2,1,0:T(8,128)}, f32[4,128,128]{2,1,0:T(8,128)}) custom-call(s32[4]{0:T(128)} %get-tuple-element.63.ids, bf16[128,320]{1,0:T(8,128)(2,1)} %slice.25.left, bf16[128,1280]{1,0:T(8,128)(2,1)} %slice.26.right, bf16[320,2048]{1,0:T(8,128)(2,1)} %acts.11, bf16[1280,2048]{1,0:T(8,128)(2,1)} %grads.11, f32[8,256,128]{2,1,0:T(8,128)} %copy-done.1), custom_call_target="tpu_custom_call" | custom-call | flops 209715200 | bytes 2162688 | tf_op jit(solution)/shard_map/project/pallas_call | solution.py:78
  59.3 1.0 collective-permute-start.15
  60.3 1.1 collective-permute-start.11
  61.4 4.9 %project.7 = (f32[4,128,128]{2,1,0:T(8,128)}, f32[4,128,128]{2,1,0:T(8,128)}) custom-call(s32[4]{0:T(128)} %get-tuple-element.62.ids, bf16[128,320]{1,0:T(8,128)(2,1)} %slice.23.left, bf16[128,1280]{1,0:T(8,128)(2,1)} %slice.24.right, bf16[320,2048]{1,0:T(8,128)(2,1)} %acts.11, bf16[1280,2048]{1,0:T(8,128)(2,1)} %grads.11, f32[8,256,128]{2,1,0:T(8,128)} %copy-done.2), custom_call_target="tpu_custom_call" | custom-call | flops 209715200 | bytes 2162688 | tf_op jit(solution)/shard_map/project/pallas_call | solution.py:78
  66.3 0.7 copy-done.7
  67.0 1.8 %merge.5 = (f32[1,128,128]{2,1,0:T(8,128)}, f32[1,128,128]{2,1,0:T(8,128)}, f32[1,128,128]{2,1,0:T(8,128)}, f32[1,128,128]{2,1,0:T(8,128)}) custom-call(f32[4,128,128]{2,1,0:T(8,128)} %get-tuple-element.38.refs_0_, f32[4,128,128]{2,1,0:T(8,128)} %copy-done.7), custom_call_target="tpu_custom_call" | custom-call | flops 196608 | bytes 786432 | tf_op jit(solution)/shard_map/merge/pallas_call | solution.py:111
  68.8 1.3 %collective-permute-start.6 = (f32[1,128,128]{2,1,0:T(8,128)}, f32[1,128,128]{2,1,0:T(8,128)S(1)}, u32[]{:S(2)}, u32[]{:S(2)}) collective-permute-start(f32[1,128,128]{2,1,0:T(8,128)} %get-tuple-element.41), channel_id=1, source_target_pairs={{0,4},{1,5},{2,6},{3,7},{4,0},{5,1},{6,2},{7,3},{8,12},{9,13},{10,... | collective-permute-start | bytes 196616 | tf_op jit(solution)/shard_map/ppermute | solution.py:16
  70.1 0.9 collective-permute-start.7
  71.0 1.1 gather_fusion
  72.2 2.2 %collective-permute-start.8 = (f32[1,128,128]{2,1,0:T(8,128)}, f32[1,128,128]{2,1,0:T(8,128)S(1)}, u32[]{:S(2)}, u32[]{:S(2)}) collective-permute-start(f32[1,128,128]{2,1,0:T(8,128)} %get-tuple-element.43), channel_id=1, source_target_pairs={{0,12},{1,13},{2,14},{3,15},{4,8},{5,9},{6,10},{7,11},{8,4},{9,5},... | collective-permute-start | bytes 196616 | tf_op jit(solution)/shard_map/ppermute | solution.py:16
  74.4 1.7 %merge.4 = (f32[1,128,128]{2,1,0:T(8,128)}, f32[1,128,128]{2,1,0:T(8,128)}, f32[1,128,128]{2,1,0:T(8,128)}, f32[1,128,128]{2,1,0:T(8,128)}) custom-call(f32[4,128,128]{2,1,0:T(8,128)} %get-tuple-element.32.refs_0_, f32[4,128,128]{2,1,0:T(8,128)} %copy-done.6), custom_call_target="tpu_custom_call" | custom-call | flops 196608 | bytes 786432 | tf_op jit(solution)/shard_map/merge/pallas_call | solution.py:111
  76.1 5.1 %project.10 = (f32[4,128,128]{2,1,0:T(8,128)}, f32[4,128,128]{2,1,0:T(8,128)}) custom-call(s32[4]{0:T(128)} %get-tuple-element.62.ids, bf16[128,320]{1,0:T(8,128)(2,1)} %slice.25.left, bf16[128,1280]{1,0:T(8,128)(2,1)} %slice.26.right, bf16[320,2048]{1,0:T(8,128)(2,1)} %acts.11, bf16[1280,2048]{1,0:T(8,128)(2,1)} %grads.11, f32[8,256,128]{2,1,0:T(8,128)} %copy-done.1), custom_call_target="tpu_custom_call" | custom-call | flops 209715200 | bytes 2162688 | tf_op jit(solution)/shard_map/project/pallas_call | solution.py:78
  81.2 0.5 collective-permute-start.2
  81.9 1.7 %merge.7 = (f32[1,128,128]{2,1,0:T(8,128)}, f32[1,128,128]{2,1,0:T(8,128)}, f32[1,128,128]{2,1,0:T(8,128)}, f32[1,128,128]{2,1,0:T(8,128)}) custom-call(f32[4,128,128]{2,1,0:T(8,128)} %get-tuple-element.50.refs_0_, f32[4,128,128]{2,1,0:T(8,128)} %copy-done.5), custom_call_target="tpu_custom_call" | custom-call | flops 196608 | bytes 786432 | tf_op jit(solution)/shard_map/merge/pallas_call | solution.py:111
  83.7 1.7 %collective-permute-start.3 = (f32[1,128,128]{2,1,0:T(8,128)S(1)}, f32[1,128,128]{2,1,0:T(8,128)S(1)}, u32[]{:S(2)}, u32[]{:S(2)}) collective-permute-start(f32[1,128,128]{2,1,0:T(8,128)S(1)} %copy-done.28), channel_id=1, source_target_pairs={{0,8},{1,9},{2,10},{3,11},{4,12},{5,13},{6,14},{7,15},{8,0},{9,1},... | collective-permute-start | bytes 196616 | tf_op jit(solution)/shard_map/ppermute | solution.py:16
  85.4 2.2 %collective-permute-start.4 = (f32[1,128,128]{2,1,0:T(8,128)S(1)}, f32[1,128,128]{2,1,0:T(8,128)S(1)}, u32[]{:S(2)}, u32[]{:S(2)}) collective-permute-start(f32[1,128,128]{2,1,0:T(8,128)S(1)} %copy-done.27), channel_id=1, source_target_pairs={{0,12},{1,13},{2,14},{3,15},{4,8},{5,9},{6,10},{7,11},{8,4},{9,5},... | collective-permute-start | bytes 196616 | tf_op jit(solution)/shard_map/ppermute | solution.py:16
  87.6 0.6 multiply_bitcast_fusion.refs_4_
  88.2 0.5 slice.27
  89.4 1.8 %merge.6 = (f32[1,128,128]{2,1,0:T(8,128)}, f32[1,128,128]{2,1,0:T(8,128)}, f32[1,128,128]{2,1,0:T(8,128)}, f32[1,128,128]{2,1,0:T(8,128)}) custom-call(f32[4,128,128]{2,1,0:T(8,128)} %get-tuple-element.44.refs_0_, f32[4,128,128]{2,1,0:T(8,128)} %copy-done.4), custom_call_target="tpu_custom_call" | custom-call | flops 196608 | bytes 786432 | tf_op jit(solution)/shard_map/merge/pallas_call | solution.py:111
  91.1 2.2 %collective-permute-start.17 = (f32[1,128,128]{2,1,0:T(8,128)}, f32[1,128,128]{2,1,0:T(8,128)S(1)}, u32[]{:S(2)}, u32[]{:S(2)}) collective-permute-start(f32[1,128,128]{2,1,0:T(8,128)} %get-tuple-element.54), channel_id=1, source_target_pairs={{0,8},{1,9},{2,10},{3,11},{4,12},{5,13},{6,14},{7,15},{8,0},{9,1},... | collective-permute-start | bytes 196616 | tf_op jit(solution)/shard_map/ppermute | solution.py:16
  93.4 2.2 %collective-permute-start.18 = (f32[1,128,128]{2,1,0:T(8,128)}, f32[1,128,128]{2,1,0:T(8,128)S(1)}, u32[]{:S(2)}, u32[]{:S(2)}) collective-permute-start(f32[1,128,128]{2,1,0:T(8,128)} %get-tuple-element.55), channel_id=1, source_target_pairs={{0,12},{1,13},{2,14},{3,15},{4,8},{5,9},{6,10},{7,11},{8,4},{9,5},... | collective-permute-start | bytes 196616 | tf_op jit(solution)/shard_map/ppermute | solution.py:16
  95.6 2.2 %collective-permute-start.13 = (f32[1,128,128]{2,1,0:T(8,128)}, f32[1,128,128]{2,1,0:T(8,128)S(1)}, u32[]{:S(2)}, u32[]{:S(2)}) collective-permute-start(f32[1,128,128]{2,1,0:T(8,128)} %get-tuple-element.48), channel_id=1, source_target_pairs={{0,8},{1,9},{2,10},{3,11},{4,12},{5,13},{6,14},{7,15},{8,0},{9,1},... | collective-permute-start | bytes 196616 | tf_op jit(solution)/shard_map/ppermute | solution.py:16
  97.8 2.2 %collective-permute-start.14 = (f32[1,128,128]{2,1,0:T(8,128)}, f32[1,128,128]{2,1,0:T(8,128)S(1)}, u32[]{:S(2)}, u32[]{:S(2)}) collective-permute-start(f32[1,128,128]{2,1,0:T(8,128)} %get-tuple-element.49), channel_id=1, source_target_pairs={{0,12},{1,13},{2,14},{3,15},{4,8},{5,9},{6,10},{7,11},{8,4},{9,5},... | collective-permute-start | bytes 196616 | tf_op jit(solution)/shard_map/ppermute | solution.py:16
  100.0 0.6 fusion.2
  100.6 1.5 %partial_scores.5.refs_1_ = f32[4,128]{1,0:T(4,128)} custom-call(f32[1,128,128]{2,1,0:T(8,128)} %get-tuple-element.40.refs_0_, f32[1,128,128]{2,1,0:T(8,128)} %copy-done.8, f32[1,128,128]{2,1,0:T(8,128)} %copy-done.9, f32[1,128,128]{2,1,0:T(8,128)} %copy-done.10), custom_call_target="tpu_custom_call" | custom-call | tf_op jit(solution)/shard_map/partial_scores/pallas_call | solution.py:132
  102.1 1.5 %partial_scores.4.refs_0_ = f32[4,128]{1,0:T(4,128)} custom-call(f32[1,128,128]{2,1,0:T(8,128)} %get-tuple-element.34.refs_0_, f32[1,128,128]{2,1,0:T(8,128)} %copy-done.11, f32[1,128,128]{2,1,0:T(8,128)} %copy-done.12, f32[1,128,128]{2,1,0:T(8,128)} %copy-done.14), custom_call_target="tpu_custom_call" | custom-call | tf_op jit(solution)/shard_map/partial_scores/pallas_call | solution.py:132
  103.7 0.6 copy-done.16
  104.3 1.5 %partial_scores.7.refs_3_ = f32[4,128]{1,0:T(4,128)} custom-call(f32[1,128,128]{2,1,0:T(8,128)} %get-tuple-element.52.refs_0_, f32[1,128,128]{2,1,0:T(8,128)} %copy-done.13, f32[1,128,128]{2,1,0:T(8,128)} %copy-done.16, f32[1,128,128]{2,1,0:T(8,128)} %copy-done.18), custom_call_target="tpu_custom_call" | custom-call | tf_op jit(solution)/shard_map/partial_scores/pallas_call | solution.py:132
  105.9 0.6 copy-done.15
  106.5 1.5 %partial_scores.6.refs_2_ = f32[4,128]{1,0:T(4,128)} custom-call(f32[1,128,128]{2,1,0:T(8,128)} %get-tuple-element.46.refs_0_, f32[1,128,128]{2,1,0:T(8,128)} %copy-done.15, f32[1,128,128]{2,1,0:T(8,128)} %copy-done.17, f32[1,128,128]{2,1,0:T(8,128)} %copy-done.19), custom_call_target="tpu_custom_call" | custom-call | tf_op jit(solution)/shard_map/partial_scores/pallas_call | solution.py:132
  108.1 0.6 broadcast_in_dim.28.refs_7_
  108.7 1.6 %tails.1 = (f32[8,128]{1,0:T(8,128)}, f32[8,128]{1,0:T(8,128)}, f32[16,128]{1,0:T(8,128)}) custom-call(f32[4,128]{1,0:T(4,128)} %partial_scores.4.refs_0_, f32[4,128]{1,0:T(4,128)} %partial_scores.5.refs_1_, f32[4,128]{1,0:T(4,128)} %partial_scores.6.refs_2_, f32[4,128]{1,0:T(4,128)} %partial_scores.7.refs_3_, f32[1,128]{1,0:T(1,128)} %multiply_bitcast_fusion.refs_4_, ...), custom_call_target="tpu_custom_call" | custom-call | tf_op jit(solution)/shard_map/tails/pallas_call | solution.py:276
  110.3 0.9 collective-permute-start.20
  111.2 0.9 collective-permute-start.21
  112.1 2.0 %collective-permute-done.20.refs_2_ = f32[16,128]{1,0:T(8,128)S(1)} collective-permute-done((f32[16,128]{1,0:T(8,128)}, f32[16,128]{1,0:T(8,128)S(1)}, u32[]{:S(2)}, u32[]{:S(2)}) %collective-permute-start.20) | collective-permute-done | bytes 8224 | tf_op jit(solution)/shard_map/ppermute | solution.py:16
  114.1 0.3 collective-permute-done.21.refs_3_
  114.7 0.3 copy-done.25
  115.1 1.4 %fold_group.2 = (f32[16,128]{1,0:T(8,128)}, f32[16,128]{1,0:T(8,128)}) custom-call(s32[1]{0:T(128)} %bitcast.9.me, f32[16,128]{1,0:T(8,128)} %get-tuple-element.57.refs_0_, f32[16,128]{1,0:T(8,128)} %copy-done.21, f32[16,128]{1,0:T(8,128)} %copy-done.23, f32[16,128]{1,0:T(8,128)} %copy-done.25), custom_call_target="tpu_custom_call" | custom-call | tf_op jit(solution)/shard_map/fold_group/pallas_call | solution.py:184
  116.5 2.7 %collective-permute-start.23 = (f32[16,128]{1,0:T(8,128)}, f32[16,128]{1,0:T(8,128)S(1)}, u32[]{:S(2)}, u32[]{:S(2)}) collective-permute-start(f32[16,128]{1,0:T(8,128)} %get-tuple-element.58.refs_0_), channel_id=1, source_target_pairs={{0,8},{1,9},{2,10},{3,11},{4,12},{5,13},{6,14},{7,15},{8,0},{9,1},... | collective-permute-start | bytes 24584 | tf_op jit(solution)/shard_map/ppermute | solution.py:16
  119.2 1.7 %collective-permute-start.24 = (f32[16,128]{1,0:T(8,128)}, f32[16,128]{1,0:T(8,128)S(1)}, u32[]{:S(2)}, u32[]{:S(2)}) collective-permute-start(f32[16,128]{1,0:T(8,128)} %get-tuple-element.58.refs_0_), channel_id=1, source_target_pairs={{0,12},{1,13},{2,14},{3,15},{4,8},{5,9},{6,10},{7,11},{8,4},{9,5},... | collective-permute-start | bytes 24584 | tf_op jit(solution)/shard_map/ppermute | solution.py:16
  120.9 0.7 convert_reduce_fusion
  121.6 3.3 %collective-permute-done.24.refs_3_ = f32[16,128]{1,0:T(8,128)S(1)} collective-permute-done((f32[16,128]{1,0:T(8,128)}, f32[16,128]{1,0:T(8,128)S(1)}, u32[]{:S(2)}, u32[]{:S(2)}) %collective-permute-start.24) | collective-permute-done | bytes 8224 | tf_op jit(solution)/shard_map/ppermute | solution.py:16
  124.9 0.6 copy-done.24
  125.5 1.4 %fold_group.3 = (f32[16,128]{1,0:T(8,128)}, f32[16,128]{1,0:T(8,128)}) custom-call(s32[1]{0:T(128)} %bitcast.9.me, f32[16,128]{1,0:T(8,128)} %get-tuple-element.58.refs_0_, f32[16,128]{1,0:T(8,128)} %copy-done.20, f32[16,128]{1,0:T(8,128)} %copy-done.22, f32[16,128]{1,0:T(8,128)} %copy-done.24), custom_call_target="tpu_custom_call" | custom-call | tf_op jit(solution)/shard_map/fold_group/pallas_call | solution.py:184
  126.9 1.3 %finish.1 = f32[8,128]{1,0:T(8,128)} custom-call(f32[16,128]{1,0:T(8,128)} %get-tuple-element.59.refs_0_, f32[16,128]{1,0:T(8,128)} %get-tuple-element.60.refs_1_, f32[8,128]{1,0:T(8,128)} %get-tuple-element.61.refs_2_, f32[1,128]{1,0:T(1,128)} %bitcast.21, f32[1,128]{1,0:T(1,128)} %bitcast.22), custom_call_target="tpu_custom_call" | custom-call | tf_op jit(solution)/shard_map/finish/pallas_call | solution.py:289
  (91 shorter events, 1.5 us)
Async XLA Ops:
  0.6 1.1 copy-start
  22.9 11.8 %collective-permute-start.9 = (bf16[128,1600]{1,0:T(8,128)(2,1)S(1)}, bf16[128,1600]{1,0:T(8,128)(2,1)S(1)}, u32[]{:S(2)}, u32[]{:S(2)}) collective-permute-start(bf16[128,1600]{1,0:T(8,128)(2,1)S(1)} %bitcast.14), channel_id=1, source_target_pairs={{0,16},{16,0},{1,17},{17,1},{2,18},{18,2},{3,19},{19,3},{4,20},{20... | collective-permute-start | bytes 1228808 | tf_op jit(solution)/shard_map/ppermute | solution.py:227
  34.0 9.8 %copy-start.26 = (s32[128]{0:T(128)S(1)}, s32[128]{0:T(128)}, u32[]{:S(2)}) copy-start(s32[128]{0:T(128)} %param.13) | copy-start | bytes 1540
  34.0 11.4 %collective-permute-start = (f32[8,256,128]{2,1,0:T(8,128)}, f32[8,256,128]{2,1,0:T(8,128)S(1)}, u32[]{:S(2)}, u32[]{:S(2)}) collective-permute-start(f32[8,256,128]{2,1,0:T(8,128)} %project.6), channel_id=1, source_target_pairs={{0,1},{1,0},{2,3},{3,2},{4,5},{5,4},{6,7},{7,6},{8,9},{9,8},{10,11... | collective-permute-start | bytes 3145736 | tf_op jit(solution)/shard_map/ppermute | solution.py:16
  43.8 9.6 %collective-permute-start.10 = (f32[8,256,128]{2,1,0:T(8,128)}, f32[8,256,128]{2,1,0:T(8,128)S(1)}, u32[]{:S(2)}, u32[]{:S(2)}) collective-permute-start(f32[8,256,128]{2,1,0:T(8,128)} %project.9), channel_id=1, source_target_pairs={{0,1},{1,0},{2,3},{3,2},{4,5},{5,4},{6,7},{7,6},{8,9},{9,8},{10,11... | collective-permute-start | bytes 3145736 | tf_op jit(solution)/shard_map/ppermute | solution.py:16
  45.4 1.0 copy-start.2
  51.3 10.1 %copy-start.30 = (s32[128]{0:T(128)S(1)}, s32[128]{0:T(128)}, u32[]{:S(2)}) copy-start(s32[128]{0:T(128)} %param.12) | copy-start | bytes 1540
  51.3 15.0 %collective-permute-start.5 = (f32[4,128,128]{2,1,0:T(8,128)}, f32[4,128,128]{2,1,0:T(8,128)S(1)}, u32[]{:S(2)}, u32[]{:S(2)}) collective-permute-start(f32[4,128,128]{2,1,0:T(8,128)} %get-tuple-element.39), channel_id=1, source_target_pairs={{0,2},{1,3},{2,0},{3,1},{4,6},{5,7},{6,4},{7,5},{8,10},{9,11},{10,... | collective-permute-start | bytes 786440 | tf_op jit(solution)/shard_map/ppermute | solution.py:16
  52.2 19.9 %collective-permute-start.1 = (f32[4,128,128]{2,1,0:T(8,128)}, f32[4,128,128]{2,1,0:T(8,128)S(1)}, u32[]{:S(2)}, u32[]{:S(2)}) collective-permute-start(f32[4,128,128]{2,1,0:T(8,128)} %get-tuple-element.33), channel_id=1, source_target_pairs={{0,2},{1,3},{2,0},{3,1},{4,6},{5,7},{6,4},{7,5},{8,10},{9,11},{10,... | collective-permute-start | bytes 786440 | tf_op jit(solution)/shard_map/ppermute | solution.py:16
  53.4 1.0 copy-start.1
  59.3 11.7 %copy-start.3 = (f32[50688]{0:T(1024)S(1)}, f32[50688]{0:T(1024)}, u32[]{:S(2)}) copy-start(f32[50688]{0:T(1024)} %param.14) | copy-start | bytes 608260
  59.3 21.9 %collective-permute-start.15 = (f32[4,128,128]{2,1,0:T(8,128)}, f32[4,128,128]{2,1,0:T(8,128)S(1)}, u32[]{:S(2)}, u32[]{:S(2)}) collective-permute-start(f32[4,128,128]{2,1,0:T(8,128)} %get-tuple-element.51), channel_id=1, source_target_pairs={{0,2},{1,3},{2,0},{3,1},{4,6},{5,7},{6,4},{7,5},{8,10},{9,11},{10,... | collective-permute-start | bytes 786440 | tf_op jit(solution)/shard_map/ppermute | solution.py:16
  60.3 27.3 %collective-permute-start.11 = (f32[4,128,128]{2,1,0:T(8,128)}, f32[4,128,128]{2,1,0:T(8,128)S(1)}, u32[]{:S(2)}, u32[]{:S(2)}) collective-permute-start(f32[4,128,128]{2,1,0:T(8,128)} %get-tuple-element.45), channel_id=1, source_target_pairs={{0,2},{1,3},{2,0},{3,1},{4,6},{5,7},{6,4},{7,5},{8,10},{9,11},{10,... | collective-permute-start | bytes 786440 | tf_op jit(solution)/shard_map/ppermute | solution.py:16
  66.3 0.7 copy-start.7
  68.8 14.9 %collective-permute-start.6 = (f32[1,128,128]{2,1,0:T(8,128)}, f32[1,128,128]{2,1,0:T(8,128)S(1)}, u32[]{:S(2)}, u32[]{:S(2)}) collective-permute-start(f32[1,128,128]{2,1,0:T(8,128)} %get-tuple-element.41), channel_id=1, source_target_pairs={{0,4},{1,5},{2,6},{3,7},{4,0},{5,1},{6,2},{7,3},{8,12},{9,13},{10,... | collective-permute-start | bytes 196616 | tf_op jit(solution)/shard_map/ppermute | solution.py:16
  70.1 15.3 %collective-permute-start.7 = (f32[1,128,128]{2,1,0:T(8,128)}, f32[1,128,128]{2,1,0:T(8,128)S(1)}, u32[]{:S(2)}, u32[]{:S(2)}) collective-permute-start(f32[1,128,128]{2,1,0:T(8,128)} %get-tuple-element.42), channel_id=1, source_target_pairs={{0,8},{1,9},{2,10},{3,11},{4,12},{5,13},{6,14},{7,15},{8,0},{9,1},... | collective-permute-start | bytes 196616 | tf_op jit(solution)/shard_map/ppermute | solution.py:16
  72.2 2.2 %copy-start.6 = (f32[4,128,128]{2,1,0:T(8,128)}, f32[4,128,128]{2,1,0:T(8,128)S(1)}, u32[]{:S(2)}) copy-start(f32[4,128,128]{2,1,0:T(8,128)S(1)} %collective-permute-done.1.refs_1_) | copy-start | bytes 786436
  72.2 19.0 %collective-permute-start.8 = (f32[1,128,128]{2,1,0:T(8,128)}, f32[1,128,128]{2,1,0:T(8,128)S(1)}, u32[]{:S(2)}, u32[]{:S(2)}) collective-permute-start(f32[1,128,128]{2,1,0:T(8,128)} %get-tuple-element.43), channel_id=1, source_target_pairs={{0,12},{1,13},{2,14},{3,15},{4,8},{5,9},{6,10},{7,11},{8,4},{9,5},... | collective-permute-start | bytes 196616 | tf_op jit(solution)/shard_map/ppermute | solution.py:16
  76.1 5.1 %copy-start.29 = (f32[1,128,128]{2,1,0:T(8,128)S(1)}, f32[1,128,128]{2,1,0:T(8,128)}, u32[]{:S(2)}) copy-start(f32[1,128,128]{2,1,0:T(8,128)} %get-tuple-element.35) | copy-start | bytes 196612
  76.1 7.5 %copy-start.28 = (f32[1,128,128]{2,1,0:T(8,128)S(1)}, f32[1,128,128]{2,1,0:T(8,128)}, u32[]{:S(2)}) copy-start(f32[1,128,128]{2,1,0:T(8,128)} %get-tuple-element.36) | copy-start | bytes 196612
  76.1 9.2 %copy-start.27 = (f32[1,128,128]{2,1,0:T(8,128)S(1)}, f32[1,128,128]{2,1,0:T(8,128)}, u32[]{:S(2)}) copy-start(f32[1,128,128]{2,1,0:T(8,128)} %get-tuple-element.37) | copy-start | bytes 196612
  81.2 0.7 copy-start.5
  81.2 12.1 %collective-permute-start.2 = (f32[1,128,128]{2,1,0:T(8,128)S(1)}, f32[1,128,128]{2,1,0:T(8,128)S(1)}, u32[]{:S(2)}, u32[]{:S(2)}) collective-permute-start(f32[1,128,128]{2,1,0:T(8,128)S(1)} %copy-done.29), channel_id=1, source_target_pairs={{0,4},{1,5},{2,6},{3,7},{4,0},{5,1},{6,2},{7,3},{8,12},{9,13},{10,... | collective-permute-start | bytes 196616 | tf_op jit(solution)/shard_map/ppermute | solution.py:16
  83.7 16.9 %copy-start.8 = (f32[1,128,128]{2,1,0:T(8,128)}, f32[1,128,128]{2,1,0:T(8,128)S(1)}, u32[]{:S(2)}) copy-start(f32[1,128,128]{2,1,0:T(8,128)S(1)} %collective-permute-done.6.refs_1_) | copy-start | bytes 196612
  83.7 11.9 %collective-permute-start.3 = (f32[1,128,128]{2,1,0:T(8,128)S(1)}, f32[1,128,128]{2,1,0:T(8,128)S(1)}, u32[]{:S(2)}, u32[]{:S(2)}) collective-permute-start(f32[1,128,128]{2,1,0:T(8,128)S(1)} %copy-done.28), channel_id=1, source_target_pairs={{0,8},{1,9},{2,10},{3,11},{4,12},{5,13},{6,14},{7,15},{8,0},{9,1},... | collective-permute-start | bytes 196616 | tf_op jit(solution)/shard_map/ppermute | solution.py:16
  85.3 15.3 %copy-start.9 = (f32[1,128,128]{2,1,0:T(8,128)}, f32[1,128,128]{2,1,0:T(8,128)S(1)}, u32[]{:S(2)}) copy-start(f32[1,128,128]{2,1,0:T(8,128)S(1)} %collective-permute-done.7.refs_2_) | copy-start | bytes 196612
  85.4 10.2 %collective-permute-start.4 = (f32[1,128,128]{2,1,0:T(8,128)S(1)}, f32[1,128,128]{2,1,0:T(8,128)S(1)}, u32[]{:S(2)}, u32[]{:S(2)}) collective-permute-start(f32[1,128,128]{2,1,0:T(8,128)S(1)} %copy-done.27), channel_id=1, source_target_pairs={{0,12},{1,13},{2,14},{3,15},{4,8},{5,9},{6,10},{7,11},{8,4},{9,5},... | collective-permute-start | bytes 196616 | tf_op jit(solution)/shard_map/ppermute | solution.py:16
  87.6 1.8 %copy-start.4 = (f32[4,128,128]{2,1,0:T(8,128)}, f32[4,128,128]{2,1,0:T(8,128)S(1)}, u32[]{:S(2)}) copy-start(f32[4,128,128]{2,1,0:T(8,128)S(1)} %collective-permute-done.11.refs_1_) | copy-start | bytes 786436
  87.6 10.2 %collective-permute-start.16 = (f32[1,128,128]{2,1,0:T(8,128)}, f32[1,128,128]{2,1,0:T(8,128)S(1)}, u32[]{:S(2)}, u32[]{:S(2)}) collective-permute-start(f32[1,128,128]{2,1,0:T(8,128)} %get-tuple-element.53), channel_id=1, source_target_pairs={{0,4},{1,5},{2,6},{3,7},{4,0},{5,1},{6,2},{7,3},{8,12},{9,13},{10,... | collective-permute-start | bytes 196616 | tf_op jit(solution)/shard_map/ppermute | solution.py:16
  91.1 9.5 %copy-start.10 = (f32[1,128,128]{2,1,0:T(8,128)}, f32[1,128,128]{2,1,0:T(8,128)S(1)}, u32[]{:S(2)}) copy-start(f32[1,128,128]{2,1,0:T(8,128)S(1)} %collective-permute-done.8.refs_3_) | copy-start | bytes 196612
  91.1 12.5 %collective-permute-start.17 = (f32[1,128,128]{2,1,0:T(8,128)}, f32[1,128,128]{2,1,0:T(8,128)S(1)}, u32[]{:S(2)}, u32[]{:S(2)}) collective-permute-start(f32[1,128,128]{2,1,0:T(8,128)} %get-tuple-element.54), channel_id=1, source_target_pairs={{0,8},{1,9},{2,10},{3,11},{4,12},{5,13},{6,14},{7,15},{8,0},{9,1},... | collective-permute-start | bytes 196616 | tf_op jit(solution)/shard_map/ppermute | solution.py:16
  93.4 8.7 %copy-start.11 = (f32[1,128,128]{2,1,0:T(8,128)}, f32[1,128,128]{2,1,0:T(8,128)S(1)}, u32[]{:S(2)}) copy-start(f32[1,128,128]{2,1,0:T(8,128)S(1)} %collective-permute-done.2.refs_1_) | copy-start | bytes 196612
  93.4 10.3 %collective-permute-start.18 = (f32[1,128,128]{2,1,0:T(8,128)}, f32[1,128,128]{2,1,0:T(8,128)S(1)}, u32[]{:S(2)}, u32[]{:S(2)}) collective-permute-start(f32[1,128,128]{2,1,0:T(8,128)} %get-tuple-element.55), channel_id=1, source_target_pairs={{0,12},{1,13},{2,14},{3,15},{4,8},{5,9},{6,10},{7,11},{8,4},{9,5},... | collective-permute-start | bytes 196616 | tf_op jit(solution)/shard_map/ppermute | solution.py:16
  95.6 6.6 %copy-start.12 = (f32[1,128,128]{2,1,0:T(8,128)}, f32[1,128,128]{2,1,0:T(8,128)S(1)}, u32[]{:S(2)}) copy-start(f32[1,128,128]{2,1,0:T(8,128)S(1)} %collective-permute-done.3.refs_2_) | copy-start | bytes 196612
  95.6 10.3 %collective-permute-start.12 = (f32[1,128,128]{2,1,0:T(8,128)}, f32[1,128,128]{2,1,0:T(8,128)S(1)}, u32[]{:S(2)}, u32[]{:S(2)}) collective-permute-start(f32[1,128,128]{2,1,0:T(8,128)} %get-tuple-element.47), channel_id=1, source_target_pairs={{0,4},{1,5},{2,6},{3,7},{4,0},{5,1},{6,2},{7,3},{8,12},{9,13},{10,... | collective-permute-start | bytes 196616 | tf_op jit(solution)/shard_map/ppermute | solution.py:16
  95.6 6.6 %copy-start.14 = (f32[1,128,128]{2,1,0:T(8,128)}, f32[1,128,128]{2,1,0:T(8,128)S(1)}, u32[]{:S(2)}) copy-start(f32[1,128,128]{2,1,0:T(8,128)S(1)} %collective-permute-done.4.refs_3_) | copy-start | bytes 196612
  95.6 10.3 %collective-permute-start.13 = (f32[1,128,128]{2,1,0:T(8,128)}, f32[1,128,128]{2,1,0:T(8,128)S(1)}, u32[]{:S(2)}, u32[]{:S(2)}) collective-permute-start(f32[1,128,128]{2,1,0:T(8,128)} %get-tuple-element.48), channel_id=1, source_target_pairs={{0,8},{1,9},{2,10},{3,11},{4,12},{5,13},{6,14},{7,15},{8,0},{9,1},... | collective-permute-start | bytes 196616 | tf_op jit(solution)/shard_map/ppermute | solution.py:16
  97.8 5.9 %copy-start.13 = (f32[1,128,128]{2,1,0:T(8,128)}, f32[1,128,128]{2,1,0:T(8,128)S(1)}, u32[]{:S(2)}) copy-start(f32[1,128,128]{2,1,0:T(8,128)S(1)} %collective-permute-done.16.refs_1_) | copy-start | bytes 196612
  97.8 8.1 %collective-permute-start.14 = (f32[1,128,128]{2,1,0:T(8,128)}, f32[1,128,128]{2,1,0:T(8,128)S(1)}, u32[]{:S(2)}, u32[]{:S(2)}) collective-permute-start(f32[1,128,128]{2,1,0:T(8,128)} %get-tuple-element.49), channel_id=1, source_target_pairs={{0,12},{1,13},{2,14},{3,15},{4,8},{5,9},{6,10},{7,11},{8,4},{9,5},... | collective-permute-start | bytes 196616 | tf_op jit(solution)/shard_map/ppermute | solution.py:16
  103.7 0.6 copy-start.16
  103.7 0.6 copy-start.18
  105.9 0.6 copy-start.15
  105.9 0.6 copy-start.17
  105.9 0.7 copy-start.19
  110.3 1.9 %collective-permute-start.19 = (f32[16,128]{1,0:T(8,128)}, f32[16,128]{1,0:T(8,128)S(1)}, u32[]{:S(2)}, u32[]{:S(2)}) collective-permute-start(f32[16,128]{1,0:T(8,128)} %get-tuple-element.57.refs_0_), channel_id=1, source_target_pairs={{0,1},{1,0},{2,3},{3,2},{4,5},{5,4},{6,7},{7,6},{8,9},{9,8},{10,11... | collective-permute-start | bytes 24584 | tf_op jit(solution)/shard_map/ppermute | solution.py:16
  110.3 3.9 %collective-permute-start.20 = (f32[16,128]{1,0:T(8,128)}, f32[16,128]{1,0:T(8,128)S(1)}, u32[]{:S(2)}, u32[]{:S(2)}) collective-permute-start(f32[16,128]{1,0:T(8,128)} %get-tuple-element.57.refs_0_), channel_id=1, source_target_pairs={{0,2},{1,3},{2,0},{3,1},{4,6},{5,7},{6,4},{7,5},{8,10},{9,11},{10,... | collective-permute-start | bytes 24584 | tf_op jit(solution)/shard_map/ppermute | solution.py:16
  111.2 3.3 %collective-permute-start.21 = (f32[16,128]{1,0:T(8,128)}, f32[16,128]{1,0:T(8,128)S(1)}, u32[]{:S(2)}, u32[]{:S(2)}) collective-permute-start(f32[16,128]{1,0:T(8,128)} %get-tuple-element.57.refs_0_), channel_id=1, source_target_pairs={{0,3},{1,2},{2,1},{3,0},{4,7},{5,6},{6,5},{7,4},{8,11},{9,10},{10,... | collective-permute-start | bytes 24584 | tf_op jit(solution)/shard_map/ppermute | solution.py:16
  112.1 2.3 %copy-start.21 = (f32[16,128]{1,0:T(8,128)}, f32[16,128]{1,0:T(8,128)S(1)}, u32[]{:S(2)}) copy-start(f32[16,128]{1,0:T(8,128)S(1)} %collective-permute-done.19.refs_1_) | copy-start | bytes 24580
  114.1 0.6 copy-start.23
  114.5 0.6 copy-start.25
  116.5 5.0 %collective-permute-start.22 = (f32[16,128]{1,0:T(8,128)}, f32[16,128]{1,0:T(8,128)S(1)}, u32[]{:S(2)}, u32[]{:S(2)}) collective-permute-start(f32[16,128]{1,0:T(8,128)} %get-tuple-element.58.refs_0_), channel_id=1, source_target_pairs={{0,4},{1,5},{2,6},{3,7},{4,0},{5,1},{6,2},{7,3},{8,12},{9,13},{10,... | collective-permute-start | bytes 24584 | tf_op jit(solution)/shard_map/ppermute | solution.py:16
  116.5 5.0 %collective-permute-start.23 = (f32[16,128]{1,0:T(8,128)}, f32[16,128]{1,0:T(8,128)S(1)}, u32[]{:S(2)}, u32[]{:S(2)}) collective-permute-start(f32[16,128]{1,0:T(8,128)} %get-tuple-element.58.refs_0_), channel_id=1, source_target_pairs={{0,8},{1,9},{2,10},{3,11},{4,12},{5,13},{6,14},{7,15},{8,0},{9,1},... | collective-permute-start | bytes 24584 | tf_op jit(solution)/shard_map/ppermute | solution.py:16
  119.2 5.7 %collective-permute-start.24 = (f32[16,128]{1,0:T(8,128)}, f32[16,128]{1,0:T(8,128)S(1)}, u32[]{:S(2)}, u32[]{:S(2)}) collective-permute-start(f32[16,128]{1,0:T(8,128)} %get-tuple-element.58.refs_0_), channel_id=1, source_target_pairs={{0,12},{1,13},{2,14},{3,15},{4,8},{5,9},{6,10},{7,11},{8,4},{9,5},... | collective-permute-start | bytes 24584 | tf_op jit(solution)/shard_map/ppermute | solution.py:16
  121.6 3.3 %copy-start.20 = (f32[16,128]{1,0:T(8,128)}, f32[16,128]{1,0:T(8,128)S(1)}, u32[]{:S(2)}) copy-start(f32[16,128]{1,0:T(8,128)S(1)} %collective-permute-done.22.refs_1_) | copy-start | bytes 24580
  121.6 3.3 %copy-start.22 = (f32[16,128]{1,0:T(8,128)}, f32[16,128]{1,0:T(8,128)S(1)}, u32[]{:S(2)}) copy-start(f32[16,128]{1,0:T(8,128)S(1)} %collective-permute-done.23.refs_2_) | copy-start | bytes 24580
  124.9 0.6 copy-start.24

commit v2 on v0

v2 whole, which is shorter than its diff:
```python
import functools
import math
import jax
import jax.numpy as jnp
from jax import lax
from jax.experimental import pallas as pl
from jax.experimental.pallas import tpu as pltpu
from jax.sharding import PartitionSpec as P

RANK = 32
LANES = 128
HALVES = 4
WIDTH = [4, 4, 4, 4]
PIECES = 4
F32 = jnp.float32


def swap(value, axis, offset):
    size = lax.axis_size(axis)
    return lax.ppermute(value, axis, [(i, i ^ offset) for i in range(size)])


def later_stages(size):
    stages = []
    bit = 4
    while bit < size:
        width = min(4, size // bit)
        stages.append([bit * k for k in range(width)])
        bit *= width
    return stages


def place(index, count):
    offset = 0
    bit = 1
    while bit < count:
        offset = offset * 2 + (index // bit) % 2
        bit *= 2
    return 4 * offset


def room(*arrays):
    total = sum(math.prod(a.shape) * jnp.dtype(a.dtype).itemsize for a in arrays)
    return pltpu.CompilerParams(vmem_limit_bytes=total + (4 << 20))


def arrange_kernel(me, acts, grads, *rest):
    outs, sems = rest[:-1], rest[-1]
    depth = grads.shape[0]
    per = outs[0].shape[0]
    half = per * len(outs) // 2

    def copies(piece, i):
        block = piece * per + i
        other_core = 1 - block // half
        near = (block % half) // (half // 2)
        offset = place(block % (half // 2), half // 2) + 2 * (1 - near) + other_core
        start = pl.multiple_of((me[0] ^ offset) * LANES, LANES)
        return [
            pltpu.make_async_copy(
                ref.at[:, pl.ds(start, LANES)],
                outs[piece].at[i, pl.ds(row, ref.shape[0])],
                sems.at[k, block],
            )
            for k, (ref, row) in enumerate(((grads, 0), (acts, depth)))
        ]

    def begin(piece, i, _):
        for copy in copies(piece, i):
            copy.start()
        return 0

    def end(piece, i, _):
        for copy in copies(piece, i):
            copy.wait()
        return 0

    for step in (begin, end):
        for piece in range(len(outs)):
            lax.fori_loop(0, per, functools.partial(step, piece), 0)


def arrange(me, acts, grads):
    blocks = acts.shape[1] // LANES
    shape = (blocks // PIECES, grads.shape[0] + acts.shape[0], LANES)
    return pl.pallas_call(
        arrange_kernel,
        in_specs=[pl.BlockSpec(memory_space=pltpu.SMEM)]
        + [pl.BlockSpec(memory_space=pltpu.HBM)] * 2,
        out_shape=[pltpu.VMEM(shape, acts.dtype)] * PIECES,
        scratch_shapes=[pltpu.SemaphoreType.DMA((2, blocks))],
        compiler_params=pltpu.CompilerParams(vmem_limit_bytes=50 << 20),
        cost_estimate=pl.CostEstimate(
            flops=0, bytes_accessed=4 * (acts.size + grads.size), transcendentals=0
        ),
        name="arrange",
    )(me, acts, grads)


def project_kernel(depths, count, factors, *rest):
    columns, outs = rest[:count], rest[count:]
    blocks = outs[0].shape[0]
    per = columns[0].shape[0]
    halves = len(outs)
    size = factors.shape[0] // halves
    gap, right_depth, left_depth = depths

    def pair(ref, base, i, _):
        left = factors[:, gap : gap + left_depth]
        right = factors[:, 0:right_depth]
        two = range(2)
        acts = jnp.concatenate([ref[2 * i + j, right_depth:] for j in two], axis=1)
        grads = jnp.concatenate([ref[2 * i + j, :right_depth] for j in two], axis=1)
        a = jnp.dot(left, acts, preferred_element_type=F32)
        b = jnp.dot(right, grads, preferred_element_type=F32)
        for h, out in enumerate(outs):
            for side, value in enumerate((a, b)):
                piece = value[h * size : (h + 1) * size]
                for j in two:
                    out[base + 2 * i + j, side * size : (side + 1) * size, :] = piece[
                        :, j * LANES : (j + 1) * LANES
                    ]
        return 0

    for k, ref in enumerate(columns):
        step = functools.partial(pair, ref, k * per)
        lax.fori_loop(0, per // 2, step, 0, unroll=blocks <= 8)


def project(factors, depths, columns, halves):
    blocks = columns[0].shape[0] * len(columns)
    rows = factors.shape[0]
    shape = jax.ShapeDtypeStruct((blocks, 2 * rows // halves, LANES), F32)
    size = sum(c.size for c in columns)
    return pl.pallas_call(
        functools.partial(project_kernel, depths, len(columns)),
        out_shape=[shape] * halves,
        compiler_params=room(factors, *columns, *[shape] * halves),
        cost_estimate=pl.CostEstimate(
            flops=2 * size * rows, bytes_accessed=2 * size, transcendentals=0
        ),
        name="project",
    )(factors, *columns)


def merge_kernel(starts, *refs):
    ins, outs = refs[: len(starts)], refs[len(starts) :]
    size = outs[0].shape[0]
    for p, out in enumerate(outs):
        value = ins[0][starts[0] + p * size : starts[0] + (p + 1) * size]
        for start, other in zip(starts[1:], ins[1:]):
            value = value + other[start + p * size : start + (p + 1) * size]
        out[...] = value


def merge(parts, starts, blocks, pieces):
    shape = jax.ShapeDtypeStruct((blocks // pieces,) + parts[0].shape[1:], F32)
    nbytes = 4 * math.prod(shape.shape) * pieces * (len(parts) + 1)
    return pl.pallas_call(
        functools.partial(merge_kernel, starts),
        out_shape=[shape] * pieces,
        compiler_params=room(*parts, *[shape] * pieces),
        cost_estimate=pl.CostEstimate(
            flops=nbytes // 4, bytes_accessed=nbytes, transcendentals=0
        ),
        name="merge",
    )(*parts)


def rank_sums(refs, queries):
    value = refs[0][0]
    for other in refs[1:]:
        value = value + other[0]
    half = value.shape[0] // 2
    product = value[:half] * value[half:]
    return product.reshape(queries, half // queries, LANES).sum(axis=1)


def partial_kernel(queries, *refs):
    refs[-1][...] = rank_sums(refs[:-1], queries)


def partial_scores(parts, queries):
    return pl.pallas_call(
        functools.partial(partial_kernel, queries),
        out_shape=jax.ShapeDtypeStruct((queries, LANES), F32),
        compiler_params=room(*parts),
        name="partial_scores",
    )(*parts)


def tail_kernel(count, halves, queries, *refs):
    ready, last = refs[:count], refs[count:-4]
    weights, doc_starts, scores, message = refs[-4:]
    parts = [ref[...] for ref in ready] + [rank_sums(last, queries // halves)]
    rows = []
    for h in range(halves):
        rows.append(functools.reduce(jnp.add, parts[h::halves]))
    value = jnp.concatenate(rows, axis=0) * weights[...]
    scores[...] = value
    lane = lax.broadcasted_iota(jnp.int32, (8, LANES), 1)
    start = jnp.where(doc_starts[...] > 0, lane, -1)
    step = 1
    while step < LANES:
        start = jnp.maximum(start, jnp.where(lane >= step, pltpu.roll(start, step, 1), -1))
        step *= 2
    start = start[0:1, :]
    lane = lane[0:1, :]
    earlier = lax.broadcasted_iota(jnp.int32, (LANES, LANES), 0)
    same_doc = ((earlier >= start) & (earlier <= lane)).astype(F32)
    total = jnp.dot(
        value, same_doc, precision=lax.Precision.HIGHEST, preferred_element_type=F32
    )
    number = (lane - jnp.maximum(start, 0) + 1).astype(F32)
    started = (start >= 0).astype(F32)
    message[0:queries, :] = total
    message[queries : queries + 1, :] = number
    message[queries + 1 : queries + 2, :] = started
    message[queries + 2 : queries + 3, :] = 1.0 - started
    message[queries + 3 :, :] = jnp.zeros_like(message[queries + 3 :, :])


def fold_members(queries, me, refs, shift):
    members = len(refs)
    tails = [ref[:, LANES - 1 : LANES] for ref in refs]
    mine = lax.rem(lax.shift_right_logical(me, shift), members)
    before = jnp.zeros_like(tails[0])
    running = jnp.zeros_like(tails[0])
    flag_row = lax.broadcasted_iota(jnp.int32, tails[0].shape, 0) == queries + 1
    for j in range(members):
        before = jnp.where(mine == j, running, before)
        value = tails[0]
        for k in range(1, members):
            value = jnp.where((mine ^ k) == j, tails[k], value)
        flag = value[queries + 1 : queries + 2, :]
        kept = jnp.where(flag > 0, value, value + running)
        running = jnp.where(flag_row, jnp.maximum(value, running), kept)
    return before, running


def group_kernel(queries, shift, me, *refs):
    before, running = fold_members(queries, me[0], refs[:-2], shift)
    refs[-2][...] = jnp.broadcast_to(before, refs[-2].shape)
    refs[-1][...] = jnp.broadcast_to(running, refs[-1].shape)


def fold_group(me, messages, queries, shift):
    shape = jax.ShapeDtypeStruct(messages[0].shape, F32)
    return pl.pallas_call(
        functools.partial(group_kernel, queries, shift),
        in_specs=[pl.BlockSpec(memory_space=pltpu.SMEM)]
        + [pl.BlockSpec(memory_space=pltpu.VMEM)] * len(messages),
        out_shape=[shape] * 2,
        compiler_params=room(),
        name="fold_group",
    )(me, *messages)


def finish_kernel(queries, shift, members, me, *refs):
    own, out = refs[-2:]
    before, _ = fold_members(queries, me[0], refs[:members], shift)
    carry = before
    for ref in refs[members:-2]:
        value = ref[:, LANES - 1 : LANES]
        flag = value[queries + 1 : queries + 2, :]
        carry = jnp.where(flag > 0, value, value + carry)
    lead = own[queries + 2 : queries + 3, :]
    total = own[0:queries, :] + lead * carry[0:queries, :]
    number = own[queries : queries + 1, :] + lead * carry[queries : queries + 1, :]
    out[...] = total / jnp.sqrt(number)


def local(
    activations, out_grads, left_factors, right_factors, token_ids, doc_starts, token_weights
):
    size = lax.axis_size("loop")
    me = lax.axis_index("loop").astype(jnp.int32).reshape(1)
    rows = left_factors.shape[0]
    queries = rows * size // RANK
    part = rows
    depths = (left_factors.shape[1] // size, right_factors.shape[1] // size)

    def cut(factors, depth):
        return factors.reshape(part, size, depth).swapaxes(0, 1)

    depth = -(-depths[1] // LANES) * LANES
    gap = jnp.zeros((size, part, depth - depths[1]), left_factors.dtype)
    outgoing = jnp.concatenate(
        [cut(right_factors, depths[1]), gap, cut(left_factors, depths[0])], axis=2
    )
    arrived = lax.all_to_all(outgoing, "loop", split_axis=0, concat_axis=0, tiled=True)
    columns = arrange(me, activations, out_grads)
    arrived, columns = lax.optimization_barrier((arrived, columns))
    own = arrived.reshape(size * part, depth + depths[0])
    stages = later_stages(size)
    count = size // 4
    halves = HALVES
    bounds = (depth, depths[1], depths[0])
    bounds = (depth, depths[1], depths[0])
    sent = project(own, bounds, columns[: PIECES // 2], halves)
    from_core = [swap(part, "loop", 1) for part in sent]
    kept = project(own, bounds, columns[PIECES // 2 :], halves)
    to_y = [merge([kept[h], from_core[h]], [0, 0], count, 1)[0] for h in range(halves)]
    from_y = [swap(part, "loop", 2) for part in to_y]
    ready = []
    wave = []
    for h in range(halves):
        if len(ready) > 1:
            from_y[h], ready[-2] = lax.optimization_barrier((from_y[h], ready[-2]))
        if wave:
            from_y[h], *wave = lax.optimization_barrier((from_y[h], *wave))
        values = [kept[h], from_core[h], from_y[h]]
        starts = [count, count, 0]
        blocks = count
        bit = 4
        wave = []
        while bit < size:
            width = WIDTH[h] if 2 * bit < size else 2
            pieces = merge(values, starts, blocks, width)
            if width == 2:
                values = [pieces[0], swap(pieces[1], "loop", bit)]
                wave = [pieces[1]]
            else:
                values = [pieces[0]] + [
                    swap(pieces[k], "loop", offset)
                    for k, offset in ((1, 2 * bit), (2, bit), (3, 3 * bit))
                ]
            blocks //= width
            starts = [0] * width
            bit *= width
        ready.append(partial_scores(values, queries // halves) if h + 1 < halves else values)
    last = ready.pop()

    weights = jnp.take(token_weights, token_ids, mode="clip") * RANK ** (-0.5)
    tile = jax.ShapeDtypeStruct((queries, LANES), F32)
    scores, message = pl.pallas_call(
        functools.partial(tail_kernel, len(ready), halves, queries),
        out_shape=[tile, jax.ShapeDtypeStruct((2 * queries, LANES), F32)],
        compiler_params=room(),
        name="tails",
    )(*ready, *last, weights[None, :], doc_starts[None, :])

    own_message = message
    befores = []
    shift = 0
    rounds = [[0, 1, 2, 3]] + stages
    for offsets in rounds[:-1]:
        messages = [message] + [swap(message, "loop", offset) for offset in offsets[1:]]
        before, message = fold_group(me, messages, queries, shift)
        befores.insert(0, before)
        shift += len(offsets).bit_length() - 1
    messages = [message] + [swap(message, "loop", offset) for offset in rounds[-1][1:]]
    influence = pl.pallas_call(
        functools.partial(finish_kernel, queries, shift, len(messages)),
        in_specs=[pl.BlockSpec(memory_space=pltpu.SMEM)]
        + [pl.BlockSpec(memory_space=pltpu.VMEM)] * (len(messages) + len(befores) + 1),
        out_shape=tile,
        compiler_params=room(),
        name="finish",
    )(me, *messages, *befores, own_message)
    return (scores.T, influence.T)


def solution(mesh):
    return jax.shard_map(
        local,
        mesh=mesh,
        in_specs=(
            P("loop", "groups"),
            P("loop", "groups"),
            P("loop", None),
            P("loop", None),
            P(("groups", "loop")),
            P(("groups", "loop")),
            P(),
        ),
        out_specs=(P(("groups", "loop"), None), P(("groups", "loop"), None)),
        check_vma=False,
    )
```

time: 353 us -> 90.1 us (0.26)
  blocking collectives: 179 us -> 0 us
  local copies, waits for them, and re-layouts: 39.6 us -> 8.49 us
  waiting for transfers between devices: 61.2 us -> 31.4 us
  loops' own time: 27.6 us -> 0 us
  starting transfers between devices: 15.7 us -> 40.3 us
  between operations: 14.9 us -> 0.89 us
  matrix products: 12 us -> 0 us
  Pallas kernels: 0 us -> 7.82 us
    unnamed x1 -> x0, blocking collectives: 136 us -> none
    all_gather x1 -> x0, blocking collectives: 43.2 us -> none  [carried_in(): everything = jax.tree.map(lambda part: lax.all_gather(part, axis), array)]
    all_gather x2 -> x0, waiting for transfers between devices: 35.2 us -> none  [the longest x1 35.2 us: local(): lax.all_gather(right_factors, 'loop', axis=0, tiled=True)]
    ppermute x0 -> x26, starting transfers between devices: none -> 32.9 us  [swap(): return lax.ppermute(value, axis, [(i, i ^ offset) for i in range(size)])]
    another operation x1 -> x0, loops' own time: 27.6 us -> none  [carried_in(): return lax.fori_loop(0, devices, lap, start)]
    ppermute x0 -> x26, waiting for transfers between devices: none -> 18.6 us  [swap(): return lax.ppermute(value, axis, [(i, i ^ offset) for i in range(size)])]
    dynamic_slice x32 -> x0, local copies, waits for them, and re-layouts: 18.6 us -> none  [lap(): new = combine(before, jax.tree.map(lambda part: part[k], everything))]
    dot_general x3 -> x0, matrix products: 12 us -> none  [the longest x2 11.8 us: project(): lax.dot_general(columns, factors, (((0,), (1,)), ((), ())), preferred_ele...]
  transfers between devices with their start and end apart: 4 -> 27, of which waited for: 2 -> 11; matrix products, arithmetic and copies ran while one was open for 7% -> 1% of each run, Pallas kernels for 0% -> 5%
where the time goes in v2:
time: 90.1 us; the launch traced here: 89.8 us
  starting transfers between devices  40.3 us (45%)
  waiting for transfers between devices  31.4 us (35%)
  local copies, waits for them, and re-layouts  8.49 us (9%)
  Pallas kernels  7.82 us (9%)
  other arithmetic  0.98 us (1%)
    ppermute x26, starting transfers between devices, swap(): return lax.ppermute(value, axis, [(i, i ^ offset) for i in range(size)])  32.9 us
    ppermute x26, waiting for transfers between devices, swap(): return lax.ppermute(value, axis, [(i, i ^ offset) for i in range(size)])  18.6 us
    all_to_all x1, waiting for transfers between devices, local(): lax.all_to_all(outgoing, 'loop', split_axis=0, concat_axis=0, tiled=True)  12.7 us
    all_to_all x1, starting transfers between devices, local(): lax.all_to_all(outgoing, 'loop', split_axis=0, concat_axis=0, tiled=True)  7.39 us
    unnamed x18, local copies, waits for them, and re-layouts  5.02 us
    pallas_call x1, Pallas kernels, arrange(): pl.pallas_call(arrange_kernel, in_specs=[pl.BlockSpec(memory_space=pltpu....  3.44 us
    reshape x3, local copies, waits for them, and re-layouts, cut(): return factors.reshape(part, size, depth).swapaxes(0, 1)  2.32 us
    pallas_call x2, Pallas kernels, project(): pl.pallas_call(functools.partial(project_kernel, depths, len(columns)), o...  2.21 us
  transfers between devices with their start and end apart: 27, of which 11 were waited for; matrix products, arithmetic and copies ran while one was open for 1% of the time, Pallas kernels for 5%

profile of v2, /device:TPU:0, one launch (start us, length us, event | category | flops | bytes accessed | tf_op | source)
XLA Modules:
  0.0 89.8 jit_solution(13532156463938832028)
XLA Ops:
  0.6 0.0 copy-start
  0.6 1.2 %copy.16 = bf16[2,16,8,1280]{3,2,0,1:T(8,128)(2,1)S(1)} copy(bf16[2,16,8,1280]{3,2,1,0:T(8,128)(2,1)} %bitcast.22) | data formatting | bytes 1310720 | tf_op jit(solution)/shard_map/reshape | solution.py:284
  1.8 1.1 %reshape.26 = bf16[16,16,320]{2,1,0:T(8,128)(2,1)S(1)} reshape(bf16[16,5120]{1,0:T(8,128)(2,1)} %param.9) | data formatting | bytes 327680 | tf_op jit(solution)/shard_map/reshape | solution.py:284
  3.0 1.0 %pad_maximum_fusion = bf16[16,16,1600]{2,1,0:T(8,128)(2,1)} fusion(bf16[16,16,320]{2,1,0:T(8,128)(2,1)S(1)} %bitcast.21, bf16[16,16,1280]{2,1,0:T(8,128)(2,1)S(1)} %bitcast.20), kind=kLoop, calls=%fused_computation.1 | loop fusion | flops 1638400 | bytes 1638400 | tf_op jit(solution)/shard_map/concatenate | solution.py:288
  3.9 7.4 %all-to-all-start = ((bf16[16,16,1600]{2,1,0:T(8,128)(2,1)}), bf16[16,16,1600]{2,1,0:T(8,128)(2,1)S(1)}, u32[]{:S(2)}, u32[]{:S(2)}) async-start(bf16[16,16,1600]{2,1,0:T(8,128)(2,1)} %pad_maximum_fusion), calls=%async_computation | async-start | bytes 1703936 | tf_op jit(solution)/shard_map/all_to_all | solution.py:291
  11.3 3.4 %arrange.1 = (bf16[4,1600,128]{2,1,0:T(8,128)(2,1)S(1)}, bf16[4,1600,128]{2,1,0:T(8,128)(2,1)S(1)}, bf16[4,1600,128]{2,1,0:T(8,128)(2,1)S(1)}, bf16[4,1600,128]{2,1,0:T(8,128)(2,1)S(1)}) custom-call(s32[1]{0:T(128)} %bitcast.2.me, bf16[320,2048]{1,0:T(8,128)(2,1)} %acts.1, bf16[1280,2048]{1,0:T(8,128)(2,1)} %grads.1), custom_call_target="tpu_custom_call" | custom-call | bytes 13107200 | tf_op jit(solution)/shard_map/arrange/pallas_call | solution.py:86
  14.8 1.2 %copy-done.1 = bf16[4,1600,128]{2,1,0:T(8,128)(2,1)} copy-done((bf16[4,1600,128]{2,1,0:T(8,128)(2,1)}, bf16[4,1600,128]{2,1,0:T(8,128)(2,1)S(1)}, u32[]{:S(2)}) %copy-start.1) | copy-done | bytes 1638424
  16.0 1.2 %copy-done.3 = bf16[4,1600,128]{2,1,0:T(8,128)(2,1)} copy-done((bf16[4,1600,128]{2,1,0:T(8,128)(2,1)}, bf16[4,1600,128]{2,1,0:T(8,128)(2,1)S(1)}, u32[]{:S(2)}) %copy-start.3) | copy-done | bytes 1638424
  17.2 1.2 %copy-done.5 = bf16[4,1600,128]{2,1,0:T(8,128)(2,1)} copy-done((bf16[4,1600,128]{2,1,0:T(8,128)(2,1)}, bf16[4,1600,128]{2,1,0:T(8,128)(2,1)S(1)}, u32[]{:S(2)}) %copy-start.5) | copy-done | bytes 1638424
  18.4 12.7 %all-to-all-done = bf16[16,16,1600]{2,1,0:T(8,128)(2,1)S(1)} async-done(((bf16[16,16,1600]{2,1,0:T(8,128)(2,1)}), bf16[16,16,1600]{2,1,0:T(8,128)(2,1)S(1)}, u32[]{:S(2)}, u32[]{:S(2)}) %all-to-all-start) | async-done | bytes 819232 | tf_op jit(solution)/shard_map/all_to_all | solution.py:291
  31.1 1.4 %copy-done.6 = bf16[4,1600,128]{2,1,0:T(8,128)(2,1)S(1)} copy-done((bf16[4,1600,128]{2,1,0:T(8,128)(2,1)S(1)}, bf16[4,1600,128]{2,1,0:T(8,128)(2,1)}, u32[]{:S(2)}) %copy-start.6) | copy-done | bytes 1638424
  32.5 1.1 %project.3 = (f32[8,128,128]{2,1,0:T(8,128)S(1)}, f32[8,128,128]{2,1,0:T(8,128)S(1)}, f32[8,128,128]{2,1,0:T(8,128)S(1)}, f32[8,128,128]{2,1,0:T(8,128)S(1)}) custom-call(bf16[256,1600]{1,0:T(8,128)(2,1)S(1)} %bitcast.17, bf16[4,1600,128]{2,1,0:T(8,128)(2,1)S(1)} %get-tuple-element.51.rest_0_, bf16[4,1600,128]{2,1,0:T(8,128)(2,1)S(1)} %copy-done.6), custom_call_target="tpu_custom_call" | custom-call | flops 838860800 | bytes 3276800 | tf_op jit(solution)/shard_map/project/pallas_call | solution.py:135
  33.6 0.4 collective-permute-start.2
  34.1 0.2 collective-permute-start.9
  34.2 0.3 collective-permute-start
  34.6 0.2 collective-permute-start.7
  34.7 1.1 %project.2 = (f32[8,128,128]{2,1,0:T(8,128)S(1)}, f32[8,128,128]{2,1,0:T(8,128)S(1)}, f32[8,128,128]{2,1,0:T(8,128)S(1)}, f32[8,128,128]{2,1,0:T(8,128)S(1)}) custom-call(bf16[256,1600]{1,0:T(8,128)(2,1)S(1)} %bitcast.18, bf16[4,1600,128]{2,1,0:T(8,128)(2,1)S(1)} %copy-done.2, bf16[4,1600,128]{2,1,0:T(8,128)(2,1)S(1)} %copy-done.4), custom_call_target="tpu_custom_call" | custom-call | flops 838860800 | bytes 3276800 | tf_op jit(solution)/shard_map/project/pallas_call | solution.py:135
  35.9 0.0 collective-permute-done.2.refs_1_
  35.9 1.7 %collective-permute-start.3 = (f32[4,128,128]{2,1,0:T(8,128)S(1)}, f32[4,128,128]{2,1,0:T(8,128)S(1)}, u32[]{:S(2)}, u32[]{:S(2)}) collective-permute-start(f32[4,128,128]{2,1,0:T(8,128)S(1)} %merge.9), channel_id=1, source_target_pairs={{0,2},{1,3},{2,0},{3,1},{4,6},{5,7},{6,4},{7,5},{8,10},{9,11},{10,... | collective-permute-start | bytes 786440 | tf_op jit(solution)/shard_map/ppermute | solution.py:20
  37.6 0.0 collective-permute-done.9.refs_1_
  37.6 0.5 collective-permute-start.10
  38.2 0.0 collective-permute-done.refs_1_
  38.2 1.6 %collective-permute-start.1 = (f32[4,128,128]{2,1,0:T(8,128)S(1)}, f32[4,128,128]{2,1,0:T(8,128)S(1)}, u32[]{:S(2)}, u32[]{:S(2)}) collective-permute-start(f32[4,128,128]{2,1,0:T(8,128)S(1)} %merge.8), channel_id=1, source_target_pairs={{0,2},{1,3},{2,0},{3,1},{4,6},{5,7},{6,4},{7,5},{8,10},{9,11},{10,... | collective-permute-start | bytes 786440 | tf_op jit(solution)/shard_map/ppermute | solution.py:20
  39.8 0.0 collective-permute-done.7.refs_1_
  39.9 0.5 collective-permute-start.8
  40.4 4.7 %collective-permute-done.3.refs_2_ = f32[4,128,128]{2,1,0:T(8,128)S(1)} collective-permute-done((f32[4,128,128]{2,1,0:T(8,128)S(1)}, f32[4,128,128]{2,1,0:T(8,128)S(1)}, u32[]{:S(2)}, u32[]{:S(2)}) %collective-permute-start.3) | collective-permute-done | bytes 262176 | tf_op jit(solution)/shard_map/ppermute | solution.py:20
  45.1 0.0 copy-start.8
  45.1 4.1 %collective-permute-start.4 = (f32[1,128,128]{2,1,0:T(8,128)S(1)}, f32[1,128,128]{2,1,0:T(8,128)S(1)}, u32[]{:S(2)}, u32[]{:S(2)}) collective-permute-start(f32[1,128,128]{2,1,0:T(8,128)S(1)} %get-tuple-element.57), channel_id=1, source_target_pairs={{0,8},{1,9},{2,10},{3,11},{4,12},{5,13},{6,14},{7,15},{8,0},{9,1},... | collective-permute-start | bytes 196616 | tf_op jit(solution)/shard_map/ppermute | solution.py:20
  49.3 0.0 collective-permute-start.5
  49.3 1.4 %collective-permute-done.10.refs_2_ = f32[4,128,128]{2,1,0:T(8,128)S(1)} collective-permute-done((f32[4,128,128]{2,1,0:T(8,128)S(1)}, f32[4,128,128]{2,1,0:T(8,128)S(1)}, u32[]{:S(2)}, u32[]{:S(2)}) %collective-permute-start.10) | collective-permute-done | bytes 262176 | tf_op jit(solution)/shard_map/ppermute | solution.py:20
  50.7 3.0 %collective-permute-start.6 = (f32[1,128,128]{2,1,0:T(8,128)S(1)}, f32[1,128,128]{2,1,0:T(8,128)S(1)}, u32[]{:S(2)}, u32[]{:S(2)}) collective-permute-start(f32[1,128,128]{2,1,0:T(8,128)S(1)} %get-tuple-element.59), channel_id=1, source_target_pairs={{0,12},{1,13},{2,14},{3,15},{4,8},{5,9},{6,10},{7,11},{8,4},{9,5},... | collective-permute-start | bytes 196616 | tf_op jit(solution)/shard_map/ppermute | solution.py:20
  53.7 0.0 collective-permute-done.4.refs_1_
  53.7 1.3 %collective-permute-start.11 = (f32[1,128,128]{2,1,0:T(8,128)S(1)}, f32[1,128,128]{2,1,0:T(8,128)S(1)}, u32[]{:S(2)}, u32[]{:S(2)}) collective-permute-start(f32[1,128,128]{2,1,0:T(8,128)S(1)} %get-tuple-element.66), channel_id=1, source_target_pairs={{0,8},{1,9},{2,10},{3,11},{4,12},{5,13},{6,14},{7,15},{8,0},{9,1},... | collective-permute-start | bytes 196616 | tf_op jit(solution)/shard_map/ppermute | solution.py:20
  55.0 0.0 collective-permute-done.5.refs_2_
  55.0 0.5 collective-permute-start.12
  55.5 1.7 %collective-permute-done.6.refs_3_ = f32[1,128,128]{2,1,0:T(8,128)S(1)} collective-permute-done((f32[1,128,128]{2,1,0:T(8,128)S(1)}, f32[1,128,128]{2,1,0:T(8,128)S(1)}, u32[]{:S(2)}, u32[]{:S(2)}) %collective-permute-start.6) | collective-permute-done | bytes 65568 | tf_op jit(solution)/shard_map/ppermute | solution.py:20
  57.2 3.1 %collective-permute-start.13 = (f32[1,128,128]{2,1,0:T(8,128)S(1)}, f32[1,128,128]{2,1,0:T(8,128)S(1)}, u32[]{:S(2)}, u32[]{:S(2)}) collective-permute-start(f32[1,128,128]{2,1,0:T(8,128)S(1)} %get-tuple-element.68), channel_id=1, source_target_pairs={{0,12},{1,13},{2,14},{3,15},{4,8},{5,9},{6,10},{7,11},{8,4},{9,5},... | collective-permute-start | bytes 196616 | tf_op jit(solution)/shard_map/ppermute | solution.py:20
  60.4 0.0 copy-start.7
  60.4 0.0 collective-permute-done.1.refs_2_
  60.5 0.8 collective-permute-start.14
  61.3 1.1 %gather_fusion = f32[128]{0:T(128)S(1)} fusion(f32[50688]{0:T(1024)S(1)} %copy-done, s32[1024]{0:T(1024)S(1)} %pad_clamp_fusion), kind=kCustom, calls=%fused_computation | custom fusion | bytes 1536 | tf_op jit(solution)/shard_map/jit(_take)/gather | solution.py:334
  62.4 0.0 collective-permute-done.11.refs_1_
  62.4 1.0 %collective-permute-done.13.refs_3_ = f32[1,128,128]{2,1,0:T(8,128)S(1)} collective-permute-done((f32[1,128,128]{2,1,0:T(8,128)S(1)}, f32[1,128,128]{2,1,0:T(8,128)S(1)}, u32[]{:S(2)}, u32[]{:S(2)}) %collective-permute-start.13) | collective-permute-done | bytes 65568 | tf_op jit(solution)/shard_map/ppermute | solution.py:20
  63.4 0.0 collective-permute-done.8.refs_2_
  63.5 3.4 %collective-permute-start.17 = (f32[1,128,128]{2,1,0:T(8,128)S(1)}, f32[1,128,128]{2,1,0:T(8,128)S(1)}, u32[]{:S(2)}, u32[]{:S(2)}) collective-permute-start(f32[1,128,128]{2,1,0:T(8,128)S(1)} %get-tuple-element.77), channel_id=1, source_target_pairs={{0,8},{1,9},{2,10},{3,11},{4,12},{5,13},{6,14},{7,15},{8,0},{9,1},... | collective-permute-start | bytes 196616 | tf_op jit(solution)/shard_map/ppermute | solution.py:20
  66.9 0.4 collective-permute-start.18
  67.3 1.2 %collective-permute-start.19 = (f32[1,128,128]{2,1,0:T(8,128)S(1)}, f32[1,128,128]{2,1,0:T(8,128)S(1)}, u32[]{:S(2)}, u32[]{:S(2)}) collective-permute-start(f32[1,128,128]{2,1,0:T(8,128)S(1)} %get-tuple-element.79), channel_id=1, source_target_pairs={{0,12},{1,13},{2,14},{3,15},{4,8},{5,9},{6,10},{7,11},{8,4},{9,5},... | collective-permute-start | bytes 196616 | tf_op jit(solution)/shard_map/ppermute | solution.py:20
  68.4 0.5 collective-permute-start.15
  68.9 2.9 %collective-permute-start.16 = (f32[1,128,128]{2,1,0:T(8,128)S(1)}, f32[1,128,128]{2,1,0:T(8,128)S(1)}, u32[]{:S(2)}, u32[]{:S(2)}) collective-permute-start(f32[1,128,128]{2,1,0:T(8,128)S(1)} %get-tuple-element.74), channel_id=1, source_target_pairs={{0,12},{1,13},{2,14},{3,15},{4,8},{5,9},{6,10},{7,11},{8,4},{9,5},... | collective-permute-start | bytes 196616 | tf_op jit(solution)/shard_map/ppermute | solution.py:20
  71.9 2.0 %collective-permute-done.15.refs_2_ = f32[1,128,128]{2,1,0:T(8,128)S(1)} collective-permute-done((f32[1,128,128]{2,1,0:T(8,128)S(1)}, f32[1,128,128]{2,1,0:T(8,128)S(1)}, u32[]{:S(2)}, u32[]{:S(2)}) %collective-permute-start.15) | collective-permute-done | bytes 65568 | tf_op jit(solution)/shard_map/ppermute | solution.py:20
  73.9 1.2 %collective-permute-done.16.refs_3_ = f32[1,128,128]{2,1,0:T(8,128)S(1)} collective-permute-done((f32[1,128,128]{2,1,0:T(8,128)S(1)}, f32[1,128,128]{2,1,0:T(8,128)S(1)}, u32[]{:S(2)}, u32[]{:S(2)}) %collective-permute-start.16) | collective-permute-done | bytes 65568 | tf_op jit(solution)/shard_map/ppermute | solution.py:20
  75.2 0.0 collective-permute-done.19.refs_6_
  75.2 1.0 %tails.1 = (f32[8,128]{1,0:T(8,128)}, f32[16,128]{1,0:T(8,128)S(1)}) custom-call(f32[2,128]{1,0:T(2,128)S(1)} %partial_scores.3.refs_0_, f32[2,128]{1,0:T(2,128)S(1)} %partial_scores.4.refs_1_, f32[2,128]{1,0:T(2,128)S(1)} %partial_scores.5.refs_2_, f32[1,128,128]{2,1,0:T(8,128)S(1)} %get-tuple-element.76.refs_3_, ...), custom_call_target="tpu_custom_call" | custom-call | tf_op jit(solution)/shard_map/tails/pallas_call | solution.py:336
  76.2 1.2 %collective-permute-start.21 = (f32[16,128]{1,0:T(8,128)S(1)}, f32[16,128]{1,0:T(8,128)S(1)}, u32[]{:S(2)}, u32[]{:S(2)}) collective-permute-start(f32[16,128]{1,0:T(8,128)S(1)} %get-tuple-element.81.refs_0_.refs_5_), channel_id=1, source_target_pairs={{0,2},{1,3},{2,0},{3,1},{4,6},{5,7},{6,4},{7,5},{8,10},{9,11},{10,... | collective-permute-start | bytes 24584 | tf_op jit(solution)/shard_map/ppermute | solution.py:20
  77.4 0.7 collective-permute-start.22
  78.1 1.8 %collective-permute-done.21.refs_2_ = f32[16,128]{1,0:T(8,128)S(1)} collective-permute-done((f32[16,128]{1,0:T(8,128)S(1)}, f32[16,128]{1,0:T(8,128)S(1)}, u32[]{:S(2)}, u32[]{:S(2)}) %collective-permute-start.21) | collective-permute-done | bytes 8224 | tf_op jit(solution)/shard_map/ppermute | solution.py:20
  79.9 0.6 collective-permute-done.22.refs_3_
  80.5 0.1 fold_group.1
  80.6 0.1 collective-permute-start.23
  80.7 3.0 %collective-permute-start.24 = (f32[16,128]{1,0:T(8,128)S(1)}, f32[16,128]{1,0:T(8,128)S(1)}, u32[]{:S(2)}, u32[]{:S(2)}) collective-permute-start(f32[16,128]{1,0:T(8,128)S(1)} %get-tuple-element.82.refs_0_), channel_id=1, source_target_pairs={{0,8},{1,9},{2,10},{3,11},{4,12},{5,13},{6,14},{7,15},{8,0},{9,1},... | collective-permute-start | bytes 24584 | tf_op jit(solution)/shard_map/ppermute | solution.py:20
  83.7 1.3 %collective-permute-start.25 = (f32[16,128]{1,0:T(8,128)S(1)}, f32[16,128]{1,0:T(8,128)S(1)}, u32[]{:S(2)}, u32[]{:S(2)}) collective-permute-start(f32[16,128]{1,0:T(8,128)S(1)} %get-tuple-element.82.refs_0_), channel_id=1, source_target_pairs={{0,12},{1,13},{2,14},{3,15},{4,8},{5,9},{6,10},{7,11},{8,4},{9,5},... | collective-permute-start | bytes 24584 | tf_op jit(solution)/shard_map/ppermute | solution.py:20
  85.0 0.3 collective-permute-done.24.refs_2_
  85.3 3.8 %collective-permute-done.25.refs_3_ = f32[16,128]{1,0:T(8,128)S(1)} collective-permute-done((f32[16,128]{1,0:T(8,128)S(1)}, f32[16,128]{1,0:T(8,128)S(1)}, u32[]{:S(2)}, u32[]{:S(2)}) %collective-permute-start.25) | collective-permute-done | bytes 8224 | tf_op jit(solution)/shard_map/ppermute | solution.py:20
  89.1 0.7 finish.1
  (32 shorter events, 0.4 us)
Async XLA Ops:
  0.6 60.6 %copy-start = (f32[50688]{0:T(1024)S(1)}, f32[50688]{0:T(1024)}, u32[]{:S(2)}) copy-start(f32[50688]{0:T(1024)} %param.13) | copy-start | bytes 608260
  3.9 27.2 %all-to-all-start = ((bf16[16,16,1600]{2,1,0:T(8,128)(2,1)}), bf16[16,16,1600]{2,1,0:T(8,128)(2,1)S(1)}, u32[]{:S(2)}, u32[]{:S(2)}) async-start(bf16[16,16,1600]{2,1,0:T(8,128)(2,1)} %pad_maximum_fusion), calls=%async_computation | async-start | bytes 1703936 | tf_op jit(solution)/shard_map/all_to_all | solution.py:291
  14.8 1.2 %copy-start.1 = (bf16[4,1600,128]{2,1,0:T(8,128)(2,1)}, bf16[4,1600,128]{2,1,0:T(8,128)(2,1)S(1)}, u32[]{:S(2)}) copy-start(bf16[4,1600,128]{2,1,0:T(8,128)(2,1)S(1)} %get-tuple-element.48.rest_0_) | copy-start | bytes 4915204
  16.0 1.2 %copy-start.3 = (bf16[4,1600,128]{2,1,0:T(8,128)(2,1)}, bf16[4,1600,128]{2,1,0:T(8,128)(2,1)S(1)}, u32[]{:S(2)}) copy-start(bf16[4,1600,128]{2,1,0:T(8,128)(2,1)S(1)} %get-tuple-element.49.rest_1_) | copy-start | bytes 4915204
  17.2 1.2 %copy-start.5 = (bf16[4,1600,128]{2,1,0:T(8,128)(2,1)}, bf16[4,1600,128]{2,1,0:T(8,128)(2,1)S(1)}, u32[]{:S(2)}) copy-start(bf16[4,1600,128]{2,1,0:T(8,128)(2,1)S(1)} %get-tuple-element.52.rest_1_) | copy-start | bytes 4915204
  31.1 1.4 %copy-start.6 = (bf16[4,1600,128]{2,1,0:T(8,128)(2,1)S(1)}, bf16[4,1600,128]{2,1,0:T(8,128)(2,1)}, u32[]{:S(2)}) copy-start(bf16[4,1600,128]{2,1,0:T(8,128)(2,1)} %copy-done.5) | copy-start | bytes 4915204
  32.5 2.2 %copy-start.2 = (bf16[4,1600,128]{2,1,0:T(8,128)(2,1)S(1)}, bf16[4,1600,128]{2,1,0:T(8,128)(2,1)}, u32[]{:S(2)}) copy-start(bf16[4,1600,128]{2,1,0:T(8,128)(2,1)} %copy-done.1) | copy-start | bytes 4915204
  32.5 2.2 %copy-start.4 = (bf16[4,1600,128]{2,1,0:T(8,128)(2,1)S(1)}, bf16[4,1600,128]{2,1,0:T(8,128)(2,1)}, u32[]{:S(2)}) copy-start(bf16[4,1600,128]{2,1,0:T(8,128)(2,1)} %copy-done.3) | copy-start | bytes 4915204
  33.6 2.2 %collective-permute-start.2 = (f32[8,128,128]{2,1,0:T(8,128)S(1)}, f32[8,128,128]{2,1,0:T(8,128)S(1)}, u32[]{:S(2)}, u32[]{:S(2)}) collective-permute-start(f32[8,128,128]{2,1,0:T(8,128)S(1)} %get-tuple-element.55), channel_id=1, source_target_pairs={{0,1},{1,0},{2,3},{3,2},{4,5},{5,4},{6,7},{7,6},{8,9},{9,8},{10,11... | collective-permute-start | bytes 1572872 | tf_op jit(solution)/shard_map/ppermute | solution.py:20
  34.1 3.5 %collective-permute-start.9 = (f32[8,128,128]{2,1,0:T(8,128)S(1)}, f32[8,128,128]{2,1,0:T(8,128)S(1)}, u32[]{:S(2)}, u32[]{:S(2)}) collective-permute-start(f32[8,128,128]{2,1,0:T(8,128)S(1)} %get-tuple-element.64), channel_id=1, source_target_pairs={{0,1},{1,0},{2,3},{3,2},{4,5},{5,4},{6,7},{7,6},{8,9},{9,8},{10,11... | collective-permute-start | bytes 1572872 | tf_op jit(solution)/shard_map/ppermute | solution.py:20
  34.2 3.9 %collective-permute-start = (f32[8,128,128]{2,1,0:T(8,128)S(1)}, f32[8,128,128]{2,1,0:T(8,128)S(1)}, u32[]{:S(2)}, u32[]{:S(2)}) collective-permute-start(f32[8,128,128]{2,1,0:T(8,128)S(1)} %get-tuple-element.53), channel_id=1, source_target_pairs={{0,1},{1,0},{2,3},{3,2},{4,5},{5,4},{6,7},{7,6},{8,9},{9,8},{10,11... | collective-permute-start | bytes 1572872 | tf_op jit(solution)/shard_map/ppermute | solution.py:20
  34.6 5.3 %collective-permute-start.7 = (f32[8,128,128]{2,1,0:T(8,128)S(1)}, f32[8,128,128]{2,1,0:T(8,128)S(1)}, u32[]{:S(2)}, u32[]{:S(2)}) collective-permute-start(f32[8,128,128]{2,1,0:T(8,128)S(1)} %get-tuple-element.62), channel_id=1, source_target_pairs={{0,1},{1,0},{2,3},{3,2},{4,5},{5,4},{6,7},{7,6},{8,9},{9,8},{10,11... | collective-permute-start | bytes 1572872 | tf_op jit(solution)/shard_map/ppermute | solution.py:20
  35.9 9.2 %collective-permute-start.3 = (f32[4,128,128]{2,1,0:T(8,128)S(1)}, f32[4,128,128]{2,1,0:T(8,128)S(1)}, u32[]{:S(2)}, u32[]{:S(2)}) collective-permute-start(f32[4,128,128]{2,1,0:T(8,128)S(1)} %merge.9), channel_id=1, source_target_pairs={{0,2},{1,3},{2,0},{3,1},{4,6},{5,7},{6,4},{7,5},{8,10},{9,11},{10,... | collective-permute-start | bytes 786440 | tf_op jit(solution)/shard_map/ppermute | solution.py:20
  37.6 13.1 %collective-permute-start.10 = (f32[4,128,128]{2,1,0:T(8,128)S(1)}, f32[4,128,128]{2,1,0:T(8,128)S(1)}, u32[]{:S(2)}, u32[]{:S(2)}) collective-permute-start(f32[4,128,128]{2,1,0:T(8,128)S(1)} %merge.12), channel_id=1, source_target_pairs={{0,2},{1,3},{2,0},{3,1},{4,6},{5,7},{6,4},{7,5},{8,10},{9,11},{10,... | collective-permute-start | bytes 786440 | tf_op jit(solution)/shard_map/ppermute | solution.py:20
  38.2 22.2 %collective-permute-start.1 = (f32[4,128,128]{2,1,0:T(8,128)S(1)}, f32[4,128,128]{2,1,0:T(8,128)S(1)}, u32[]{:S(2)}, u32[]{:S(2)}) collective-permute-start(f32[4,128,128]{2,1,0:T(8,128)S(1)} %merge.8), channel_id=1, source_target_pairs={{0,2},{1,3},{2,0},{3,1},{4,6},{5,7},{6,4},{7,5},{8,10},{9,11},{10,... | collective-permute-start | bytes 786440 | tf_op jit(solution)/shard_map/ppermute | solution.py:20
  39.9 23.6 %collective-permute-start.8 = (f32[4,128,128]{2,1,0:T(8,128)S(1)}, f32[4,128,128]{2,1,0:T(8,128)S(1)}, u32[]{:S(2)}, u32[]{:S(2)}) collective-permute-start(f32[4,128,128]{2,1,0:T(8,128)S(1)} %merge.11), channel_id=1, source_target_pairs={{0,2},{1,3},{2,0},{3,1},{4,6},{5,7},{6,4},{7,5},{8,10},{9,11},{10,... | collective-permute-start | bytes 786440 | tf_op jit(solution)/shard_map/ppermute | solution.py:20
  45.1 16.1 %copy-start.8 = (s32[128]{0:T(128)S(1)}, s32[128]{0:T(128)}, u32[]{:S(2)}) copy-start(s32[128]{0:T(128)} %param.11) | copy-start | bytes 1540
  45.1 8.6 %collective-permute-start.4 = (f32[1,128,128]{2,1,0:T(8,128)S(1)}, f32[1,128,128]{2,1,0:T(8,128)S(1)}, u32[]{:S(2)}, u32[]{:S(2)}) collective-permute-start(f32[1,128,128]{2,1,0:T(8,128)S(1)} %get-tuple-element.57), channel_id=1, source_target_pairs={{0,8},{1,9},{2,10},{3,11},{4,12},{5,13},{6,14},{7,15},{8,0},{9,1},... | collective-permute-start | bytes 196616 | tf_op jit(solution)/shard_map/ppermute | solution.py:20
  49.3 5.8 %collective-permute-start.5 = (f32[1,128,128]{2,1,0:T(8,128)S(1)}, f32[1,128,128]{2,1,0:T(8,128)S(1)}, u32[]{:S(2)}, u32[]{:S(2)}) collective-permute-start(f32[1,128,128]{2,1,0:T(8,128)S(1)} %get-tuple-element.58), channel_id=1, source_target_pairs={{0,4},{1,5},{2,6},{3,7},{4,0},{5,1},{6,2},{7,3},{8,12},{9,13},{10,... | collective-permute-start | bytes 196616 | tf_op jit(solution)/shard_map/ppermute | solution.py:20
  50.7 6.5 %collective-permute-start.6 = (f32[1,128,128]{2,1,0:T(8,128)S(1)}, f32[1,128,128]{2,1,0:T(8,128)S(1)}, u32[]{:S(2)}, u32[]{:S(2)}) collective-permute-start(f32[1,128,128]{2,1,0:T(8,128)S(1)} %get-tuple-element.59), channel_id=1, source_target_pairs={{0,12},{1,13},{2,14},{3,15},{4,8},{5,9},{6,10},{7,11},{8,4},{9,5},... | collective-permute-start | bytes 196616 | tf_op jit(solution)/shard_map/ppermute | solution.py:20
  53.7 8.7 %collective-permute-start.11 = (f32[1,128,128]{2,1,0:T(8,128)S(1)}, f32[1,128,128]{2,1,0:T(8,128)S(1)}, u32[]{:S(2)}, u32[]{:S(2)}) collective-permute-start(f32[1,128,128]{2,1,0:T(8,128)S(1)} %get-tuple-element.66), channel_id=1, source_target_pairs={{0,8},{1,9},{2,10},{3,11},{4,12},{5,13},{6,14},{7,15},{8,0},{9,1},... | collective-permute-start | bytes 196616 | tf_op jit(solution)/shard_map/ppermute | solution.py:20
  55.0 7.4 %collective-permute-start.12 = (f32[1,128,128]{2,1,0:T(8,128)S(1)}, f32[1,128,128]{2,1,0:T(8,128)S(1)}, u32[]{:S(2)}, u32[]{:S(2)}) collective-permute-start(f32[1,128,128]{2,1,0:T(8,128)S(1)} %get-tuple-element.67), channel_id=1, source_target_pairs={{0,4},{1,5},{2,6},{3,7},{4,0},{5,1},{6,2},{7,3},{8,12},{9,13},{10,... | collective-permute-start | bytes 196616 | tf_op jit(solution)/shard_map/ppermute | solution.py:20
  57.2 6.2 %collective-permute-start.13 = (f32[1,128,128]{2,1,0:T(8,128)S(1)}, f32[1,128,128]{2,1,0:T(8,128)S(1)}, u32[]{:S(2)}, u32[]{:S(2)}) collective-permute-start(f32[1,128,128]{2,1,0:T(8,128)S(1)} %get-tuple-element.68), channel_id=1, source_target_pairs={{0,12},{1,13},{2,14},{3,15},{4,8},{5,9},{6,10},{7,11},{8,4},{9,5},... | collective-permute-start | bytes 196616 | tf_op jit(solution)/shard_map/ppermute | solution.py:20
  60.4 14.8 %copy-start.7 = (s32[128]{0:T(128)S(1)}, s32[128]{0:T(128)}, u32[]{:S(2)}) copy-start(s32[128]{0:T(128)} %param.12) | copy-start | bytes 1540
  60.5 8.5 %collective-permute-start.14 = (f32[1,128,128]{2,1,0:T(8,128)S(1)}, f32[1,128,128]{2,1,0:T(8,128)S(1)}, u32[]{:S(2)}, u32[]{:S(2)}) collective-permute-start(f32[1,128,128]{2,1,0:T(8,128)S(1)} %get-tuple-element.72), channel_id=1, source_target_pairs={{0,8},{1,9},{2,10},{3,11},{4,12},{5,13},{6,14},{7,15},{8,0},{9,1},... | collective-permute-start | bytes 196616 | tf_op jit(solution)/shard_map/ppermute | solution.py:20
  63.5 11.6 %collective-permute-start.17 = (f32[1,128,128]{2,1,0:T(8,128)S(1)}, f32[1,128,128]{2,1,0:T(8,128)S(1)}, u32[]{:S(2)}, u32[]{:S(2)}) collective-permute-start(f32[1,128,128]{2,1,0:T(8,128)S(1)} %get-tuple-element.77), channel_id=1, source_target_pairs={{0,8},{1,9},{2,10},{3,11},{4,12},{5,13},{6,14},{7,15},{8,0},{9,1},... | collective-permute-start | bytes 196616 | tf_op jit(solution)/shard_map/ppermute | solution.py:20
  66.9 8.2 %collective-permute-start.18 = (f32[1,128,128]{2,1,0:T(8,128)S(1)}, f32[1,128,128]{2,1,0:T(8,128)S(1)}, u32[]{:S(2)}, u32[]{:S(2)}) collective-permute-start(f32[1,128,128]{2,1,0:T(8,128)S(1)} %get-tuple-element.78), channel_id=1, source_target_pairs={{0,4},{1,5},{2,6},{3,7},{4,0},{5,1},{6,2},{7,3},{8,12},{9,13},{10,... | collective-permute-start | bytes 196616 | tf_op jit(solution)/shard_map/ppermute | solution.py:20
  67.3 7.9 %collective-permute-start.19 = (f32[1,128,128]{2,1,0:T(8,128)S(1)}, f32[1,128,128]{2,1,0:T(8,128)S(1)}, u32[]{:S(2)}, u32[]{:S(2)}) collective-permute-start(f32[1,128,128]{2,1,0:T(8,128)S(1)} %get-tuple-element.79), channel_id=1, source_target_pairs={{0,12},{1,13},{2,14},{3,15},{4,8},{5,9},{6,10},{7,11},{8,4},{9,5},... | collective-permute-start | bytes 196616 | tf_op jit(solution)/shard_map/ppermute | solution.py:20
  68.4 5.5 %collective-permute-start.15 = (f32[1,128,128]{2,1,0:T(8,128)S(1)}, f32[1,128,128]{2,1,0:T(8,128)S(1)}, u32[]{:S(2)}, u32[]{:S(2)}) collective-permute-start(f32[1,128,128]{2,1,0:T(8,128)S(1)} %get-tuple-element.73), channel_id=1, source_target_pairs={{0,4},{1,5},{2,6},{3,7},{4,0},{5,1},{6,2},{7,3},{8,12},{9,13},{10,... | collective-permute-start | bytes 196616 | tf_op jit(solution)/shard_map/ppermute | solution.py:20
  68.9 6.2 %collective-permute-start.16 = (f32[1,128,128]{2,1,0:T(8,128)S(1)}, f32[1,128,128]{2,1,0:T(8,128)S(1)}, u32[]{:S(2)}, u32[]{:S(2)}) collective-permute-start(f32[1,128,128]{2,1,0:T(8,128)S(1)} %get-tuple-element.74), channel_id=1, source_target_pairs={{0,12},{1,13},{2,14},{3,15},{4,8},{5,9},{6,10},{7,11},{8,4},{9,5},... | collective-permute-start | bytes 196616 | tf_op jit(solution)/shard_map/ppermute | solution.py:20
  76.2 1.9 %collective-permute-start.20 = (f32[16,128]{1,0:T(8,128)S(1)}, f32[16,128]{1,0:T(8,128)S(1)}, u32[]{:S(2)}, u32[]{:S(2)}) collective-permute-start(f32[16,128]{1,0:T(8,128)S(1)} %get-tuple-element.81.refs_0_.refs_5_), channel_id=1, source_target_pairs={{0,1},{1,0},{2,3},{3,2},{4,5},{5,4},{6,7},{7,6},{8,9},{9,8},{10,11... | collective-permute-start | bytes 24584 | tf_op jit(solution)/shard_map/ppermute | solution.py:20
  76.2 3.7 %collective-permute-start.21 = (f32[16,128]{1,0:T(8,128)S(1)}, f32[16,128]{1,0:T(8,128)S(1)}, u32[]{:S(2)}, u32[]{:S(2)}) collective-permute-start(f32[16,128]{1,0:T(8,128)S(1)} %get-tuple-element.81.refs_0_.refs_5_), channel_id=1, source_target_pairs={{0,2},{1,3},{2,0},{3,1},{4,6},{5,7},{6,4},{7,5},{8,10},{9,11},{10,... | collective-permute-start | bytes 24584 | tf_op jit(solution)/shard_map/ppermute | solution.py:20
  77.4 3.1 %collective-permute-start.22 = (f32[16,128]{1,0:T(8,128)S(1)}, f32[16,128]{1,0:T(8,128)S(1)}, u32[]{:S(2)}, u32[]{:S(2)}) collective-permute-start(f32[16,128]{1,0:T(8,128)S(1)} %get-tuple-element.81.refs_0_.refs_5_), channel_id=1, source_target_pairs={{0,3},{1,2},{2,1},{3,0},{4,7},{5,6},{6,5},{7,4},{8,11},{9,10},{10,... | collective-permute-start | bytes 24584 | tf_op jit(solution)/shard_map/ppermute | solution.py:20
  80.6 4.4 %collective-permute-start.23 = (f32[16,128]{1,0:T(8,128)S(1)}, f32[16,128]{1,0:T(8,128)S(1)}, u32[]{:S(2)}, u32[]{:S(2)}) collective-permute-start(f32[16,128]{1,0:T(8,128)S(1)} %get-tuple-element.82.refs_0_), channel_id=1, source_target_pairs={{0,4},{1,5},{2,6},{3,7},{4,0},{5,1},{6,2},{7,3},{8,12},{9,13},{10,... | collective-permute-start | bytes 24584 | tf_op jit(solution)/shard_map/ppermute | solution.py:20
  80.7 4.6 %collective-permute-start.24 = (f32[16,128]{1,0:T(8,128)S(1)}, f32[16,128]{1,0:T(8,128)S(1)}, u32[]{:S(2)}, u32[]{:S(2)}) collective-permute-start(f32[16,128]{1,0:T(8,128)S(1)} %get-tuple-element.82.refs_0_), channel_id=1, source_target_pairs={{0,8},{1,9},{2,10},{3,11},{4,12},{5,13},{6,14},{7,15},{8,0},{9,1},... | collective-permute-start | bytes 24584 | tf_op jit(solution)/shard_map/ppermute | solution.py:20
  83.7 5.4 %collective-permute-start.25 = (f32[16,128]{1,0:T(8,128)S(1)}, f32[16,128]{1,0:T(8,128)S(1)}, u32[]{:S(2)}, u32[]{:S(2)}) collective-permute-start(f32[16,128]{1,0:T(8,128)S(1)} %get-tuple-element.82.refs_0_), channel_id=1, source_target_pairs={{0,12},{1,13},{2,14},{3,15},{4,8},{5,9},{6,10},{7,11},{8,4},{9,5},... | collective-permute-start | bytes 24584 | tf_op jit(solution)/shard_map/ppermute | solution.py:20

commit v3 on v2

--- a/solution.py
+++ b/solution.py
@@ -9,9 +9,8 @@
 
 RANK = 32
 LANES = 128
-HALVES = 4
-WIDTH = [4, 4, 4, 4]
 PIECES = 4
+CHUNKS = ((1,), (1,))
 F32 = jnp.float32
 
 
@@ -101,8 +100,6 @@
     columns, outs = rest[:count], rest[count:]
     blocks = outs[0].shape[0]
     per = columns[0].shape[0]
-    halves = len(outs)
-    size = factors.shape[0] // halves
     gap, right_depth, left_depth = depths
 
     def pair(ref, base, i, _):
@@ -113,13 +110,16 @@
         grads = jnp.concatenate([ref[2 * i + j, :right_depth] for j in two], axis=1)
         a = jnp.dot(left, acts, preferred_element_type=F32)
         b = jnp.dot(right, grads, preferred_element_type=F32)
-        for h, out in enumerate(outs):
+        first = 0
+        for out in outs:
+            size = out.shape[1] // 2
             for side, value in enumerate((a, b)):
-                piece = value[h * size : (h + 1) * size]
+                piece = value[first : first + size]
                 for j in two:
                     out[base + 2 * i + j, side * size : (side + 1) * size, :] = piece[
                         :, j * LANES : (j + 1) * LANES
                     ]
+            first += size
         return 0
 
     for k, ref in enumerate(columns):
@@ -127,39 +127,91 @@
         lax.fori_loop(0, per // 2, step, 0, unroll=blocks <= 8)
 
 
-def project(factors, depths, columns, halves):
+def project(factors, depths, columns, waves):
     blocks = columns[0].shape[0] * len(columns)
-    rows = factors.shape[0]
-    shape = jax.ShapeDtypeStruct((blocks, 2 * rows // halves, LANES), F32)
+    shapes = [jax.ShapeDtypeStruct((blocks, 2 * w, LANES), F32) for w in waves]
     size = sum(c.size for c in columns)
     return pl.pallas_call(
         functools.partial(project_kernel, depths, len(columns)),
-        out_shape=[shape] * halves,
-        compiler_params=room(factors, *columns, *[shape] * halves),
+        out_shape=shapes,
+        compiler_params=room(factors, *columns, *shapes),
         cost_estimate=pl.CostEstimate(
-            flops=2 * size * rows, bytes_accessed=2 * size, transcendentals=0
+            flops=2 * size * factors.shape[0], bytes_accessed=2 * size, transcendentals=0
         ),
         name="project",
     )(factors, *columns)
 
 
-def merge_kernel(starts, *refs):
+def message_rows(blocks, rows):
+    return blocks * rows // 4 * 3 + -(-blocks // 8) * 8
+
+
+def encode(out, block, blocks, value):
+    size = value.shape[0] // 4
+    codes, powers = [], None
+    for g in range(4):
+        group = value[g * size : (g + 1) * size]
+        most = jnp.max(jnp.abs(group), axis=0, keepdims=True)
+        power = jnp.clip(jnp.floor(jnp.log(most) * (1 / math.log(2.0))) + 2.0, -100.0, 100.0)
+        codes.append(jnp.floor(group * jnp.exp2(23.0 - power) + 0.5).astype(jnp.int32))
+        byte = (power.astype(jnp.int32) + 128) << (8 * g)
+        powers = byte if powers is None else powers | byte
+    for g in range(3):
+        high = lax.shift_right_arithmetic(codes[3], 8 * g) << 24
+        words = (codes[g] & 0xFFFFFF) | high
+        out[pl.ds((3 * block + g) * size, size), :] = words
+    out[pl.ds(3 * blocks * size + block, 1), :] = powers
+
+
+def decode(ref, block, blocks, rows):
+    size = rows // 4
+    words = [ref[pl.ds((3 * block + g) * size, size), :] for g in range(3)]
+    powers = ref[pl.ds(3 * blocks * size + block, 1), :]
+    codes = [lax.shift_right_arithmetic(word << 8, 8) for word in words]
+    low = lax.shift_right_logical(words[0], 24) | (lax.shift_right_logical(words[1], 24) << 8)
+    codes.append(low | (lax.shift_right_arithmetic(words[2], 24) << 16))
+    groups = []
+    for g, code in enumerate(codes):
+        power = (lax.shift_right_logical(powers, 8 * g) & 0xFF) - 128
+        groups.append(code.astype(F32) * jnp.exp2(power.astype(F32) - 23.0))
+    return jnp.concatenate(groups, axis=0)
+
+
+def total_of(refs, starts, block, blocks, rows):
+    value = None
+    for ref, start in zip(refs, starts):
+        term = decode(ref, block, blocks, rows) if start is None else ref[start + block]
+        value = term if value is None else value + term
+    return value
+
+
+def merge_kernel(starts, blocks, rows, stay, *refs):
     ins, outs = refs[: len(starts)], refs[len(starts) :]
-    size = outs[0].shape[0]
+    size = blocks // len(outs)
     for p, out in enumerate(outs):
-        value = ins[0][starts[0] + p * size : starts[0] + (p + 1) * size]
-        for start, other in zip(starts[1:], ins[1:]):
-            value = value + other[start + p * size : start + (p + 1) * size]
-        out[...] = value
-
-
-def merge(parts, starts, blocks, pieces):
-    shape = jax.ShapeDtypeStruct((blocks // pieces,) + parts[0].shape[1:], F32)
-    nbytes = 4 * math.prod(shape.shape) * pieces * (len(parts) + 1)
+
+        def step(i, _):
+            value = total_of(ins, starts, p * size + i, blocks, rows)
+            if stay and p == 0:
+                out[i] = value
+            else:
+                encode(out, i, size, value)
+            return 0
+
+        lax.fori_loop(0, size, step, 0, unroll=blocks <= 8)
+
+
+def merge(parts, starts, blocks, pieces, stay=True):
+    rows = parts[0].shape[1]
+    size = blocks // pieces
+    message = jax.ShapeDtypeStruct((message_rows(size, rows), LANES), jnp.int32)
+    first = jax.ShapeDtypeStruct((size, rows, LANES), F32)
+    shapes = [first if stay else message] + [message] * (pieces - 1)
+    nbytes = 4 * blocks * rows * LANES * (len(parts) + 1)
     return pl.pallas_call(
-        functools.partial(merge_kernel, starts),
-        out_shape=[shape] * pieces,
-        compiler_params=room(*parts, *[shape] * pieces),
+        functools.partial(merge_kernel, starts, blocks, rows, stay),
+        out_shape=shapes,
+        compiler_params=room(*parts, *shapes),
         cost_estimate=pl.CostEstimate(
             flops=nbytes // 4, bytes_accessed=nbytes, transcendentals=0
         ),
@@ -167,36 +219,40 @@
     )(*parts)
 
 
-def rank_sums(refs, queries):
-    value = refs[0][0]
-    for other in refs[1:]:
-        value = value + other[0]
-    half = value.shape[0] // 2
-    product = value[:half] * value[half:]
-    return product.reshape(queries, half // queries, LANES).sum(axis=1)
-
-
-def partial_kernel(queries, *refs):
-    refs[-1][...] = rank_sums(refs[:-1], queries)
-
-
-def partial_scores(parts, queries):
+def rank_sums(refs, ranks):
+    rows = refs[0].shape[1]
+    starts = [0] + [None] * (len(refs) - 1)
+    value = total_of(refs, starts, 0, 1, rows)
+    product = value[: rows // 2] * value[rows // 2 :]
+    return product.reshape(rows // 2 // ranks, ranks, LANES).sum(axis=1)
+
+
+def partial_kernel(ranks, *refs):
+    refs[-1][...] = rank_sums(refs[:-1], ranks)
+
+
+def partial_scores(parts, ranks):
+    queries = parts[0].shape[1] // 2 // ranks
     return pl.pallas_call(
-        functools.partial(partial_kernel, queries),
+        functools.partial(partial_kernel, ranks),
         out_shape=jax.ShapeDtypeStruct((queries, LANES), F32),
         compiler_params=room(*parts),
         name="partial_scores",
     )(*parts)
 
 
-def tail_kernel(count, halves, queries, *refs):
+def tail_kernel(count, queries, ranks, *refs):
     ready, last = refs[:count], refs[count:-4]
     weights, doc_starts, scores, message = refs[-4:]
-    parts = [ref[...] for ref in ready] + [rank_sums(last, queries // halves)]
-    rows = []
-    for h in range(halves):
-        rows.append(functools.reduce(jnp.add, parts[h::halves]))
-    value = jnp.concatenate(rows, axis=0) * weights[...]
+    parts = [ref[...] for ref in ready] + [rank_sums(last, ranks)]
+    value = None
+    while parts:
+        chunk = []
+        while sum(part.shape[0] for part in chunk) < queries:
+            chunk.append(parts.pop(0))
+        chunk = jnp.concatenate(chunk, axis=0)
+        value = chunk if value is None else value + chunk
+    value = value * weights[...]
     scores[...] = value
     lane = lax.broadcasted_iota(jnp.int32, (8, LANES), 1)
     start = jnp.where(doc_starts[...] > 0, lane, -1)
@@ -273,15 +329,17 @@
 def local(
     activations, out_grads, left_factors, right_factors, token_ids, doc_starts, token_weights
 ):
-    size = lax.axis_size("loop")
+    size, groups = lax.axis_size("loop"), lax.axis_size("groups")
     me = lax.axis_index("loop").astype(jnp.int32).reshape(1)
     rows = left_factors.shape[0]
     queries = rows * size // RANK
-    part = rows
+    part = rows // groups
+    group = lax.axis_index("groups")
     depths = (left_factors.shape[1] // size, right_factors.shape[1] // size)
 
     def cut(factors, depth):
-        return factors.reshape(part, size, depth).swapaxes(0, 1)
+        mine = lax.dynamic_slice_in_dim(factors, group * part, part, axis=0)
+        return mine.reshape(part, size, depth).swapaxes(0, 1)
 
     depth = -(-depths[1] // LANES) * LANES
     gap = jnp.zeros((size, part, depth - depths[1]), left_factors.dtype)
@@ -290,51 +348,50 @@
     )
     arrived = lax.all_to_all(outgoing, "loop", split_axis=0, concat_axis=0, tiled=True)
     columns = arrange(me, activations, out_grads)
-    arrived, columns = lax.optimization_barrier((arrived, columns))
+    weights = jnp.take(token_weights, token_ids, mode="clip") * RANK ** (-0.5)
+    arrived, columns, weights = lax.optimization_barrier((arrived, columns, weights))
     own = arrived.reshape(size * part, depth + depths[0])
     stages = later_stages(size)
     count = size // 4
-    halves = HALVES
     bounds = (depth, depths[1], depths[0])
-    bounds = (depth, depths[1], depths[0])
-    sent = project(own, bounds, columns[: PIECES // 2], halves)
-    from_core = [swap(part, "loop", 1) for part in sent]
-    kept = project(own, bounds, columns[PIECES // 2 :], halves)
-    to_y = [merge([kept[h], from_core[h]], [0, 0], count, 1)[0] for h in range(halves)]
-    from_y = [swap(part, "loop", 2) for part in to_y]
+    ranks = RANK // groups
+    other = lax.ppermute(own, "groups", [(i, i ^ 1) for i in range(groups)])
+    flows = []
+    for factors, waves in zip((own, other), CHUNKS):
+        if flows:
+            factors, flows[-1][2] = lax.optimization_barrier((factors, flows[-1][2]))
+        waves = [factors.shape[0] // w for w in waves]
+        sent = project(factors, bounds, columns[: PIECES // 2], waves)
+        from_core = [swap(part, "loop", 1) for part in sent]
+        kept = project(factors, bounds, columns[PIECES // 2 :], waves)
+        to_y = [merge([k, f], [0, 0], count, 1, stay=False)[0] for k, f in zip(kept, from_core)]
+        from_y = [swap(part, "loop", 2) for part in to_y]
+        flows.extend([list(flow) for flow in zip(kept, from_core, from_y)])
+        if len(flows) > 1:
+            flows[0][2], to_y[-1] = lax.optimization_barrier((flows[0][2], to_y[-1]))
     ready = []
-    wave = []
-    for h in range(halves):
+    for h, values in enumerate(flows):
         if len(ready) > 1:
-            from_y[h], ready[-2] = lax.optimization_barrier((from_y[h], ready[-2]))
-        if wave:
-            from_y[h], *wave = lax.optimization_barrier((from_y[h], *wave))
-        values = [kept[h], from_core[h], from_y[h]]
-        starts = [count, count, 0]
+            values[2], ready[-2] = lax.optimization_barrier((values[2], ready[-2]))
+        starts = [count, count, None]
         blocks = count
         bit = 4
-        wave = []
         while bit < size:
-            width = WIDTH[h] if 2 * bit < size else 2
+            width = 4 if 2 * bit < size else 2
             pieces = merge(values, starts, blocks, width)
-            if width == 2:
-                values = [pieces[0], swap(pieces[1], "loop", bit)]
-                wave = [pieces[1]]
-            else:
-                values = [pieces[0]] + [
-                    swap(pieces[k], "loop", offset)
-                    for k, offset in ((1, 2 * bit), (2, bit), (3, 3 * bit))
-                ]
+            offsets = (0, 2 * bit, bit, 3 * bit) if width == 4 else (0, bit)
+            values = [pieces[0]] + [
+                swap(piece, "loop", offset) for piece, offset in zip(pieces[1:], offsets[1:])
+            ]
             blocks //= width
-            starts = [0] * width
+            starts = [0] + [None] * (width - 1)
             bit *= width
-        ready.append(partial_scores(values, queries // halves) if h + 1 < halves else values)
+        ready.append(partial_scores(values, ranks) if h + 1 < len(flows) else values)
     last = ready.pop()
 
-    weights = jnp.take(token_weights, token_ids, mode="clip") * RANK ** (-0.5)
     tile = jax.ShapeDtypeStruct((queries, LANES), F32)
     scores, message = pl.pallas_call(
-        functools.partial(tail_kernel, len(ready), halves, queries),
+        functools.partial(tail_kernel, len(ready), queries, ranks),
         out_shape=[tile, jax.ShapeDtypeStruct((2 * queries, LANES), F32)],
         compiler_params=room(),
         name="tails",

time: 90.1 us -> 79.1 us (0.88)
  starting transfers between devices: 40.3 us -> 26 us
  waiting for transfers between devices: 31.4 us -> 33.2 us
  Pallas kernels: 7.82 us -> 9.06 us
    ppermute x26 -> x16, starting transfers between devices: 32.9 us -> 17.1 us  [swap(): return lax.ppermute(value, axis, [(i, i ^ offset) for i in range(size)])]
    ppermute x0 -> x1, waiting for transfers between devices: none -> 8.64 us  [local(): other = lax.ppermute(own, 'groups', [(i, i ^ 1) for i in range(groups)])]
    all_to_all x1, waiting for transfers between devices: 12.7 us -> 4.48 us  [local(): lax.all_to_all(outgoing, 'loop', split_axis=0, concat_axis=0, tiled=True)]
    reshape x3 -> x1, local copies, waits for them, and re-layouts: 2.32 us -> 0.14 us  [cut(): return mine.reshape(part, size, depth).swapaxes(0, 1)]
    ppermute x26 -> x16, waiting for transfers between devices: 18.6 us -> 20.1 us  [swap(): return lax.ppermute(value, axis, [(i, i ^ offset) for i in range(size)])]
    ppermute x0 -> x1, starting transfers between devices: none -> 1.49 us  [local(): other = lax.ppermute(own, 'groups', [(i, i ^ 1) for i in range(groups)])]
    unnamed x18 -> x22, local copies, waits for them, and re-layouts: 5.02 us -> 6.47 us
    dynamic_slice x0 -> x2, local copies, waits for them, and re-layouts: none -> 1 us  [cut(): mine = lax.dynamic_slice_in_dim(factors, group * part, part, axis=0)]
  transfers between devices with their start and end apart: 27 -> 18, of which waited for: 11 -> 13; matrix products, arithmetic and copies ran while one was open for 1% -> 1% of each run, Pallas kernels for 5% -> 7%
where the time goes in v3:
time: 79.1 us; the launch traced here: 78.8 us
  waiting for transfers between devices  33.2 us (42%)
  starting transfers between devices  26 us (33%)
  Pallas kernels  9.06 us (11%)
  local copies, waits for them, and re-layouts  8.78 us (11%)
  between operations  0.85 us (1%)
  other arithmetic  0.84 us (1%)
    ppermute x16, waiting for transfers between devices, swap(): return lax.ppermute(value, axis, [(i, i ^ offset) for i in range(size)])  20.1 us
    ppermute x16, starting transfers between devices, swap(): return lax.ppermute(value, axis, [(i, i ^ offset) for i in range(size)])  17.1 us
    ppermute x1, waiting for transfers between devices, local(): other = lax.ppermute(own, 'groups', [(i, i ^ 1) for i in range(groups)])  8.64 us
    all_to_all x1, starting transfers between devices, local(): lax.all_to_all(outgoing, 'loop', split_axis=0, concat_axis=0, tiled=True)  7.39 us
    unnamed x22, local copies, waits for them, and re-layouts  6.47 us
    all_to_all x1, waiting for transfers between devices, local(): lax.all_to_all(outgoing, 'loop', split_axis=0, concat_axis=0, tiled=True)  4.48 us
    pallas_call x1, Pallas kernels, arrange(): pl.pallas_call(arrange_kernel, in_specs=[pl.BlockSpec(memory_space=pltpu....  3.44 us
    pallas_call x4, Pallas kernels, project(): pl.pallas_call(functools.partial(project_kernel, depths, len(columns)), o...  2.59 us
  transfers between devices with their start and end apart: 18, of which 13 were waited for; matrix products, arithmetic and copies ran while one was open for 1% of the time, Pallas kernels for 7%

profile of v3, /device:TPU:0, one launch (start us, length us, event | category | flops | bytes accessed | tf_op | source)
XLA Modules:
  0.0 78.8 jit_solution(2729023362381403879)
XLA Ops:
  0.6 0.0 copy-start
  0.6 0.0 copy-start.10
  0.7 0.0 copy-start.9
  0.7 1.0 %constant_dynamic-slice_fusion = bf16[8,5120]{1,0:T(8,128)(2,1)S(1)} fusion(bf16[16,5120]{1,0:T(8,128)(2,1)} %param.9, s32[]{:T(128)S(6)} %select_n.4), kind=kLoop, calls=%fused_computation.3 | loop fusion | bytes 163844 | tf_op jit(solution)/shard_map/dynamic_slice | solution.py:341
  1.6 0.1 reshape.17
  1.8 0.0 copy-done
  1.9 0.8 %pad_maximum_fusion = bf16[16,8,1600]{2,1,0:T(8,128)(2,1)} fusion(bf16[16,8,320]{2,1,0:T(8,128)(2,1)S(1)} %copy.9, bf16[16,8,1280]{2,1,0:T(8,128)(2,1)S(1)} %bitcast.15), kind=kLoop, calls=%fused_computation.1 | loop fusion | flops 819200 | bytes 819200 | tf_op jit(solution)/shard_map/concatenate | solution.py:346
  2.7 7.4 %all-to-all-start = ((bf16[16,8,1600]{2,1,0:T(8,128)(2,1)}), bf16[16,8,1600]{2,1,0:T(8,128)(2,1)S(1)}, u32[]{:S(2)}, u32[]{:S(2)}) async-start(bf16[16,8,1600]{2,1,0:T(8,128)(2,1)} %pad_maximum_fusion), calls=%async_computation | async-start | bytes 851968 | tf_op jit(solution)/shard_map/all_to_all | solution.py:349
  10.1 1.1 %gather_fusion = f32[128]{0:T(128)S(1)} fusion(f32[50688]{0:T(1024)S(1)} %copy-done.9, s32[1024]{0:T(1024)S(1)} %pad_clamp_fusion), kind=kCustom, calls=%fused_computation | custom fusion | bytes 1536 | tf_op jit(solution)/shard_map/jit(_take)/gather | solution.py:351
  11.3 3.4 %arrange.1 = (bf16[4,1600,128]{2,1,0:T(8,128)(2,1)S(1)}, bf16[4,1600,128]{2,1,0:T(8,128)(2,1)S(1)}, bf16[4,1600,128]{2,1,0:T(8,128)(2,1)S(1)}, bf16[4,1600,128]{2,1,0:T(8,128)(2,1)S(1)}) custom-call(s32[1]{0:T(128)} %bitcast.3.me, bf16[320,2048]{1,0:T(8,128)(2,1)} %acts.1, bf16[1280,2048]{1,0:T(8,128)(2,1)} %grads.1), custom_call_target="tpu_custom_call" | custom-call | bytes 13107200 | tf_op jit(solution)/shard_map/arrange/pallas_call | solution.py:85
  14.7 1.2 %copy-done.1 = bf16[4,1600,128]{2,1,0:T(8,128)(2,1)} copy-done((bf16[4,1600,128]{2,1,0:T(8,128)(2,1)}, bf16[4,1600,128]{2,1,0:T(8,128)(2,1)S(1)}, u32[]{:S(2)}) %copy-start.1) | copy-done | bytes 1638424
  16.0 1.2 %copy-done.3 = bf16[4,1600,128]{2,1,0:T(8,128)(2,1)} copy-done((bf16[4,1600,128]{2,1,0:T(8,128)(2,1)}, bf16[4,1600,128]{2,1,0:T(8,128)(2,1)S(1)}, u32[]{:S(2)}) %copy-start.3) | copy-done | bytes 1638424
  17.1 1.2 %copy-done.6 = bf16[4,1600,128]{2,1,0:T(8,128)(2,1)} copy-done((bf16[4,1600,128]{2,1,0:T(8,128)(2,1)}, bf16[4,1600,128]{2,1,0:T(8,128)(2,1)S(1)}, u32[]{:S(2)}) %copy-start.6) | copy-done | bytes 1638424
  18.3 4.5 %all-to-all-done = bf16[16,8,1600]{2,1,0:T(8,128)(2,1)S(1)} async-done(((bf16[16,8,1600]{2,1,0:T(8,128)(2,1)}), bf16[16,8,1600]{2,1,0:T(8,128)(2,1)S(1)}, u32[]{:S(2)}, u32[]{:S(2)}) %all-to-all-start) | async-done | bytes 409632 | tf_op jit(solution)/shard_map/all_to_all | solution.py:349
  22.8 1.4 %copy-done.4 = bf16[4,1600,128]{2,1,0:T(8,128)(2,1)S(1)} copy-done((bf16[4,1600,128]{2,1,0:T(8,128)(2,1)S(1)}, bf16[4,1600,128]{2,1,0:T(8,128)(2,1)}, u32[]{:S(2)}) %copy-start.4) | copy-done | bytes 1638424
  24.2 1.4 %copy-done.7 = bf16[4,1600,128]{2,1,0:T(8,128)(2,1)S(1)} copy-done((bf16[4,1600,128]{2,1,0:T(8,128)(2,1)S(1)}, bf16[4,1600,128]{2,1,0:T(8,128)(2,1)}, u32[]{:S(2)}) %copy-start.7) | copy-done | bytes 1638424
  25.7 0.6 project.5
  26.3 0.2 collective-permute-start
  26.5 1.5 %collective-permute-start.1 = (bf16[128,1600]{1,0:T(8,128)(2,1)S(1)}, bf16[128,1600]{1,0:T(8,128)(2,1)S(1)}, u32[]{:S(2)}, u32[]{:S(2)}) collective-permute-start(bf16[128,1600]{1,0:T(8,128)(2,1)S(1)} %bitcast.11), channel_id=1, source_target_pairs={{0,16},{16,0},{1,17},{17,1},{2,18},{18,2},{3,19},{19,3},{4,20},{20... | collective-permute-start | bytes 1228808 | tf_op jit(solution)/shard_map/ppermute | solution.py:358
  28.0 0.0 copy-done.2
  28.0 0.6 project.4.refs_0_
  28.6 0.4 collective-permute-done.refs_1_
  29.0 0.2 merge.4
  29.3 0.8 collective-permute-start.2
  30.0 8.6 %collective-permute-done.1.factors = bf16[128,1600]{1,0:T(8,128)(2,1)S(1)} collective-permute-done((bf16[128,1600]{1,0:T(8,128)(2,1)S(1)}, bf16[128,1600]{1,0:T(8,128)(2,1)S(1)}, u32[]{:S(2)}, u32[]{:S(2)}) %collective-permute-start.1) | collective-permute-done | bytes 409632 | tf_op jit(solution)/shard_map/ppermute | solution.py:358
  38.7 1.9 %collective-permute-done.2.refs_2_ = s32[776,128]{1,0:T(8,128)S(1)} collective-permute-done((s32[776,128]{1,0:T(8,128)S(1)}, s32[776,128]{1,0:T(8,128)S(1)}, u32[]{:S(2)}, u32[]{:S(2)}) %collective-permute-start.2) | collective-permute-done | bytes 397344 | tf_op jit(solution)/shard_map/ppermute | solution.py:19
  40.6 0.7 project.7
  41.2 0.1 collective-permute-start.3
  41.3 0.7 project.6.refs_0_
  42.0 2.0 %collective-permute-done.3.refs_1_ = f32[8,256,128]{2,1,0:T(8,128)S(1)} collective-permute-done((f32[8,256,128]{2,1,0:T(8,128)S(1)}, f32[8,256,128]{2,1,0:T(8,128)S(1)}, u32[]{:S(2)}, u32[]{:S(2)}) %collective-permute-start.3) | collective-permute-done | bytes 1048608 | tf_op jit(solution)/shard_map/ppermute | solution.py:19
  44.0 0.2 merge.5
  44.2 1.0 %collective-permute-start.7 = (s32[776,128]{1,0:T(8,128)S(1)}, s32[776,128]{1,0:T(8,128)S(1)}, u32[]{:S(2)}, u32[]{:S(2)}) collective-permute-start(s32[776,128]{1,0:T(8,128)S(1)} %merge.5), channel_id=1, source_target_pairs={{0,2},{1,3},{2,0},{3,1},{4,6},{5,7},{6,4},{7,5},{8,10},{9,11},{10,... | collective-permute-start | bytes 1191944 | tf_op jit(solution)/shard_map/ppermute | solution.py:19
  45.2 0.3 merge.6
  45.4 0.0 copy-start.8
  45.5 1.3 %collective-permute-start.4 = (s32[200,128]{1,0:T(8,128)S(1)}, s32[200,128]{1,0:T(8,128)S(1)}, u32[]{:S(2)}, u32[]{:S(2)}) collective-permute-start(s32[200,128]{1,0:T(8,128)S(1)} %get-tuple-element.40), channel_id=1, source_target_pairs={{0,8},{1,9},{2,10},{3,11},{4,12},{5,13},{6,14},{7,15},{8,0},{9,1},... | collective-permute-start | bytes 307208 | tf_op jit(solution)/shard_map/ppermute | solution.py:19
  46.8 1.4 %collective-permute-start.5 = (s32[200,128]{1,0:T(8,128)S(1)}, s32[200,128]{1,0:T(8,128)S(1)}, u32[]{:S(2)}, u32[]{:S(2)}) collective-permute-start(s32[200,128]{1,0:T(8,128)S(1)} %get-tuple-element.41), channel_id=1, source_target_pairs={{0,4},{1,5},{2,6},{3,7},{4,0},{5,1},{6,2},{7,3},{8,12},{9,13},{10,... | collective-permute-start | bytes 307208 | tf_op jit(solution)/shard_map/ppermute | solution.py:19
  48.2 1.7 %collective-permute-start.6 = (s32[200,128]{1,0:T(8,128)S(1)}, s32[200,128]{1,0:T(8,128)S(1)}, u32[]{:S(2)}, u32[]{:S(2)}) collective-permute-start(s32[200,128]{1,0:T(8,128)S(1)} %get-tuple-element.42), channel_id=1, source_target_pairs={{0,12},{1,13},{2,14},{3,15},{4,8},{5,9},{6,10},{7,11},{8,4},{9,5},... | collective-permute-start | bytes 307208 | tf_op jit(solution)/shard_map/ppermute | solution.py:19
  49.9 5.6 %collective-permute-done.7.refs_2_ = s32[776,128]{1,0:T(8,128)S(1)} collective-permute-done((s32[776,128]{1,0:T(8,128)S(1)}, s32[776,128]{1,0:T(8,128)S(1)}, u32[]{:S(2)}, u32[]{:S(2)}) %collective-permute-start.7) | collective-permute-done | bytes 397344 | tf_op jit(solution)/shard_map/ppermute | solution.py:19
  55.5 0.3 merge.7
  55.8 2.0 %collective-permute-start.8 = (s32[200,128]{1,0:T(8,128)S(1)}, s32[200,128]{1,0:T(8,128)S(1)}, u32[]{:S(2)}, u32[]{:S(2)}) collective-permute-start(s32[200,128]{1,0:T(8,128)S(1)} %get-tuple-element.44), channel_id=1, source_target_pairs={{0,8},{1,9},{2,10},{3,11},{4,12},{5,13},{6,14},{7,15},{8,0},{9,1},... | collective-permute-start | bytes 307208 | tf_op jit(solution)/shard_map/ppermute | solution.py:19
  57.7 0.3 collective-permute-start.9
  58.1 0.0 collective-permute-done.4.refs_1_
  58.1 2.2 %collective-permute-start.10 = (s32[200,128]{1,0:T(8,128)S(1)}, s32[200,128]{1,0:T(8,128)S(1)}, u32[]{:S(2)}, u32[]{:S(2)}) collective-permute-start(s32[200,128]{1,0:T(8,128)S(1)} %get-tuple-element.46), channel_id=1, source_target_pairs={{0,12},{1,13},{2,14},{3,15},{4,8},{5,9},{6,10},{7,11},{8,4},{9,5},... | collective-permute-start | bytes 307208 | tf_op jit(solution)/shard_map/ppermute | solution.py:19
  60.2 0.0 collective-permute-done.5.refs_2_
  60.2 0.0 collective-permute-done.6.refs_3_
  60.2 0.1 partial_scores.1.refs_0_
  60.4 4.7 %collective-permute-done.8.refs_2_ = s32[200,128]{1,0:T(8,128)S(1)} collective-permute-done((s32[200,128]{1,0:T(8,128)S(1)}, s32[200,128]{1,0:T(8,128)S(1)}, u32[]{:S(2)}, u32[]{:S(2)}) %collective-permute-start.8) | collective-permute-done | bytes 102432 | tf_op jit(solution)/shard_map/ppermute | solution.py:19
  65.0 0.0 collective-permute-done.9.refs_3_
  65.0 1.1 %collective-permute-done.10.refs_4_ = s32[200,128]{1,0:T(8,128)S(1)} collective-permute-done((s32[200,128]{1,0:T(8,128)S(1)}, s32[200,128]{1,0:T(8,128)S(1)}, u32[]{:S(2)}, u32[]{:S(2)}) %collective-permute-start.10) | collective-permute-done | bytes 102432 | tf_op jit(solution)/shard_map/ppermute | solution.py:19
  66.2 1.1 %tails.1 = (f32[8,128]{1,0:T(8,128)}, f32[16,128]{1,0:T(8,128)S(1)}) custom-call(f32[8,128]{1,0:T(8,128)S(1)} %partial_scores.1.refs_0_, f32[1,256,128]{2,1,0:T(8,128)S(1)} %get-tuple-element.43.refs_1_, s32[200,128]{1,0:T(8,128)S(1)} %collective-permute-done.8.refs_2_, s32[200,128]{1,0:T(8,128)S(1)} %collective-permute-done.9.refs_3_, ...), custom_call_target="tpu_custom_call" | custom-call | tf_op jit(solution)/shard_map/tails/pallas_call | solution.py:393
  67.3 0.0 collective-permute-start.13
  67.3 0.9 %collective-permute-start.12 = (f32[16,128]{1,0:T(8,128)S(1)}, f32[16,128]{1,0:T(8,128)S(1)}, u32[]{:S(2)}, u32[]{:S(2)}) collective-permute-start(f32[16,128]{1,0:T(8,128)S(1)} %get-tuple-element.49.refs_0_.refs_5_), channel_id=1, source_target_pairs={{0,2},{1,3},{2,0},{3,1},{4,6},{5,7},{6,4},{7,5},{8,10},{9,11},{10,... | collective-permute-start | bytes 24584 | tf_op jit(solution)/shard_map/ppermute | solution.py:19
  68.2 1.0 %collective-permute-start.11 = (f32[16,128]{1,0:T(8,128)S(1)}, f32[16,128]{1,0:T(8,128)S(1)}, u32[]{:S(2)}, u32[]{:S(2)}) collective-permute-start(f32[16,128]{1,0:T(8,128)S(1)} %get-tuple-element.49.refs_0_.refs_5_), channel_id=1, source_target_pairs={{0,1},{1,0},{2,3},{3,2},{4,5},{5,4},{6,7},{7,6},{8,9},{9,8},{10,11... | collective-permute-start | bytes 24584 | tf_op jit(solution)/shard_map/ppermute | solution.py:19
  69.2 1.2 %collective-permute-done.13.refs_3_ = f32[16,128]{1,0:T(8,128)S(1)} collective-permute-done((f32[16,128]{1,0:T(8,128)S(1)}, f32[16,128]{1,0:T(8,128)S(1)}, u32[]{:S(2)}, u32[]{:S(2)}) %collective-permute-start.13) | collective-permute-done | bytes 8224 | tf_op jit(solution)/shard_map/ppermute | solution.py:19
  70.4 0.7 collective-permute-done.12.refs_2_
  71.0 0.0 collective-permute-done.11.refs_1_
  71.0 0.1 fold_group.1
  71.1 2.0 %collective-permute-start.16 = (f32[16,128]{1,0:T(8,128)S(1)}, f32[16,128]{1,0:T(8,128)S(1)}, u32[]{:S(2)}, u32[]{:S(2)}) collective-permute-start(f32[16,128]{1,0:T(8,128)S(1)} %get-tuple-element.50.refs_0_), channel_id=1, source_target_pairs={{0,12},{1,13},{2,14},{3,15},{4,8},{5,9},{6,10},{7,11},{8,4},{9,5},... | collective-permute-start | bytes 24584 | tf_op jit(solution)/shard_map/ppermute | solution.py:19
  73.1 1.3 %collective-permute-start.15 = (f32[16,128]{1,0:T(8,128)S(1)}, f32[16,128]{1,0:T(8,128)S(1)}, u32[]{:S(2)}, u32[]{:S(2)}) collective-permute-start(f32[16,128]{1,0:T(8,128)S(1)} %get-tuple-element.50.refs_0_), channel_id=1, source_target_pairs={{0,8},{1,9},{2,10},{3,11},{4,12},{5,13},{6,14},{7,15},{8,0},{9,1},... | collective-permute-start | bytes 24584 | tf_op jit(solution)/shard_map/ppermute | solution.py:19
  74.4 1.1 %collective-permute-start.14 = (f32[16,128]{1,0:T(8,128)S(1)}, f32[16,128]{1,0:T(8,128)S(1)}, u32[]{:S(2)}, u32[]{:S(2)}) collective-permute-start(f32[16,128]{1,0:T(8,128)S(1)} %get-tuple-element.50.refs_0_), channel_id=1, source_target_pairs={{0,4},{1,5},{2,6},{3,7},{4,0},{5,1},{6,2},{7,3},{8,12},{9,13},{10,... | collective-permute-start | bytes 24584 | tf_op jit(solution)/shard_map/ppermute | solution.py:19
  75.5 1.1 %collective-permute-done.16.refs_3_ = f32[16,128]{1,0:T(8,128)S(1)} collective-permute-done((f32[16,128]{1,0:T(8,128)S(1)}, f32[16,128]{1,0:T(8,128)S(1)}, u32[]{:S(2)}, u32[]{:S(2)}) %collective-permute-start.16) | collective-permute-done | bytes 8224 | tf_op jit(solution)/shard_map/ppermute | solution.py:19
  76.6 1.1 %collective-permute-done.15.refs_2_ = f32[16,128]{1,0:T(8,128)S(1)} collective-permute-done((f32[16,128]{1,0:T(8,128)S(1)}, f32[16,128]{1,0:T(8,128)S(1)}, u32[]{:S(2)}, u32[]{:S(2)}) %collective-permute-start.15) | collective-permute-done | bytes 8224 | tf_op jit(solution)/shard_map/ppermute | solution.py:19
  77.6 0.4 collective-permute-done.14.refs_1_
  78.1 0.7 finish.1
  (15 shorter events, 0.1 us)
Async XLA Ops:
  0.6 1.2 %copy-start = (bf16[16,20480]{1,0:T(8,128)(2,1)S(1)}, bf16[16,20480]{1,0:T(8,128)(2,1)}, u32[]{:S(2)}) copy-start(bf16[16,20480]{1,0:T(8,128)(2,1)} %param.10) | copy-start | bytes 1966084
  0.6 9.4 %copy-start.10 = (s32[128]{0:T(128)S(1)}, s32[128]{0:T(128)}, u32[]{:S(2)}) copy-start(s32[128]{0:T(128)} %param.11) | copy-start | bytes 1540
  0.7 9.5 %copy-start.9 = (f32[50688]{0:T(1024)S(1)}, f32[50688]{0:T(1024)}, u32[]{:S(2)}) copy-start(f32[50688]{0:T(1024)} %param.13) | copy-start | bytes 608260
  2.7 20.1 %all-to-all-start = ((bf16[16,8,1600]{2,1,0:T(8,128)(2,1)}), bf16[16,8,1600]{2,1,0:T(8,128)(2,1)S(1)}, u32[]{:S(2)}, u32[]{:S(2)}) async-start(bf16[16,8,1600]{2,1,0:T(8,128)(2,1)} %pad_maximum_fusion), calls=%async_computation | async-start | bytes 851968 | tf_op jit(solution)/shard_map/all_to_all | solution.py:349
  14.7 1.2 %copy-start.1 = (bf16[4,1600,128]{2,1,0:T(8,128)(2,1)}, bf16[4,1600,128]{2,1,0:T(8,128)(2,1)S(1)}, u32[]{:S(2)}) copy-start(bf16[4,1600,128]{2,1,0:T(8,128)(2,1)S(1)} %get-tuple-element.33.rest_1_) | copy-start | bytes 4915204
  16.0 1.2 %copy-start.3 = (bf16[4,1600,128]{2,1,0:T(8,128)(2,1)}, bf16[4,1600,128]{2,1,0:T(8,128)(2,1)S(1)}, u32[]{:S(2)}) copy-start(bf16[4,1600,128]{2,1,0:T(8,128)(2,1)S(1)} %get-tuple-element.34.rest_0_) | copy-start | bytes 4915204
  17.1 1.2 %copy-start.6 = (bf16[4,1600,128]{2,1,0:T(8,128)(2,1)}, bf16[4,1600,128]{2,1,0:T(8,128)(2,1)S(1)}, u32[]{:S(2)}) copy-start(bf16[4,1600,128]{2,1,0:T(8,128)(2,1)S(1)} %get-tuple-element.35.rest_1_) | copy-start | bytes 4915204
  22.8 1.4 %copy-start.4 = (bf16[4,1600,128]{2,1,0:T(8,128)(2,1)S(1)}, bf16[4,1600,128]{2,1,0:T(8,128)(2,1)}, u32[]{:S(2)}) copy-start(bf16[4,1600,128]{2,1,0:T(8,128)(2,1)} %copy-done.3) | copy-start | bytes 4915204
  24.2 1.4 %copy-start.7 = (bf16[4,1600,128]{2,1,0:T(8,128)(2,1)S(1)}, bf16[4,1600,128]{2,1,0:T(8,128)(2,1)}, u32[]{:S(2)}) copy-start(bf16[4,1600,128]{2,1,0:T(8,128)(2,1)} %copy-done.6) | copy-start | bytes 4915204
  25.7 2.3 %copy-start.2 = (bf16[4,1600,128]{2,1,0:T(8,128)(2,1)S(1)}, bf16[4,1600,128]{2,1,0:T(8,128)(2,1)}, u32[]{:S(2)}) copy-start(bf16[4,1600,128]{2,1,0:T(8,128)(2,1)} %copy-done.1) | copy-start | bytes 4915204
  26.3 2.7 %collective-permute-start = (f32[8,256,128]{2,1,0:T(8,128)S(1)}, f32[8,256,128]{2,1,0:T(8,128)S(1)}, u32[]{:S(2)}, u32[]{:S(2)}) collective-permute-start(f32[8,256,128]{2,1,0:T(8,128)S(1)} %project.5), channel_id=1, source_target_pairs={{0,1},{1,0},{2,3},{3,2},{4,5},{5,4},{6,7},{7,6},{8,9},{9,8},{10,11... | collective-permute-start | bytes 3145736 | tf_op jit(solution)/shard_map/ppermute | solution.py:19
  26.5 12.2 %collective-permute-start.1 = (bf16[128,1600]{1,0:T(8,128)(2,1)S(1)}, bf16[128,1600]{1,0:T(8,128)(2,1)S(1)}, u32[]{:S(2)}, u32[]{:S(2)}) collective-permute-start(bf16[128,1600]{1,0:T(8,128)(2,1)S(1)} %bitcast.11), channel_id=1, source_target_pairs={{0,16},{16,0},{1,17},{17,1},{2,18},{18,2},{3,19},{19,3},{4,20},{20... | collective-permute-start | bytes 1228808 | tf_op jit(solution)/shard_map/ppermute | solution.py:358
  28.6 11.9 %copy-start.5 = (bf16[4,1600,128]{2,1,0:T(8,128)(2,1)S(1)}, bf16[4,1600,128]{2,1,0:T(8,128)(2,1)}, u32[]{:S(2)}) copy-start(bf16[4,1600,128]{2,1,0:T(8,128)(2,1)} %copy-done.3) | copy-start | bytes 4915204
  29.3 11.3 %collective-permute-start.2 = (s32[776,128]{1,0:T(8,128)S(1)}, s32[776,128]{1,0:T(8,128)S(1)}, u32[]{:S(2)}, u32[]{:S(2)}) collective-permute-start(s32[776,128]{1,0:T(8,128)S(1)} %merge.4), channel_id=1, source_target_pairs={{0,2},{1,3},{2,0},{3,1},{4,6},{5,7},{6,4},{7,5},{8,10},{9,11},{10,... | collective-permute-start | bytes 1191944 | tf_op jit(solution)/shard_map/ppermute | solution.py:19
  41.2 2.7 %collective-permute-start.3 = (f32[8,256,128]{2,1,0:T(8,128)S(1)}, f32[8,256,128]{2,1,0:T(8,128)S(1)}, u32[]{:S(2)}, u32[]{:S(2)}) collective-permute-start(f32[8,256,128]{2,1,0:T(8,128)S(1)} %project.7), channel_id=1, source_target_pairs={{0,1},{1,0},{2,3},{3,2},{4,5},{5,4},{6,7},{7,6},{8,9},{9,8},{10,11... | collective-permute-start | bytes 3145736 | tf_op jit(solution)/shard_map/ppermute | solution.py:19
  44.2 11.3 %collective-permute-start.7 = (s32[776,128]{1,0:T(8,128)S(1)}, s32[776,128]{1,0:T(8,128)S(1)}, u32[]{:S(2)}, u32[]{:S(2)}) collective-permute-start(s32[776,128]{1,0:T(8,128)S(1)} %merge.5), channel_id=1, source_target_pairs={{0,2},{1,3},{2,0},{3,1},{4,6},{5,7},{6,4},{7,5},{8,10},{9,11},{10,... | collective-permute-start | bytes 1191944 | tf_op jit(solution)/shard_map/ppermute | solution.py:19
  45.4 20.7 %copy-start.8 = (s32[128]{0:T(128)S(1)}, s32[128]{0:T(128)}, u32[]{:S(2)}) copy-start(s32[128]{0:T(128)} %param.12) | copy-start | bytes 1540
  45.5 12.6 %collective-permute-start.4 = (s32[200,128]{1,0:T(8,128)S(1)}, s32[200,128]{1,0:T(8,128)S(1)}, u32[]{:S(2)}, u32[]{:S(2)}) collective-permute-start(s32[200,128]{1,0:T(8,128)S(1)} %get-tuple-element.40), channel_id=1, source_target_pairs={{0,8},{1,9},{2,10},{3,11},{4,12},{5,13},{6,14},{7,15},{8,0},{9,1},... | collective-permute-start | bytes 307208 | tf_op jit(solution)/shard_map/ppermute | solution.py:19
  46.8 13.5 %collective-permute-start.5 = (s32[200,128]{1,0:T(8,128)S(1)}, s32[200,128]{1,0:T(8,128)S(1)}, u32[]{:S(2)}, u32[]{:S(2)}) collective-permute-start(s32[200,128]{1,0:T(8,128)S(1)} %get-tuple-element.41), channel_id=1, source_target_pairs={{0,4},{1,5},{2,6},{3,7},{4,0},{5,1},{6,2},{7,3},{8,12},{9,13},{10,... | collective-permute-start | bytes 307208 | tf_op jit(solution)/shard_map/ppermute | solution.py:19
  48.2 12.0 %collective-permute-start.6 = (s32[200,128]{1,0:T(8,128)S(1)}, s32[200,128]{1,0:T(8,128)S(1)}, u32[]{:S(2)}, u32[]{:S(2)}) collective-permute-start(s32[200,128]{1,0:T(8,128)S(1)} %get-tuple-element.42), channel_id=1, source_target_pairs={{0,12},{1,13},{2,14},{3,15},{4,8},{5,9},{6,10},{7,11},{8,4},{9,5},... | collective-permute-start | bytes 307208 | tf_op jit(solution)/shard_map/ppermute | solution.py:19
  55.8 9.3 %collective-permute-start.8 = (s32[200,128]{1,0:T(8,128)S(1)}, s32[200,128]{1,0:T(8,128)S(1)}, u32[]{:S(2)}, u32[]{:S(2)}) collective-permute-start(s32[200,128]{1,0:T(8,128)S(1)} %get-tuple-element.44), channel_id=1, source_target_pairs={{0,8},{1,9},{2,10},{3,11},{4,12},{5,13},{6,14},{7,15},{8,0},{9,1},... | collective-permute-start | bytes 307208 | tf_op jit(solution)/shard_map/ppermute | solution.py:19
  57.7 7.3 %collective-permute-start.9 = (s32[200,128]{1,0:T(8,128)S(1)}, s32[200,128]{1,0:T(8,128)S(1)}, u32[]{:S(2)}, u32[]{:S(2)}) collective-permute-start(s32[200,128]{1,0:T(8,128)S(1)} %get-tuple-element.45), channel_id=1, source_target_pairs={{0,4},{1,5},{2,6},{3,7},{4,0},{5,1},{6,2},{7,3},{8,12},{9,13},{10,... | collective-permute-start | bytes 307208 | tf_op jit(solution)/shard_map/ppermute | solution.py:19
  58.1 8.1 %collective-permute-start.10 = (s32[200,128]{1,0:T(8,128)S(1)}, s32[200,128]{1,0:T(8,128)S(1)}, u32[]{:S(2)}, u32[]{:S(2)}) collective-permute-start(s32[200,128]{1,0:T(8,128)S(1)} %get-tuple-element.46), channel_id=1, source_target_pairs={{0,12},{1,13},{2,14},{3,15},{4,8},{5,9},{6,10},{7,11},{8,4},{9,5},... | collective-permute-start | bytes 307208 | tf_op jit(solution)/shard_map/ppermute | solution.py:19
  67.3 3.1 %collective-permute-start.13 = (f32[16,128]{1,0:T(8,128)S(1)}, f32[16,128]{1,0:T(8,128)S(1)}, u32[]{:S(2)}, u32[]{:S(2)}) collective-permute-start(f32[16,128]{1,0:T(8,128)S(1)} %get-tuple-element.49.refs_0_.refs_5_), channel_id=1, source_target_pairs={{0,3},{1,2},{2,1},{3,0},{4,7},{5,6},{6,5},{7,4},{8,11},{9,10},{10,... | collective-permute-start | bytes 24584 | tf_op jit(solution)/shard_map/ppermute | solution.py:19
  67.3 3.7 %collective-permute-start.12 = (f32[16,128]{1,0:T(8,128)S(1)}, f32[16,128]{1,0:T(8,128)S(1)}, u32[]{:S(2)}, u32[]{:S(2)}) collective-permute-start(f32[16,128]{1,0:T(8,128)S(1)} %get-tuple-element.49.refs_0_.refs_5_), channel_id=1, source_target_pairs={{0,2},{1,3},{2,0},{3,1},{4,6},{5,7},{6,4},{7,5},{8,10},{9,11},{10,... | collective-permute-start | bytes 24584 | tf_op jit(solution)/shard_map/ppermute | solution.py:19
  68.2 2.9 %collective-permute-start.11 = (f32[16,128]{1,0:T(8,128)S(1)}, f32[16,128]{1,0:T(8,128)S(1)}, u32[]{:S(2)}, u32[]{:S(2)}) collective-permute-start(f32[16,128]{1,0:T(8,128)S(1)} %get-tuple-element.49.refs_0_.refs_5_), channel_id=1, source_target_pairs={{0,1},{1,0},{2,3},{3,2},{4,5},{5,4},{6,7},{7,6},{8,9},{9,8},{10,11... | collective-permute-start | bytes 24584 | tf_op jit(solution)/shard_map/ppermute | solution.py:19
  71.1 5.5 %collective-permute-start.16 = (f32[16,128]{1,0:T(8,128)S(1)}, f32[16,128]{1,0:T(8,128)S(1)}, u32[]{:S(2)}, u32[]{:S(2)}) collective-permute-start(f32[16,128]{1,0:T(8,128)S(1)} %get-tuple-element.50.refs_0_), channel_id=1, source_target_pairs={{0,12},{1,13},{2,14},{3,15},{4,8},{5,9},{6,10},{7,11},{8,4},{9,5},... | collective-permute-start | bytes 24584 | tf_op jit(solution)/shard_map/ppermute | solution.py:19
  73.1 4.5 %collective-permute-start.15 = (f32[16,128]{1,0:T(8,128)S(1)}, f32[16,128]{1,0:T(8,128)S(1)}, u32[]{:S(2)}, u32[]{:S(2)}) collective-permute-start(f32[16,128]{1,0:T(8,128)S(1)} %get-tuple-element.50.refs_0_), channel_id=1, source_target_pairs={{0,8},{1,9},{2,10},{3,11},{4,12},{5,13},{6,14},{7,15},{8,0},{9,1},... | collective-permute-start | bytes 24584 | tf_op jit(solution)/shard_map/ppermute | solution.py:19
  74.4 3.7 %collective-permute-start.14 = (f32[16,128]{1,0:T(8,128)S(1)}, f32[16,128]{1,0:T(8,128)S(1)}, u32[]{:S(2)}, u32[]{:S(2)}) collective-permute-start(f32[16,128]{1,0:T(8,128)S(1)} %get-tuple-element.50.refs_0_), channel_id=1, source_target_pairs={{0,4},{1,5},{2,6},{3,7},{4,0},{5,1},{6,2},{7,3},{8,12},{9,13},{10,... | collective-permute-start | bytes 24584 | tf_op jit(solution)/shard_map/ppermute | solution.py:19

commit v4 on v3

--- a/solution.py
+++ b/solution.py
@@ -12,6 +12,10 @@
 PIECES = 4
 CHUNKS = ((1,), (1,))
 F32 = jnp.float32
+BITS = 18
+GROUPS, WORDS = 16, 9
+RANGE = 24.0
+LEVELS = (1 << (BITS - 1)) - 1
 
 
 def swap(value, axis, offset):
@@ -143,38 +147,63 @@
 
 
 def message_rows(blocks, rows):
-    return blocks * rows // 4 * 3 + -(-blocks // 8) * 8
+    return blocks * rows // GROUPS * WORDS + -(-blocks // 8) * 8
+
+
+def spread():
+    spare = 32 - BITS
+    places = []
+    for j in range(GROUPS - WORDS):
+        start = j * BITS
+        while start < (j + 1) * BITS:
+            word = start // spare
+            end = min((j + 1) * BITS, (word + 1) * spare)
+            places.append((j, word, start - j * BITS, BITS + start - word * spare, end - start))
+            start = end
+    return places
 
 
 def encode(out, block, blocks, value):
-    size = value.shape[0] // 4
+    size = value.shape[0] // GROUPS
+    half = value.shape[0] // 2
     codes, powers = [], None
-    for g in range(4):
-        group = value[g * size : (g + 1) * size]
-        most = jnp.max(jnp.abs(group), axis=0, keepdims=True)
-        power = jnp.clip(jnp.floor(jnp.log(most) * (1 / math.log(2.0))) + 2.0, -100.0, 100.0)
-        codes.append(jnp.floor(group * jnp.exp2(23.0 - power) + 0.5).astype(jnp.int32))
-        byte = (power.astype(jnp.int32) + 128) << (8 * g)
+    for side in range(2):
+        part = value[side * half : (side + 1) * half]
+        logs = jnp.log(jnp.abs(part)) * (1 / math.log(2.0))
+        top = jnp.clip(jnp.ceil(jnp.max(logs, axis=0, keepdims=True)), -100.0, 100.0)
+        steps = jnp.maximum((logs + (RANGE - top)) * (LEVELS / RANGE) + 0.5, 0.0)
+        code = jnp.minimum(steps, float(LEVELS)).astype(jnp.int32)
+        code = jnp.where(part < 0, code | (LEVELS + 1), code)
+        codes.extend(code[g * size : (g + 1) * size] for g in range(GROUPS // 2))
+        byte = (top.astype(jnp.int32) + 128) << (8 * side)
         powers = byte if powers is None else powers | byte
-    for g in range(3):
-        high = lax.shift_right_arithmetic(codes[3], 8 * g) << 24
-        words = (codes[g] & 0xFFFFFF) | high
-        out[pl.ds((3 * block + g) * size, size), :] = words
-    out[pl.ds(3 * blocks * size + block, 1), :] = powers
+    words = codes[:WORDS]
+    for j, word, low, shift, bits in spread():
+        piece = lax.shift_right_logical(codes[WORDS + j], low) & ((1 << bits) - 1)
+        words[word] = words[word] | (piece << shift)
+    for g, word in enumerate(words):
+        out[pl.ds((WORDS * block + g) * size, size), :] = word
+    out[pl.ds(WORDS * blocks * size + block, 1), :] = powers
 
 
 def decode(ref, block, blocks, rows):
-    size = rows // 4
-    words = [ref[pl.ds((3 * block + g) * size, size), :] for g in range(3)]
-    powers = ref[pl.ds(3 * blocks * size + block, 1), :]
-    codes = [lax.shift_right_arithmetic(word << 8, 8) for word in words]
-    low = lax.shift_right_logical(words[0], 24) | (lax.shift_right_logical(words[1], 24) << 8)
-    codes.append(low | (lax.shift_right_arithmetic(words[2], 24) << 16))
-    groups = []
-    for g, code in enumerate(codes):
-        power = (lax.shift_right_logical(powers, 8 * g) & 0xFF) - 128
-        groups.append(code.astype(F32) * jnp.exp2(power.astype(F32) - 23.0))
-    return jnp.concatenate(groups, axis=0)
+    size = rows // GROUPS
+    words = [ref[pl.ds((WORDS * block + g) * size, size), :] for g in range(WORDS)]
+    powers = ref[pl.ds(WORDS * blocks * size + block, 1), :]
+    codes = [word & ((1 << BITS) - 1) for word in words] + [None] * (GROUPS - WORDS)
+    for j, word, low, shift, bits in spread():
+        piece = (lax.shift_right_logical(words[word], shift) & ((1 << bits) - 1)) << low
+        code = codes[WORDS + j]
+        codes[WORDS + j] = piece if code is None else code | piece
+    parts = []
+    for side in range(2):
+        top = ((lax.shift_right_logical(powers, 8 * side) & 0xFF) - 128).astype(F32)
+        code = jnp.concatenate(codes[side * GROUPS // 2 : (side + 1) * GROUPS // 2], axis=0)
+        level = code & LEVELS
+        size_of = jnp.exp2(level.astype(F32) * (RANGE / LEVELS) + (top - RANGE))
+        size_of = jnp.where(level == 0, 0.0, size_of)
+        parts.append(jnp.where(code > LEVELS, -size_of, size_of))
+    return jnp.concatenate(parts, axis=0)
 
 
 def total_of(refs, starts, block, blocks, rows):

time: 79.1 us -> 73.6 us (0.930)
  waiting for transfers between devices: 33.2 us -> 26.8 us
  Pallas kernels: 9.06 us -> 10.1 us
    ppermute x16, waiting for transfers between devices: 20.1 us -> 13.8 us  [swap(): return lax.ppermute(value, axis, [(i, i ^ offset) for i in range(size)])]
    pallas_call x4, Pallas kernels: 1 us -> 1.8 us  [merge(): pl.pallas_call(functools.partial(merge_kernel, starts, blocks, rows, stay...]
  transfers between devices with their start and end apart: 18 -> 18, of which waited for: 13 -> 11; matrix products, arithmetic and copies ran while one was open for 1% -> 2% of each run, Pallas kernels for 7% -> 9%
where the time goes in v4:
time: 73.6 us; the launch traced here: 73.3 us
  waiting for transfers between devices  26.8 us (36%)
  starting transfers between devices  26 us (35%)
  Pallas kernels  10.1 us (14%)
  local copies, waits for them, and re-layouts  8.78 us (12%)
  between operations  0.85 us (1%)
  other arithmetic  0.84 us (1%)
    ppermute x16, starting transfers between devices, swap(): return lax.ppermute(value, axis, [(i, i ^ offset) for i in range(size)])  17.1 us
    ppermute x16, waiting for transfers between devices, swap(): return lax.ppermute(value, axis, [(i, i ^ offset) for i in range(size)])  13.8 us
    ppermute x1, waiting for transfers between devices, local(): other = lax.ppermute(own, 'groups', [(i, i ^ 1) for i in range(groups)])  8.49 us
    all_to_all x1, starting transfers between devices, local(): lax.all_to_all(outgoing, 'loop', split_axis=0, concat_axis=0, tiled=True)  7.39 us
    unnamed x22, local copies, waits for them, and re-layouts  6.47 us
    all_to_all x1, waiting for transfers between devices, local(): lax.all_to_all(outgoing, 'loop', split_axis=0, concat_axis=0, tiled=True)  4.48 us
    pallas_call x1, Pallas kernels, arrange(): pl.pallas_call(arrange_kernel, in_specs=[pl.BlockSpec(memory_space=pltpu....  3.44 us
    pallas_call x4, Pallas kernels, project(): pl.pallas_call(functools.partial(project_kernel, depths, len(columns)), o...  2.59 us
  transfers between devices with their start and end apart: 18, of which 11 were waited for; matrix products, arithmetic and copies ran while one was open for 2% of the time, Pallas kernels for 9%

profile of v4, /device:TPU:0, one launch (start us, length us, event | category | flops | bytes accessed | tf_op | source)
XLA Modules:
  0.0 73.3 jit_solution(13157580308768869783)
XLA Ops:
  0.6 0.0 copy-start
  0.6 0.0 copy-start.10
  0.7 0.0 copy-start.9
  0.7 1.0 %constant_dynamic-slice_fusion = bf16[8,5120]{1,0:T(8,128)(2,1)S(1)} fusion(bf16[16,5120]{1,0:T(8,128)(2,1)} %param.9, s32[]{:T(128)S(6)} %select_n.4), kind=kLoop, calls=%fused_computation.3 | loop fusion | bytes 163844 | tf_op jit(solution)/shard_map/dynamic_slice | solution.py:370
  1.6 0.1 reshape.17
  1.9 0.8 %pad_maximum_fusion = bf16[16,8,1600]{2,1,0:T(8,128)(2,1)} fusion(bf16[16,8,320]{2,1,0:T(8,128)(2,1)S(1)} %copy.9, bf16[16,8,1280]{2,1,0:T(8,128)(2,1)S(1)} %bitcast.15), kind=kLoop, calls=%fused_computation.1 | loop fusion | flops 819200 | bytes 819200 | tf_op jit(solution)/shard_map/concatenate | solution.py:375
  2.7 7.4 %all-to-all-start = ((bf16[16,8,1600]{2,1,0:T(8,128)(2,1)}), bf16[16,8,1600]{2,1,0:T(8,128)(2,1)S(1)}, u32[]{:S(2)}, u32[]{:S(2)}) async-start(bf16[16,8,1600]{2,1,0:T(8,128)(2,1)} %pad_maximum_fusion), calls=%async_computation | async-start | bytes 851968 | tf_op jit(solution)/shard_map/all_to_all | solution.py:378
  10.1 0.0 copy-done.10
  10.1 0.0 copy-done.9
  10.1 1.1 %gather_fusion = f32[128]{0:T(128)S(1)} fusion(f32[50688]{0:T(1024)S(1)} %copy-done.9, s32[1024]{0:T(1024)S(1)} %pad_clamp_fusion), kind=kCustom, calls=%fused_computation | custom fusion | bytes 1536 | tf_op jit(solution)/shard_map/jit(_take)/gather | solution.py:380
  11.3 3.4 %arrange.1 = (bf16[4,1600,128]{2,1,0:T(8,128)(2,1)S(1)}, bf16[4,1600,128]{2,1,0:T(8,128)(2,1)S(1)}, bf16[4,1600,128]{2,1,0:T(8,128)(2,1)S(1)}, bf16[4,1600,128]{2,1,0:T(8,128)(2,1)S(1)}) custom-call(s32[1]{0:T(128)} %bitcast.3.me, bf16[320,2048]{1,0:T(8,128)(2,1)} %acts.1, bf16[1280,2048]{1,0:T(8,128)(2,1)} %grads.1), custom_call_target="tpu_custom_call" | custom-call | bytes 13107200 | tf_op jit(solution)/shard_map/arrange/pallas_call | solution.py:89
  14.7 1.2 %copy-done.1 = bf16[4,1600,128]{2,1,0:T(8,128)(2,1)} copy-done((bf16[4,1600,128]{2,1,0:T(8,128)(2,1)}, bf16[4,1600,128]{2,1,0:T(8,128)(2,1)S(1)}, u32[]{:S(2)}) %copy-start.1) | copy-done | bytes 1638424
  16.0 1.2 %copy-done.3 = bf16[4,1600,128]{2,1,0:T(8,128)(2,1)} copy-done((bf16[4,1600,128]{2,1,0:T(8,128)(2,1)}, bf16[4,1600,128]{2,1,0:T(8,128)(2,1)S(1)}, u32[]{:S(2)}) %copy-start.3) | copy-done | bytes 1638424
  17.1 1.2 %copy-done.6 = bf16[4,1600,128]{2,1,0:T(8,128)(2,1)} copy-done((bf16[4,1600,128]{2,1,0:T(8,128)(2,1)}, bf16[4,1600,128]{2,1,0:T(8,128)(2,1)S(1)}, u32[]{:S(2)}) %copy-start.6) | copy-done | bytes 1638424
  18.3 4.5 %all-to-all-done = bf16[16,8,1600]{2,1,0:T(8,128)(2,1)S(1)} async-done(((bf16[16,8,1600]{2,1,0:T(8,128)(2,1)}), bf16[16,8,1600]{2,1,0:T(8,128)(2,1)S(1)}, u32[]{:S(2)}, u32[]{:S(2)}) %all-to-all-start) | async-done | bytes 409632 | tf_op jit(solution)/shard_map/all_to_all | solution.py:378
  22.8 1.4 %copy-done.4 = bf16[4,1600,128]{2,1,0:T(8,128)(2,1)S(1)} copy-done((bf16[4,1600,128]{2,1,0:T(8,128)(2,1)S(1)}, bf16[4,1600,128]{2,1,0:T(8,128)(2,1)}, u32[]{:S(2)}) %copy-start.4) | copy-done | bytes 1638424
  24.2 1.4 %copy-done.7 = bf16[4,1600,128]{2,1,0:T(8,128)(2,1)S(1)} copy-done((bf16[4,1600,128]{2,1,0:T(8,128)(2,1)S(1)}, bf16[4,1600,128]{2,1,0:T(8,128)(2,1)}, u32[]{:S(2)}) %copy-start.7) | copy-done | bytes 1638424
  25.7 0.6 project.5
  26.3 0.2 collective-permute-start
  26.5 1.5 %collective-permute-start.1 = (bf16[128,1600]{1,0:T(8,128)(2,1)S(1)}, bf16[128,1600]{1,0:T(8,128)(2,1)S(1)}, u32[]{:S(2)}, u32[]{:S(2)}) collective-permute-start(bf16[128,1600]{1,0:T(8,128)(2,1)S(1)} %bitcast.11), channel_id=1, source_target_pairs={{0,16},{16,0},{1,17},{17,1},{2,18},{18,2},{3,19},{19,3},{4,20},{20... | collective-permute-start | bytes 1228808 | tf_op jit(solution)/shard_map/ppermute | solution.py:387
  28.0 0.6 project.4.refs_0_
  28.6 0.4 collective-permute-done.refs_1_
  29.0 0.4 merge.4
  29.4 0.8 %collective-permute-start.2 = (s32[584,128]{1,0:T(8,128)S(1)}, s32[584,128]{1,0:T(8,128)S(1)}, u32[]{:S(2)}, u32[]{:S(2)}) collective-permute-start(s32[584,128]{1,0:T(8,128)S(1)} %merge.4), channel_id=1, source_target_pairs={{0,2},{1,3},{2,0},{3,1},{4,6},{5,7},{6,4},{7,5},{8,10},{9,11},{10,... | collective-permute-start | bytes 897032 | tf_op jit(solution)/shard_map/ppermute | solution.py:23
  30.2 8.5 %collective-permute-done.1.factors = bf16[128,1600]{1,0:T(8,128)(2,1)S(1)} collective-permute-done((bf16[128,1600]{1,0:T(8,128)(2,1)S(1)}, bf16[128,1600]{1,0:T(8,128)(2,1)S(1)}, u32[]{:S(2)}, u32[]{:S(2)}) %collective-permute-start.1) | collective-permute-done | bytes 409632 | tf_op jit(solution)/shard_map/ppermute | solution.py:387
  38.7 0.0 collective-permute-done.2.refs_2_
  38.7 0.7 project.7
  39.3 0.1 collective-permute-start.3
  39.4 0.7 project.6.refs_0_
  40.1 2.0 %collective-permute-done.3.refs_1_ = f32[8,256,128]{2,1,0:T(8,128)S(1)} collective-permute-done((f32[8,256,128]{2,1,0:T(8,128)S(1)}, f32[8,256,128]{2,1,0:T(8,128)S(1)}, u32[]{:S(2)}, u32[]{:S(2)}) %collective-permute-start.3) | collective-permute-done | bytes 1048608 | tf_op jit(solution)/shard_map/ppermute | solution.py:23
  42.1 0.4 merge.5
  42.4 0.9 %collective-permute-start.7 = (s32[584,128]{1,0:T(8,128)S(1)}, s32[584,128]{1,0:T(8,128)S(1)}, u32[]{:S(2)}, u32[]{:S(2)}) collective-permute-start(s32[584,128]{1,0:T(8,128)S(1)} %merge.5), channel_id=1, source_target_pairs={{0,2},{1,3},{2,0},{3,1},{4,6},{5,7},{6,4},{7,5},{8,10},{9,11},{10,... | collective-permute-start | bytes 897032 | tf_op jit(solution)/shard_map/ppermute | solution.py:23
  43.3 0.5 merge.6
  43.9 0.0 copy-start.8
  43.9 1.3 %collective-permute-start.4 = (s32[152,128]{1,0:T(8,128)S(1)}, s32[152,128]{1,0:T(8,128)S(1)}, u32[]{:S(2)}, u32[]{:S(2)}) collective-permute-start(s32[152,128]{1,0:T(8,128)S(1)} %get-tuple-element.40), channel_id=1, source_target_pairs={{0,8},{1,9},{2,10},{3,11},{4,12},{5,13},{6,14},{7,15},{8,0},{9,1},... | collective-permute-start | bytes 233480 | tf_op jit(solution)/shard_map/ppermute | solution.py:23
  45.2 1.4 %collective-permute-start.5 = (s32[152,128]{1,0:T(8,128)S(1)}, s32[152,128]{1,0:T(8,128)S(1)}, u32[]{:S(2)}, u32[]{:S(2)}) collective-permute-start(s32[152,128]{1,0:T(8,128)S(1)} %get-tuple-element.41), channel_id=1, source_target_pairs={{0,4},{1,5},{2,6},{3,7},{4,0},{5,1},{6,2},{7,3},{8,12},{9,13},{10,... | collective-permute-start | bytes 233480 | tf_op jit(solution)/shard_map/ppermute | solution.py:23
  46.7 1.7 %collective-permute-start.6 = (s32[152,128]{1,0:T(8,128)S(1)}, s32[152,128]{1,0:T(8,128)S(1)}, u32[]{:S(2)}, u32[]{:S(2)}) collective-permute-start(s32[152,128]{1,0:T(8,128)S(1)} %get-tuple-element.42), channel_id=1, source_target_pairs={{0,12},{1,13},{2,14},{3,15},{4,8},{5,9},{6,10},{7,11},{8,4},{9,5},... | collective-permute-start | bytes 233480 | tf_op jit(solution)/shard_map/ppermute | solution.py:23
  48.4 3.3 %collective-permute-done.7.refs_2_ = s32[584,128]{1,0:T(8,128)S(1)} collective-permute-done((s32[584,128]{1,0:T(8,128)S(1)}, s32[584,128]{1,0:T(8,128)S(1)}, u32[]{:S(2)}, u32[]{:S(2)}) %collective-permute-start.7) | collective-permute-done | bytes 299040 | tf_op jit(solution)/shard_map/ppermute | solution.py:23
  51.6 0.5 merge.7
  52.2 1.9 %collective-permute-start.8 = (s32[152,128]{1,0:T(8,128)S(1)}, s32[152,128]{1,0:T(8,128)S(1)}, u32[]{:S(2)}, u32[]{:S(2)}) collective-permute-start(s32[152,128]{1,0:T(8,128)S(1)} %get-tuple-element.44), channel_id=1, source_target_pairs={{0,8},{1,9},{2,10},{3,11},{4,12},{5,13},{6,14},{7,15},{8,0},{9,1},... | collective-permute-start | bytes 233480 | tf_op jit(solution)/shard_map/ppermute | solution.py:23
  54.1 0.3 collective-permute-start.9
  54.4 0.0 collective-permute-done.4.refs_1_
  54.4 2.2 %collective-permute-start.10 = (s32[152,128]{1,0:T(8,128)S(1)}, s32[152,128]{1,0:T(8,128)S(1)}, u32[]{:S(2)}, u32[]{:S(2)}) collective-permute-start(s32[152,128]{1,0:T(8,128)S(1)} %get-tuple-element.46), channel_id=1, source_target_pairs={{0,12},{1,13},{2,14},{3,15},{4,8},{5,9},{6,10},{7,11},{8,4},{9,5},... | collective-permute-start | bytes 233480 | tf_op jit(solution)/shard_map/ppermute | solution.py:23
  56.6 0.0 collective-permute-done.5.refs_2_
  56.6 0.0 collective-permute-done.6.refs_3_
  56.6 0.2 partial_scores.1.refs_0_
  56.8 3.0 %collective-permute-done.8.refs_2_ = s32[152,128]{1,0:T(8,128)S(1)} collective-permute-done((s32[152,128]{1,0:T(8,128)S(1)}, s32[152,128]{1,0:T(8,128)S(1)}, u32[]{:S(2)}, u32[]{:S(2)}) %collective-permute-start.8) | collective-permute-done | bytes 77856 | tf_op jit(solution)/shard_map/ppermute | solution.py:23
  59.8 0.0 collective-permute-done.9.refs_3_
  59.8 1.0 %collective-permute-done.10.refs_4_ = s32[152,128]{1,0:T(8,128)S(1)} collective-permute-done((s32[152,128]{1,0:T(8,128)S(1)}, s32[152,128]{1,0:T(8,128)S(1)}, u32[]{:S(2)}, u32[]{:S(2)}) %collective-permute-start.10) | collective-permute-done | bytes 77856 | tf_op jit(solution)/shard_map/ppermute | solution.py:23
  60.9 1.2 %tails.1 = (f32[8,128]{1,0:T(8,128)}, f32[16,128]{1,0:T(8,128)S(1)}) custom-call(f32[8,128]{1,0:T(8,128)S(1)} %partial_scores.1.refs_0_, f32[1,256,128]{2,1,0:T(8,128)S(1)} %get-tuple-element.43.refs_1_, s32[152,128]{1,0:T(8,128)S(1)} %collective-permute-done.8.refs_2_, s32[152,128]{1,0:T(8,128)S(1)} %collective-permute-done.9.refs_3_, ...), custom_call_target="tpu_custom_call" | custom-call | tf_op jit(solution)/shard_map/tails/pallas_call | solution.py:422
  62.1 0.0 collective-permute-start.13
  62.1 1.3 %collective-permute-start.12 = (f32[16,128]{1,0:T(8,128)S(1)}, f32[16,128]{1,0:T(8,128)S(1)}, u32[]{:S(2)}, u32[]{:S(2)}) collective-permute-start(f32[16,128]{1,0:T(8,128)S(1)} %get-tuple-element.49.refs_0_.refs_5_), channel_id=1, source_target_pairs={{0,2},{1,3},{2,0},{3,1},{4,6},{5,7},{6,4},{7,5},{8,10},{9,11},{10,... | collective-permute-start | bytes 24584 | tf_op jit(solution)/shard_map/ppermute | solution.py:23
  63.4 0.6 collective-permute-start.11
  64.0 1.2 %collective-permute-done.13.refs_3_ = f32[16,128]{1,0:T(8,128)S(1)} collective-permute-done((f32[16,128]{1,0:T(8,128)S(1)}, f32[16,128]{1,0:T(8,128)S(1)}, u32[]{:S(2)}, u32[]{:S(2)}) %collective-permute-start.13) | collective-permute-done | bytes 8224 | tf_op jit(solution)/shard_map/ppermute | solution.py:23
  65.2 0.6 collective-permute-done.12.refs_2_
  65.8 0.0 collective-permute-done.11.refs_1_
  65.8 0.1 fold_group.1
  65.9 2.1 %collective-permute-start.16 = (f32[16,128]{1,0:T(8,128)S(1)}, f32[16,128]{1,0:T(8,128)S(1)}, u32[]{:S(2)}, u32[]{:S(2)}) collective-permute-start(f32[16,128]{1,0:T(8,128)S(1)} %get-tuple-element.50.refs_0_), channel_id=1, source_target_pairs={{0,12},{1,13},{2,14},{3,15},{4,8},{5,9},{6,10},{7,11},{8,4},{9,5},... | collective-permute-start | bytes 24584 | tf_op jit(solution)/shard_map/ppermute | solution.py:23
  68.0 0.8 %collective-permute-start.15 = (f32[16,128]{1,0:T(8,128)S(1)}, f32[16,128]{1,0:T(8,128)S(1)}, u32[]{:S(2)}, u32[]{:S(2)}) collective-permute-start(f32[16,128]{1,0:T(8,128)S(1)} %get-tuple-element.50.refs_0_), channel_id=1, source_target_pairs={{0,8},{1,9},{2,10},{3,11},{4,12},{5,13},{6,14},{7,15},{8,0},{9,1},... | collective-permute-start | bytes 24584 | tf_op jit(solution)/shard_map/ppermute | solution.py:23
  68.8 1.5 %collective-permute-start.14 = (f32[16,128]{1,0:T(8,128)S(1)}, f32[16,128]{1,0:T(8,128)S(1)}, u32[]{:S(2)}, u32[]{:S(2)}) collective-permute-start(f32[16,128]{1,0:T(8,128)S(1)} %get-tuple-element.50.refs_0_), channel_id=1, source_target_pairs={{0,4},{1,5},{2,6},{3,7},{4,0},{5,1},{6,2},{7,3},{8,12},{9,13},{10,... | collective-permute-start | bytes 24584 | tf_op jit(solution)/shard_map/ppermute | solution.py:23
  70.3 1.1 %collective-permute-done.16.refs_3_ = f32[16,128]{1,0:T(8,128)S(1)} collective-permute-done((f32[16,128]{1,0:T(8,128)S(1)}, f32[16,128]{1,0:T(8,128)S(1)}, u32[]{:S(2)}, u32[]{:S(2)}) %collective-permute-start.16) | collective-permute-done | bytes 8224 | tf_op jit(solution)/shard_map/ppermute | solution.py:23
  71.3 1.2 %collective-permute-done.15.refs_2_ = f32[16,128]{1,0:T(8,128)S(1)} collective-permute-done((f32[16,128]{1,0:T(8,128)S(1)}, f32[16,128]{1,0:T(8,128)S(1)}, u32[]{:S(2)}, u32[]{:S(2)}) %collective-permute-start.15) | collective-permute-done | bytes 8224 | tf_op jit(solution)/shard_map/ppermute | solution.py:23
  72.6 0.0 collective-permute-done.14.refs_1_
  72.6 0.7 finish.1
  (15 shorter events, 0.1 us)
Async XLA Ops:
  0.6 1.2 %copy-start = (bf16[16,20480]{1,0:T(8,128)(2,1)S(1)}, bf16[16,20480]{1,0:T(8,128)(2,1)}, u32[]{:S(2)}) copy-start(bf16[16,20480]{1,0:T(8,128)(2,1)} %param.10) | copy-start | bytes 1966084
  0.6 9.4 %copy-start.10 = (s32[128]{0:T(128)S(1)}, s32[128]{0:T(128)}, u32[]{:S(2)}) copy-start(s32[128]{0:T(128)} %param.11) | copy-start | bytes 1540
  0.7 9.5 %copy-start.9 = (f32[50688]{0:T(1024)S(1)}, f32[50688]{0:T(1024)}, u32[]{:S(2)}) copy-start(f32[50688]{0:T(1024)} %param.13) | copy-start | bytes 608260
  2.7 20.1 %all-to-all-start = ((bf16[16,8,1600]{2,1,0:T(8,128)(2,1)}), bf16[16,8,1600]{2,1,0:T(8,128)(2,1)S(1)}, u32[]{:S(2)}, u32[]{:S(2)}) async-start(bf16[16,8,1600]{2,1,0:T(8,128)(2,1)} %pad_maximum_fusion), calls=%async_computation | async-start | bytes 851968 | tf_op jit(solution)/shard_map/all_to_all | solution.py:378
  14.7 1.2 %copy-start.1 = (bf16[4,1600,128]{2,1,0:T(8,128)(2,1)}, bf16[4,1600,128]{2,1,0:T(8,128)(2,1)S(1)}, u32[]{:S(2)}) copy-start(bf16[4,1600,128]{2,1,0:T(8,128)(2,1)S(1)} %get-tuple-element.33.rest_1_) | copy-start | bytes 4915204
  16.0 1.2 %copy-start.3 = (bf16[4,1600,128]{2,1,0:T(8,128)(2,1)}, bf16[4,1600,128]{2,1,0:T(8,128)(2,1)S(1)}, u32[]{:S(2)}) copy-start(bf16[4,1600,128]{2,1,0:T(8,128)(2,1)S(1)} %get-tuple-element.34.rest_0_) | copy-start | bytes 4915204
  17.1 1.2 %copy-start.6 = (bf16[4,1600,128]{2,1,0:T(8,128)(2,1)}, bf16[4,1600,128]{2,1,0:T(8,128)(2,1)S(1)}, u32[]{:S(2)}) copy-start(bf16[4,1600,128]{2,1,0:T(8,128)(2,1)S(1)} %get-tuple-element.35.rest_1_) | copy-start | bytes 4915204
  22.8 1.4 %copy-start.4 = (bf16[4,1600,128]{2,1,0:T(8,128)(2,1)S(1)}, bf16[4,1600,128]{2,1,0:T(8,128)(2,1)}, u32[]{:S(2)}) copy-start(bf16[4,1600,128]{2,1,0:T(8,128)(2,1)} %copy-done.3) | copy-start | bytes 4915204
  24.2 1.4 %copy-start.7 = (bf16[4,1600,128]{2,1,0:T(8,128)(2,1)S(1)}, bf16[4,1600,128]{2,1,0:T(8,128)(2,1)}, u32[]{:S(2)}) copy-start(bf16[4,1600,128]{2,1,0:T(8,128)(2,1)} %copy-done.6) | copy-start | bytes 4915204
  25.7 2.3 %copy-start.2 = (bf16[4,1600,128]{2,1,0:T(8,128)(2,1)S(1)}, bf16[4,1600,128]{2,1,0:T(8,128)(2,1)}, u32[]{:S(2)}) copy-start(bf16[4,1600,128]{2,1,0:T(8,128)(2,1)} %copy-done.1) | copy-start | bytes 4915204
  26.3 2.7 %collective-permute-start = (f32[8,256,128]{2,1,0:T(8,128)S(1)}, f32[8,256,128]{2,1,0:T(8,128)S(1)}, u32[]{:S(2)}, u32[]{:S(2)}) collective-permute-start(f32[8,256,128]{2,1,0:T(8,128)S(1)} %project.5), channel_id=1, source_target_pairs={{0,1},{1,0},{2,3},{3,2},{4,5},{5,4},{6,7},{7,6},{8,9},{9,8},{10,11... | collective-permute-start | bytes 3145736 | tf_op jit(solution)/shard_map/ppermute | solution.py:23
  26.5 12.2 %collective-permute-start.1 = (bf16[128,1600]{1,0:T(8,128)(2,1)S(1)}, bf16[128,1600]{1,0:T(8,128)(2,1)S(1)}, u32[]{:S(2)}, u32[]{:S(2)}) collective-permute-start(bf16[128,1600]{1,0:T(8,128)(2,1)S(1)} %bitcast.11), channel_id=1, source_target_pairs={{0,16},{16,0},{1,17},{17,1},{2,18},{18,2},{3,19},{19,3},{4,20},{20... | collective-permute-start | bytes 1228808 | tf_op jit(solution)/shard_map/ppermute | solution.py:387
  28.6 10.0 %copy-start.5 = (bf16[4,1600,128]{2,1,0:T(8,128)(2,1)S(1)}, bf16[4,1600,128]{2,1,0:T(8,128)(2,1)}, u32[]{:S(2)}) copy-start(bf16[4,1600,128]{2,1,0:T(8,128)(2,1)} %copy-done.3) | copy-start | bytes 4915204
  29.4 9.2 %collective-permute-start.2 = (s32[584,128]{1,0:T(8,128)S(1)}, s32[584,128]{1,0:T(8,128)S(1)}, u32[]{:S(2)}, u32[]{:S(2)}) collective-permute-start(s32[584,128]{1,0:T(8,128)S(1)} %merge.4), channel_id=1, source_target_pairs={{0,2},{1,3},{2,0},{3,1},{4,6},{5,7},{6,4},{7,5},{8,10},{9,11},{10,... | collective-permute-start | bytes 897032 | tf_op jit(solution)/shard_map/ppermute | solution.py:23
  39.3 2.7 %collective-permute-start.3 = (f32[8,256,128]{2,1,0:T(8,128)S(1)}, f32[8,256,128]{2,1,0:T(8,128)S(1)}, u32[]{:S(2)}, u32[]{:S(2)}) collective-permute-start(f32[8,256,128]{2,1,0:T(8,128)S(1)} %project.7), channel_id=1, source_target_pairs={{0,1},{1,0},{2,3},{3,2},{4,5},{5,4},{6,7},{7,6},{8,9},{9,8},{10,11... | collective-permute-start | bytes 3145736 | tf_op jit(solution)/shard_map/ppermute | solution.py:23
  42.4 9.2 %collective-permute-start.7 = (s32[584,128]{1,0:T(8,128)S(1)}, s32[584,128]{1,0:T(8,128)S(1)}, u32[]{:S(2)}, u32[]{:S(2)}) collective-permute-start(s32[584,128]{1,0:T(8,128)S(1)} %merge.5), channel_id=1, source_target_pairs={{0,2},{1,3},{2,0},{3,1},{4,6},{5,7},{6,4},{7,5},{8,10},{9,11},{10,... | collective-permute-start | bytes 897032 | tf_op jit(solution)/shard_map/ppermute | solution.py:23
  43.9 17.0 %copy-start.8 = (s32[128]{0:T(128)S(1)}, s32[128]{0:T(128)}, u32[]{:S(2)}) copy-start(s32[128]{0:T(128)} %param.12) | copy-start | bytes 1540
  43.9 10.5 %collective-permute-start.4 = (s32[152,128]{1,0:T(8,128)S(1)}, s32[152,128]{1,0:T(8,128)S(1)}, u32[]{:S(2)}, u32[]{:S(2)}) collective-permute-start(s32[152,128]{1,0:T(8,128)S(1)} %get-tuple-element.40), channel_id=1, source_target_pairs={{0,8},{1,9},{2,10},{3,11},{4,12},{5,13},{6,14},{7,15},{8,0},{9,1},... | collective-permute-start | bytes 233480 | tf_op jit(solution)/shard_map/ppermute | solution.py:23
  45.2 11.4 %collective-permute-start.5 = (s32[152,128]{1,0:T(8,128)S(1)}, s32[152,128]{1,0:T(8,128)S(1)}, u32[]{:S(2)}, u32[]{:S(2)}) collective-permute-start(s32[152,128]{1,0:T(8,128)S(1)} %get-tuple-element.41), channel_id=1, source_target_pairs={{0,4},{1,5},{2,6},{3,7},{4,0},{5,1},{6,2},{7,3},{8,12},{9,13},{10,... | collective-permute-start | bytes 233480 | tf_op jit(solution)/shard_map/ppermute | solution.py:23
  46.7 10.0 %collective-permute-start.6 = (s32[152,128]{1,0:T(8,128)S(1)}, s32[152,128]{1,0:T(8,128)S(1)}, u32[]{:S(2)}, u32[]{:S(2)}) collective-permute-start(s32[152,128]{1,0:T(8,128)S(1)} %get-tuple-element.42), channel_id=1, source_target_pairs={{0,12},{1,13},{2,14},{3,15},{4,8},{5,9},{6,10},{7,11},{8,4},{9,5},... | collective-permute-start | bytes 233480 | tf_op jit(solution)/shard_map/ppermute | solution.py:23
  52.2 7.7 %collective-permute-start.8 = (s32[152,128]{1,0:T(8,128)S(1)}, s32[152,128]{1,0:T(8,128)S(1)}, u32[]{:S(2)}, u32[]{:S(2)}) collective-permute-start(s32[152,128]{1,0:T(8,128)S(1)} %get-tuple-element.44), channel_id=1, source_target_pairs={{0,8},{1,9},{2,10},{3,11},{4,12},{5,13},{6,14},{7,15},{8,0},{9,1},... | collective-permute-start | bytes 233480 | tf_op jit(solution)/shard_map/ppermute | solution.py:23
  54.1 5.7 %collective-permute-start.9 = (s32[152,128]{1,0:T(8,128)S(1)}, s32[152,128]{1,0:T(8,128)S(1)}, u32[]{:S(2)}, u32[]{:S(2)}) collective-permute-start(s32[152,128]{1,0:T(8,128)S(1)} %get-tuple-element.45), channel_id=1, source_target_pairs={{0,4},{1,5},{2,6},{3,7},{4,0},{5,1},{6,2},{7,3},{8,12},{9,13},{10,... | collective-permute-start | bytes 233480 | tf_op jit(solution)/shard_map/ppermute | solution.py:23
  54.4 6.5 %collective-permute-start.10 = (s32[152,128]{1,0:T(8,128)S(1)}, s32[152,128]{1,0:T(8,128)S(1)}, u32[]{:S(2)}, u32[]{:S(2)}) collective-permute-start(s32[152,128]{1,0:T(8,128)S(1)} %get-tuple-element.46), channel_id=1, source_target_pairs={{0,12},{1,13},{2,14},{3,15},{4,8},{5,9},{6,10},{7,11},{8,4},{9,5},... | collective-permute-start | bytes 233480 | tf_op jit(solution)/shard_map/ppermute | solution.py:23
  62.1 3.1 %collective-permute-start.13 = (f32[16,128]{1,0:T(8,128)S(1)}, f32[16,128]{1,0:T(8,128)S(1)}, u32[]{:S(2)}, u32[]{:S(2)}) collective-permute-start(f32[16,128]{1,0:T(8,128)S(1)} %get-tuple-element.49.refs_0_.refs_5_), channel_id=1, source_target_pairs={{0,3},{1,2},{2,1},{3,0},{4,7},{5,6},{6,5},{7,4},{8,11},{9,10},{10,... | collective-permute-start | bytes 24584 | tf_op jit(solution)/shard_map/ppermute | solution.py:23
  62.1 3.7 %collective-permute-start.12 = (f32[16,128]{1,0:T(8,128)S(1)}, f32[16,128]{1,0:T(8,128)S(1)}, u32[]{:S(2)}, u32[]{:S(2)}) collective-permute-start(f32[16,128]{1,0:T(8,128)S(1)} %get-tuple-element.49.refs_0_.refs_5_), channel_id=1, source_target_pairs={{0,2},{1,3},{2,0},{3,1},{4,6},{5,7},{6,4},{7,5},{8,10},{9,11},{10,... | collective-permute-start | bytes 24584 | tf_op jit(solution)/shard_map/ppermute | solution.py:23
  63.4 2.4 %collective-permute-start.11 = (f32[16,128]{1,0:T(8,128)S(1)}, f32[16,128]{1,0:T(8,128)S(1)}, u32[]{:S(2)}, u32[]{:S(2)}) collective-permute-start(f32[16,128]{1,0:T(8,128)S(1)} %get-tuple-element.49.refs_0_.refs_5_), channel_id=1, source_target_pairs={{0,1},{1,0},{2,3},{3,2},{4,5},{5,4},{6,7},{7,6},{8,9},{9,8},{10,11... | collective-permute-start | bytes 24584 | tf_op jit(solution)/shard_map/ppermute | solution.py:23
  65.9 5.5 %collective-permute-start.16 = (f32[16,128]{1,0:T(8,128)S(1)}, f32[16,128]{1,0:T(8,128)S(1)}, u32[]{:S(2)}, u32[]{:S(2)}) collective-permute-start(f32[16,128]{1,0:T(8,128)S(1)} %get-tuple-element.50.refs_0_), channel_id=1, source_target_pairs={{0,12},{1,13},{2,14},{3,15},{4,8},{5,9},{6,10},{7,11},{8,4},{9,5},... | collective-permute-start | bytes 24584 | tf_op jit(solution)/shard_map/ppermute | solution.py:23
  68.0 4.5 %collective-permute-start.15 = (f32[16,128]{1,0:T(8,128)S(1)}, f32[16,128]{1,0:T(8,128)S(1)}, u32[]{:S(2)}, u32[]{:S(2)}) collective-permute-start(f32[16,128]{1,0:T(8,128)S(1)} %get-tuple-element.50.refs_0_), channel_id=1, source_target_pairs={{0,8},{1,9},{2,10},{3,11},{4,12},{5,13},{6,14},{7,15},{8,0},{9,1},... | collective-permute-start | bytes 24584 | tf_op jit(solution)/shard_map/ppermute | solution.py:23
  68.8 3.8 %collective-permute-start.14 = (f32[16,128]{1,0:T(8,128)S(1)}, f32[16,128]{1,0:T(8,128)S(1)}, u32[]{:S(2)}, u32[]{:S(2)}) collective-permute-start(f32[16,128]{1,0:T(8,128)S(1)} %get-tuple-element.50.refs_0_), channel_id=1, source_target_pairs={{0,4},{1,5},{2,6},{3,7},{4,0},{5,1},{6,2},{7,3},{8,12},{9,13},{10,... | collective-permute-start | bytes 24584 | tf_op jit(solution)/shard_map/ppermute | solution.py:23

commit v5 on v4

--- a/solution.py
+++ b/solution.py
@@ -9,7 +9,7 @@
 
 RANK = 32
 LANES = 128
-PIECES = 4
+SENT, KEPT = (6, 2), (8,)
 CHUNKS = ((1,), (1,))
 F32 = jnp.float32
 BITS = 18
@@ -50,11 +50,10 @@
 def arrange_kernel(me, acts, grads, *rest):
     outs, sems = rest[:-1], rest[-1]
     depth = grads.shape[0]
-    per = outs[0].shape[0]
-    half = per * len(outs) // 2
-
-    def copies(piece, i):
-        block = piece * per + i
+    half = sum(out.shape[0] for out in outs) // 2
+
+    def copies(out, first, i):
+        block = first + i
         other_core = 1 - block // half
         near = (block % half) // (half // 2)
         offset = place(block % (half // 2), half // 2) + 2 * (1 - near) + other_core
@@ -62,35 +61,41 @@
         return [
             pltpu.make_async_copy(
                 ref.at[:, pl.ds(start, LANES)],
-                outs[piece].at[i, pl.ds(row, ref.shape[0])],
+                out.at[i, pl.ds(row, ref.shape[0])],
                 sems.at[k, block],
             )
             for k, (ref, row) in enumerate(((grads, 0), (acts, depth)))
         ]
 
-    def begin(piece, i, _):
-        for copy in copies(piece, i):
+    def begin(out, first, i, _):
+        for copy in copies(out, first, i):
             copy.start()
         return 0
 
-    def end(piece, i, _):
-        for copy in copies(piece, i):
+    def end(out, first, i, _):
+        for copy in copies(out, first, i):
             copy.wait()
         return 0
 
     for step in (begin, end):
-        for piece in range(len(outs)):
-            lax.fori_loop(0, per, functools.partial(step, piece), 0)
+        first = 0
+        for out in outs:
+            lax.fori_loop(0, out.shape[0], functools.partial(step, out, first), 0)
+            first += out.shape[0]
 
 
 def arrange(me, acts, grads):
     blocks = acts.shape[1] // LANES
-    shape = (blocks // PIECES, grads.shape[0] + acts.shape[0], LANES)
+    unit = blocks // 2 // sum(SENT)
+    depth = grads.shape[0] + acts.shape[0]
+    shapes = [((n * unit, depth, LANES), pltpu.VMEM) for n in SENT] + [
+        ((n * unit, depth, LANES), pltpu.HBM) for n in KEPT
+    ]
     return pl.pallas_call(
         arrange_kernel,
         in_specs=[pl.BlockSpec(memory_space=pltpu.SMEM)]
         + [pl.BlockSpec(memory_space=pltpu.HBM)] * 2,
-        out_shape=[pltpu.VMEM(shape, acts.dtype)] * PIECES,
+        out_shape=[space(shape, acts.dtype) for shape, space in shapes],
         scratch_shapes=[pltpu.SemaphoreType.DMA((2, blocks))],
         compiler_params=pltpu.CompilerParams(vmem_limit_bytes=50 << 20),
         cost_estimate=pl.CostEstimate(
@@ -103,7 +108,6 @@
 def project_kernel(depths, count, factors, *rest):
     columns, outs = rest[:count], rest[count:]
     blocks = outs[0].shape[0]
-    per = columns[0].shape[0]
     gap, right_depth, left_depth = depths
 
     def pair(ref, base, i, _):
@@ -126,13 +130,15 @@
             first += size
         return 0
 
-    for k, ref in enumerate(columns):
-        step = functools.partial(pair, ref, k * per)
-        lax.fori_loop(0, per // 2, step, 0, unroll=blocks <= 8)
+    first = 0
+    for ref in columns:
+        step = functools.partial(pair, ref, first)
+        lax.fori_loop(0, ref.shape[0] // 2, step, 0, unroll=blocks <= 8)
+        first += ref.shape[0]
 
 
 def project(factors, depths, columns, waves):
-    blocks = columns[0].shape[0] * len(columns)
+    blocks = sum(c.shape[0] for c in columns)
     shapes = [jax.ShapeDtypeStruct((blocks, 2 * w, LANES), F32) for w in waves]
     size = sum(c.size for c in columns)
     return pl.pallas_call(
@@ -390,9 +396,9 @@
         if flows:
             factors, flows[-1][2] = lax.optimization_barrier((factors, flows[-1][2]))
         waves = [factors.shape[0] // w for w in waves]
-        sent = project(factors, bounds, columns[: PIECES // 2], waves)
+        sent = project(factors, bounds, columns[: len(SENT)], waves)
         from_core = [swap(part, "loop", 1) for part in sent]
-        kept = project(factors, bounds, columns[PIECES // 2 :], waves)
+        kept = project(factors, bounds, columns[len(SENT) :], waves)
         to_y = [merge([k, f], [0, 0], count, 1, stay=False)[0] for k, f in zip(kept, from_core)]
         from_y = [swap(part, "loop", 2) for part in to_y]
         flows.extend([list(flow) for flow in zip(kept, from_core, from_y)])

time: 73.6 us -> 71.9 us (0.977)
  local copies, waits for them, and re-layouts: 8.78 us -> 4.51 us
  Pallas kernels: 10.1 us -> 11.7 us
    unnamed x22 -> x14, local copies, waits for them, and re-layouts: 6.47 us -> 2.21 us
    pallas_call x1, Pallas kernels: 3.44 us -> 5.11 us  [arrange(): pl.pallas_call(arrange_kernel, in_specs=[pl.BlockSpec(memory_space=pltpu....]
  transfers between devices with their start and end apart: 18 -> 18, of which waited for: 11 -> 11; matrix products, arithmetic and copies ran while one was open for 2% -> 3% of each run, Pallas kernels for 9% -> 11%
where the time goes in v5:
time: 71.9 us; the launch traced here: 71.7 us
  waiting for transfers between devices  27.2 us (38%)
  starting transfers between devices  26 us (36%)
  Pallas kernels  11.7 us (16%)
  local copies, waits for them, and re-layouts  4.51 us (6%)
  other arithmetic  1.46 us (2%)
  between operations  0.81 us (1%)
    ppermute x16, starting transfers between devices, swap(): return lax.ppermute(value, axis, [(i, i ^ offset) for i in range(size)])  17.1 us
    ppermute x16, waiting for transfers between devices, swap(): return lax.ppermute(value, axis, [(i, i ^ offset) for i in range(size)])  13.8 us
    ppermute x1, waiting for transfers between devices, local(): other = lax.ppermute(own, 'groups', [(i, i ^ 1) for i in range(groups)])  8.5 us
    all_to_all x1, starting transfers between devices, local(): lax.all_to_all(outgoing, 'loop', split_axis=0, concat_axis=0, tiled=True)  7.39 us
    pallas_call x1, Pallas kernels, arrange(): pl.pallas_call(arrange_kernel, in_specs=[pl.BlockSpec(memory_space=pltpu....  5.11 us
    all_to_all x1, waiting for transfers between devices, local(): lax.all_to_all(outgoing, 'loop', split_axis=0, concat_axis=0, tiled=True)  4.88 us
    pallas_call x4, Pallas kernels, project(): pl.pallas_call(functools.partial(project_kernel, depths, len(columns)), o...  2.58 us
    unnamed x14, local copies, waits for them, and re-layouts  2.21 us
  transfers between devices with their start and end apart: 18, of which 11 were waited for; matrix products, arithmetic and copies ran while one was open for 3% of the time, Pallas kernels for 11%

profile of v5, /device:TPU:0, one launch (start us, length us, event | category | flops | bytes accessed | tf_op | source)
XLA Modules:
  0.0 71.7 jit_solution(15567187895583369120)
XLA Ops:
  0.6 0.0 copy-start
  0.6 0.0 copy-start.6
  0.7 1.0 %constant_dynamic-slice_fusion = bf16[8,5120]{1,0:T(8,128)(2,1)S(1)} fusion(bf16[16,5120]{1,0:T(8,128)(2,1)} %param.9, s32[]{:T(128)S(6)} %select_n.4), kind=kLoop, calls=%fused_computation.3 | loop fusion | bytes 163844 | tf_op jit(solution)/shard_map/dynamic_slice | solution.py:376
  1.6 0.1 reshape.17
  1.8 0.0 copy-done
  1.9 0.8 %pad_maximum_fusion = bf16[16,8,1600]{2,1,0:T(8,128)(2,1)} fusion(bf16[16,8,320]{2,1,0:T(8,128)(2,1)S(1)} %copy.9, bf16[16,8,1280]{2,1,0:T(8,128)(2,1)S(1)} %bitcast.15), kind=kLoop, calls=%fused_computation.1 | loop fusion | flops 819200 | bytes 819200 | tf_op jit(solution)/shard_map/concatenate | solution.py:381
  2.7 7.4 %all-to-all-start = ((bf16[16,8,1600]{2,1,0:T(8,128)(2,1)}), bf16[16,8,1600]{2,1,0:T(8,128)(2,1)S(1)}, u32[]{:S(2)}, u32[]{:S(2)}) async-start(bf16[16,8,1600]{2,1,0:T(8,128)(2,1)} %pad_maximum_fusion), calls=%async_computation | async-start | bytes 851968 | tf_op jit(solution)/shard_map/all_to_all | solution.py:384
  10.0 0.7 pad_clamp_fusion
  10.7 1.1 %gather_fusion = f32[128]{0:T(128)S(1)} fusion(f32[50688]{0:T(1024)S(1)} %copy-done.6, s32[1024]{0:T(1024)S(1)} %pad_clamp_fusion), kind=kCustom, calls=%fused_computation | custom fusion | bytes 1536 | tf_op jit(solution)/shard_map/jit(_take)/gather | solution.py:386
  11.9 5.1 %arrange.1 = (bf16[6,1600,128]{2,1,0:T(8,128)(2,1)S(1)}, bf16[2,1600,128]{2,1,0:T(8,128)(2,1)S(1)}, bf16[8,1600,128]{2,1,0:T(8,128)(2,1)}) custom-call(s32[1]{0:T(128)} %bitcast.3.me, bf16[320,2048]{1,0:T(8,128)(2,1)} %acts.1, bf16[1280,2048]{1,0:T(8,128)(2,1)} %grads.1), custom_call_target="tpu_custom_call" | custom-call | bytes 13107200 | tf_op jit(solution)/shard_map/arrange/pallas_call | solution.py:94
  17.0 0.0 copy-start.2
  17.0 0.9 %copy-done.2 = bf16[2,1600,128]{2,1,0:T(8,128)(2,1)} copy-done((bf16[2,1600,128]{2,1,0:T(8,128)(2,1)}, bf16[2,1600,128]{2,1,0:T(8,128)(2,1)S(1)}, u32[]{:S(2)}) %copy-start.2) | copy-done | bytes 819224
  17.9 4.9 %all-to-all-done = bf16[16,8,1600]{2,1,0:T(8,128)(2,1)S(1)} async-done(((bf16[16,8,1600]{2,1,0:T(8,128)(2,1)}), bf16[16,8,1600]{2,1,0:T(8,128)(2,1)S(1)}, u32[]{:S(2)}, u32[]{:S(2)}) %all-to-all-start) | async-done | bytes 409632 | tf_op jit(solution)/shard_map/all_to_all | solution.py:384
  22.8 1.3 %copy-done.3 = bf16[2,1600,128]{2,1,0:T(8,128)(2,1)S(1)} copy-done((bf16[2,1600,128]{2,1,0:T(8,128)(2,1)S(1)}, bf16[2,1600,128]{2,1,0:T(8,128)(2,1)}, u32[]{:S(2)}) %copy-start.3) | copy-done | bytes 819224
  24.1 0.6 project.5
  24.7 0.0 copy-start.4
  24.7 0.2 collective-permute-start
  24.9 1.5 %collective-permute-start.1 = (bf16[128,1600]{1,0:T(8,128)(2,1)S(1)}, bf16[128,1600]{1,0:T(8,128)(2,1)S(1)}, u32[]{:S(2)}, u32[]{:S(2)}) collective-permute-start(bf16[128,1600]{1,0:T(8,128)(2,1)S(1)} %bitcast.11), channel_id=1, source_target_pairs={{0,16},{16,0},{1,17},{17,1},{2,18},{18,2},{3,19},{19,3},{4,20},{20... | collective-permute-start | bytes 1228808 | tf_op jit(solution)/shard_map/ppermute | solution.py:393
  26.4 0.0 copy-done.1
  26.4 0.6 project.4.refs_0_
  27.0 0.4 collective-permute-done.refs_1_
  27.5 0.4 merge.4
  27.8 0.7 %collective-permute-start.2 = (s32[584,128]{1,0:T(8,128)S(1)}, s32[584,128]{1,0:T(8,128)S(1)}, u32[]{:S(2)}, u32[]{:S(2)}) collective-permute-start(s32[584,128]{1,0:T(8,128)S(1)} %merge.4), channel_id=1, source_target_pairs={{0,2},{1,3},{2,0},{3,1},{4,6},{5,7},{6,4},{7,5},{8,10},{9,11},{10,... | collective-permute-start | bytes 897032 | tf_op jit(solution)/shard_map/ppermute | solution.py:23
  28.6 8.5 %collective-permute-done.1.factors = bf16[128,1600]{1,0:T(8,128)(2,1)S(1)} collective-permute-done((bf16[128,1600]{1,0:T(8,128)(2,1)S(1)}, bf16[128,1600]{1,0:T(8,128)(2,1)S(1)}, u32[]{:S(2)}, u32[]{:S(2)}) %collective-permute-start.1) | collective-permute-done | bytes 409632 | tf_op jit(solution)/shard_map/ppermute | solution.py:393
  37.1 0.0 collective-permute-done.2.refs_2_
  37.1 0.6 project.7
  37.7 0.1 collective-permute-start.3
  37.8 0.7 project.6.refs_0_
  38.5 0.0 copy-start.5
  38.5 2.0 %collective-permute-done.3.refs_1_ = f32[8,256,128]{2,1,0:T(8,128)S(1)} collective-permute-done((f32[8,256,128]{2,1,0:T(8,128)S(1)}, f32[8,256,128]{2,1,0:T(8,128)S(1)}, u32[]{:S(2)}, u32[]{:S(2)}) %collective-permute-start.3) | collective-permute-done | bytes 1048608 | tf_op jit(solution)/shard_map/ppermute | solution.py:23
  40.4 0.4 merge.5
  40.8 0.9 %collective-permute-start.7 = (s32[584,128]{1,0:T(8,128)S(1)}, s32[584,128]{1,0:T(8,128)S(1)}, u32[]{:S(2)}, u32[]{:S(2)}) collective-permute-start(s32[584,128]{1,0:T(8,128)S(1)} %merge.5), channel_id=1, source_target_pairs={{0,2},{1,3},{2,0},{3,1},{4,6},{5,7},{6,4},{7,5},{8,10},{9,11},{10,... | collective-permute-start | bytes 897032 | tf_op jit(solution)/shard_map/ppermute | solution.py:23
  41.7 0.5 merge.6
  42.3 1.3 %collective-permute-start.4 = (s32[152,128]{1,0:T(8,128)S(1)}, s32[152,128]{1,0:T(8,128)S(1)}, u32[]{:S(2)}, u32[]{:S(2)}) collective-permute-start(s32[152,128]{1,0:T(8,128)S(1)} %get-tuple-element.36), channel_id=1, source_target_pairs={{0,8},{1,9},{2,10},{3,11},{4,12},{5,13},{6,14},{7,15},{8,0},{9,1},... | collective-permute-start | bytes 233480 | tf_op jit(solution)/shard_map/ppermute | solution.py:23
  43.6 1.4 %collective-permute-start.5 = (s32[152,128]{1,0:T(8,128)S(1)}, s32[152,128]{1,0:T(8,128)S(1)}, u32[]{:S(2)}, u32[]{:S(2)}) collective-permute-start(s32[152,128]{1,0:T(8,128)S(1)} %get-tuple-element.37), channel_id=1, source_target_pairs={{0,4},{1,5},{2,6},{3,7},{4,0},{5,1},{6,2},{7,3},{8,12},{9,13},{10,... | collective-permute-start | bytes 233480 | tf_op jit(solution)/shard_map/ppermute | solution.py:23
  45.0 1.7 %collective-permute-start.6 = (s32[152,128]{1,0:T(8,128)S(1)}, s32[152,128]{1,0:T(8,128)S(1)}, u32[]{:S(2)}, u32[]{:S(2)}) collective-permute-start(s32[152,128]{1,0:T(8,128)S(1)} %get-tuple-element.38), channel_id=1, source_target_pairs={{0,12},{1,13},{2,14},{3,15},{4,8},{5,9},{6,10},{7,11},{8,4},{9,5},... | collective-permute-start | bytes 233480 | tf_op jit(solution)/shard_map/ppermute | solution.py:23
  46.7 3.3 %collective-permute-done.7.refs_2_ = s32[584,128]{1,0:T(8,128)S(1)} collective-permute-done((s32[584,128]{1,0:T(8,128)S(1)}, s32[584,128]{1,0:T(8,128)S(1)}, u32[]{:S(2)}, u32[]{:S(2)}) %collective-permute-start.7) | collective-permute-done | bytes 299040 | tf_op jit(solution)/shard_map/ppermute | solution.py:23
  50.0 0.5 merge.7
  50.6 1.9 %collective-permute-start.8 = (s32[152,128]{1,0:T(8,128)S(1)}, s32[152,128]{1,0:T(8,128)S(1)}, u32[]{:S(2)}, u32[]{:S(2)}) collective-permute-start(s32[152,128]{1,0:T(8,128)S(1)} %get-tuple-element.40), channel_id=1, source_target_pairs={{0,8},{1,9},{2,10},{3,11},{4,12},{5,13},{6,14},{7,15},{8,0},{9,1},... | collective-permute-start | bytes 233480 | tf_op jit(solution)/shard_map/ppermute | solution.py:23
  52.5 0.3 collective-permute-start.9
  52.8 0.0 collective-permute-done.4.refs_1_
  52.8 2.2 %collective-permute-start.10 = (s32[152,128]{1,0:T(8,128)S(1)}, s32[152,128]{1,0:T(8,128)S(1)}, u32[]{:S(2)}, u32[]{:S(2)}) collective-permute-start(s32[152,128]{1,0:T(8,128)S(1)} %get-tuple-element.42), channel_id=1, source_target_pairs={{0,12},{1,13},{2,14},{3,15},{4,8},{5,9},{6,10},{7,11},{8,4},{9,5},... | collective-permute-start | bytes 233480 | tf_op jit(solution)/shard_map/ppermute | solution.py:23
  55.0 0.0 collective-permute-done.5.refs_2_
  55.0 0.0 collective-permute-done.6.refs_3_
  55.0 0.2 partial_scores.1.refs_0_
  55.2 3.0 %collective-permute-done.8.refs_2_ = s32[152,128]{1,0:T(8,128)S(1)} collective-permute-done((s32[152,128]{1,0:T(8,128)S(1)}, s32[152,128]{1,0:T(8,128)S(1)}, u32[]{:S(2)}, u32[]{:S(2)}) %collective-permute-start.8) | collective-permute-done | bytes 77856 | tf_op jit(solution)/shard_map/ppermute | solution.py:23
  58.2 0.0 collective-permute-done.9.refs_3_
  58.2 1.0 %collective-permute-done.10.refs_4_ = s32[152,128]{1,0:T(8,128)S(1)} collective-permute-done((s32[152,128]{1,0:T(8,128)S(1)}, s32[152,128]{1,0:T(8,128)S(1)}, u32[]{:S(2)}, u32[]{:S(2)}) %collective-permute-start.10) | collective-permute-done | bytes 77856 | tf_op jit(solution)/shard_map/ppermute | solution.py:23
  59.3 0.0 copy-done.5
  59.3 1.2 %tails.1 = (f32[8,128]{1,0:T(8,128)}, f32[16,128]{1,0:T(8,128)S(1)}) custom-call(f32[8,128]{1,0:T(8,128)S(1)} %partial_scores.1.refs_0_, f32[1,256,128]{2,1,0:T(8,128)S(1)} %get-tuple-element.39.refs_1_, s32[152,128]{1,0:T(8,128)S(1)} %collective-permute-done.8.refs_2_, s32[152,128]{1,0:T(8,128)S(1)} %collective-permute-done.9.refs_3_, ...), custom_call_target="tpu_custom_call" | custom-call | tf_op jit(solution)/shard_map/tails/pallas_call | solution.py:428
  60.5 0.0 collective-permute-start.13
  60.5 1.3 %collective-permute-start.12 = (f32[16,128]{1,0:T(8,128)S(1)}, f32[16,128]{1,0:T(8,128)S(1)}, u32[]{:S(2)}, u32[]{:S(2)}) collective-permute-start(f32[16,128]{1,0:T(8,128)S(1)} %get-tuple-element.45.refs_0_.refs_5_), channel_id=1, source_target_pairs={{0,2},{1,3},{2,0},{3,1},{4,6},{5,7},{6,4},{7,5},{8,10},{9,11},{10,... | collective-permute-start | bytes 24584 | tf_op jit(solution)/shard_map/ppermute | solution.py:23
  61.8 0.6 collective-permute-start.11
  62.4 1.2 %collective-permute-done.13.refs_3_ = f32[16,128]{1,0:T(8,128)S(1)} collective-permute-done((f32[16,128]{1,0:T(8,128)S(1)}, f32[16,128]{1,0:T(8,128)S(1)}, u32[]{:S(2)}, u32[]{:S(2)}) %collective-permute-start.13) | collective-permute-done | bytes 8224 | tf_op jit(solution)/shard_map/ppermute | solution.py:23
  63.6 0.6 collective-permute-done.12.refs_2_
  64.2 0.0 collective-permute-done.11.refs_1_
  64.2 0.1 fold_group.1
  64.3 2.1 %collective-permute-start.16 = (f32[16,128]{1,0:T(8,128)S(1)}, f32[16,128]{1,0:T(8,128)S(1)}, u32[]{:S(2)}, u32[]{:S(2)}) collective-permute-start(f32[16,128]{1,0:T(8,128)S(1)} %get-tuple-element.46.refs_0_), channel_id=1, source_target_pairs={{0,12},{1,13},{2,14},{3,15},{4,8},{5,9},{6,10},{7,11},{8,4},{9,5},... | collective-permute-start | bytes 24584 | tf_op jit(solution)/shard_map/ppermute | solution.py:23
  66.4 0.8 %collective-permute-start.15 = (f32[16,128]{1,0:T(8,128)S(1)}, f32[16,128]{1,0:T(8,128)S(1)}, u32[]{:S(2)}, u32[]{:S(2)}) collective-permute-start(f32[16,128]{1,0:T(8,128)S(1)} %get-tuple-element.46.refs_0_), channel_id=1, source_target_pairs={{0,8},{1,9},{2,10},{3,11},{4,12},{5,13},{6,14},{7,15},{8,0},{9,1},... | collective-permute-start | bytes 24584 | tf_op jit(solution)/shard_map/ppermute | solution.py:23
  67.2 1.5 %collective-permute-start.14 = (f32[16,128]{1,0:T(8,128)S(1)}, f32[16,128]{1,0:T(8,128)S(1)}, u32[]{:S(2)}, u32[]{:S(2)}) collective-permute-start(f32[16,128]{1,0:T(8,128)S(1)} %get-tuple-element.46.refs_0_), channel_id=1, source_target_pairs={{0,4},{1,5},{2,6},{3,7},{4,0},{5,1},{6,2},{7,3},{8,12},{9,13},{10,... | collective-permute-start | bytes 24584 | tf_op jit(solution)/shard_map/ppermute | solution.py:23
  68.7 1.1 %collective-permute-done.16.refs_3_ = f32[16,128]{1,0:T(8,128)S(1)} collective-permute-done((f32[16,128]{1,0:T(8,128)S(1)}, f32[16,128]{1,0:T(8,128)S(1)}, u32[]{:S(2)}, u32[]{:S(2)}) %collective-permute-start.16) | collective-permute-done | bytes 8224 | tf_op jit(solution)/shard_map/ppermute | solution.py:23
  69.7 1.2 %collective-permute-done.15.refs_2_ = f32[16,128]{1,0:T(8,128)S(1)} collective-permute-done((f32[16,128]{1,0:T(8,128)S(1)}, f32[16,128]{1,0:T(8,128)S(1)}, u32[]{:S(2)}, u32[]{:S(2)}) %collective-permute-start.15) | collective-permute-done | bytes 8224 | tf_op jit(solution)/shard_map/ppermute | solution.py:23
  71.0 0.0 collective-permute-done.14.refs_1_
  71.0 0.7 finish.1
  (7 shorter events, 0.1 us)
Async XLA Ops:
  0.6 1.2 %copy-start = (bf16[16,20480]{1,0:T(8,128)(2,1)S(1)}, bf16[16,20480]{1,0:T(8,128)(2,1)}, u32[]{:S(2)}) copy-start(bf16[16,20480]{1,0:T(8,128)(2,1)} %param.10) | copy-start | bytes 1966084
  0.6 10.1 %copy-start.6 = (f32[50688]{0:T(1024)S(1)}, f32[50688]{0:T(1024)}, u32[]{:S(2)}) copy-start(f32[50688]{0:T(1024)} %param.13) | copy-start | bytes 608260
  2.7 20.1 %all-to-all-start = ((bf16[16,8,1600]{2,1,0:T(8,128)(2,1)}), bf16[16,8,1600]{2,1,0:T(8,128)(2,1)S(1)}, u32[]{:S(2)}, u32[]{:S(2)}) async-start(bf16[16,8,1600]{2,1,0:T(8,128)(2,1)} %pad_maximum_fusion), calls=%async_computation | async-start | bytes 851968 | tf_op jit(solution)/shard_map/all_to_all | solution.py:384
  17.0 0.9 %copy-start.2 = (bf16[2,1600,128]{2,1,0:T(8,128)(2,1)}, bf16[2,1600,128]{2,1,0:T(8,128)(2,1)S(1)}, u32[]{:S(2)}) copy-start(bf16[2,1600,128]{2,1,0:T(8,128)(2,1)S(1)} %get-tuple-element.31.rest_1_) | copy-start | bytes 2457604
  22.8 3.6 %copy-start.1 = (bf16[8,1600,128]{2,1,0:T(8,128)(2,1)S(1)}, bf16[8,1600,128]{2,1,0:T(8,128)(2,1)}, u32[]{:S(2)}) copy-start(bf16[8,1600,128]{2,1,0:T(8,128)(2,1)} %get-tuple-element.29.rest_0_) | copy-start | bytes 9830404
  22.8 1.3 %copy-start.3 = (bf16[2,1600,128]{2,1,0:T(8,128)(2,1)S(1)}, bf16[2,1600,128]{2,1,0:T(8,128)(2,1)}, u32[]{:S(2)}) copy-start(bf16[2,1600,128]{2,1,0:T(8,128)(2,1)} %copy-done.2) | copy-start | bytes 2457604
  24.7 12.3 %copy-start.4 = (bf16[2,1600,128]{2,1,0:T(8,128)(2,1)S(1)}, bf16[2,1600,128]{2,1,0:T(8,128)(2,1)}, u32[]{:S(2)}) copy-start(bf16[2,1600,128]{2,1,0:T(8,128)(2,1)} %copy-done.2) | copy-start | bytes 2457604
  24.7 2.7 %collective-permute-start = (f32[8,256,128]{2,1,0:T(8,128)S(1)}, f32[8,256,128]{2,1,0:T(8,128)S(1)}, u32[]{:S(2)}, u32[]{:S(2)}) collective-permute-start(f32[8,256,128]{2,1,0:T(8,128)S(1)} %project.5), channel_id=1, source_target_pairs={{0,1},{1,0},{2,3},{3,2},{4,5},{5,4},{6,7},{7,6},{8,9},{9,8},{10,11... | collective-permute-start | bytes 3145736 | tf_op jit(solution)/shard_map/ppermute | solution.py:23
  24.9 12.2 %collective-permute-start.1 = (bf16[128,1600]{1,0:T(8,128)(2,1)S(1)}, bf16[128,1600]{1,0:T(8,128)(2,1)S(1)}, u32[]{:S(2)}, u32[]{:S(2)}) collective-permute-start(bf16[128,1600]{1,0:T(8,128)(2,1)S(1)} %bitcast.11), channel_id=1, source_target_pairs={{0,16},{16,0},{1,17},{17,1},{2,18},{18,2},{3,19},{19,3},{4,20},{20... | collective-permute-start | bytes 1228808 | tf_op jit(solution)/shard_map/ppermute | solution.py:393
  27.8 9.2 %collective-permute-start.2 = (s32[584,128]{1,0:T(8,128)S(1)}, s32[584,128]{1,0:T(8,128)S(1)}, u32[]{:S(2)}, u32[]{:S(2)}) collective-permute-start(s32[584,128]{1,0:T(8,128)S(1)} %merge.4), channel_id=1, source_target_pairs={{0,2},{1,3},{2,0},{3,1},{4,6},{5,7},{6,4},{7,5},{8,10},{9,11},{10,... | collective-permute-start | bytes 897032 | tf_op jit(solution)/shard_map/ppermute | solution.py:23
  37.7 2.7 %collective-permute-start.3 = (f32[8,256,128]{2,1,0:T(8,128)S(1)}, f32[8,256,128]{2,1,0:T(8,128)S(1)}, u32[]{:S(2)}, u32[]{:S(2)}) collective-permute-start(f32[8,256,128]{2,1,0:T(8,128)S(1)} %project.7), channel_id=1, source_target_pairs={{0,1},{1,0},{2,3},{3,2},{4,5},{5,4},{6,7},{7,6},{8,9},{9,8},{10,11... | collective-permute-start | bytes 3145736 | tf_op jit(solution)/shard_map/ppermute | solution.py:23
  38.5 20.8 %copy-start.5 = (s32[128]{0:T(128)S(1)}, s32[128]{0:T(128)}, u32[]{:S(2)}) copy-start(s32[128]{0:T(128)} %param.12) | copy-start | bytes 1540
  40.8 9.2 %collective-permute-start.7 = (s32[584,128]{1,0:T(8,128)S(1)}, s32[584,128]{1,0:T(8,128)S(1)}, u32[]{:S(2)}, u32[]{:S(2)}) collective-permute-start(s32[584,128]{1,0:T(8,128)S(1)} %merge.5), channel_id=1, source_target_pairs={{0,2},{1,3},{2,0},{3,1},{4,6},{5,7},{6,4},{7,5},{8,10},{9,11},{10,... | collective-permute-start | bytes 897032 | tf_op jit(solution)/shard_map/ppermute | solution.py:23
  42.3 10.5 %collective-permute-start.4 = (s32[152,128]{1,0:T(8,128)S(1)}, s32[152,128]{1,0:T(8,128)S(1)}, u32[]{:S(2)}, u32[]{:S(2)}) collective-permute-start(s32[152,128]{1,0:T(8,128)S(1)} %get-tuple-element.36), channel_id=1, source_target_pairs={{0,8},{1,9},{2,10},{3,11},{4,12},{5,13},{6,14},{7,15},{8,0},{9,1},... | collective-permute-start | bytes 233480 | tf_op jit(solution)/shard_map/ppermute | solution.py:23
  43.6 11.4 %collective-permute-start.5 = (s32[152,128]{1,0:T(8,128)S(1)}, s32[152,128]{1,0:T(8,128)S(1)}, u32[]{:S(2)}, u32[]{:S(2)}) collective-permute-start(s32[152,128]{1,0:T(8,128)S(1)} %get-tuple-element.37), channel_id=1, source_target_pairs={{0,4},{1,5},{2,6},{3,7},{4,0},{5,1},{6,2},{7,3},{8,12},{9,13},{10,... | collective-permute-start | bytes 233480 | tf_op jit(solution)/shard_map/ppermute | solution.py:23
  45.0 10.0 %collective-permute-start.6 = (s32[152,128]{1,0:T(8,128)S(1)}, s32[152,128]{1,0:T(8,128)S(1)}, u32[]{:S(2)}, u32[]{:S(2)}) collective-permute-start(s32[152,128]{1,0:T(8,128)S(1)} %get-tuple-element.38), channel_id=1, source_target_pairs={{0,12},{1,13},{2,14},{3,15},{4,8},{5,9},{6,10},{7,11},{8,4},{9,5},... | collective-permute-start | bytes 233480 | tf_op jit(solution)/shard_map/ppermute | solution.py:23
  50.6 7.7 %collective-permute-start.8 = (s32[152,128]{1,0:T(8,128)S(1)}, s32[152,128]{1,0:T(8,128)S(1)}, u32[]{:S(2)}, u32[]{:S(2)}) collective-permute-start(s32[152,128]{1,0:T(8,128)S(1)} %get-tuple-element.40), channel_id=1, source_target_pairs={{0,8},{1,9},{2,10},{3,11},{4,12},{5,13},{6,14},{7,15},{8,0},{9,1},... | collective-permute-start | bytes 233480 | tf_op jit(solution)/shard_map/ppermute | solution.py:23
  52.5 5.7 %collective-permute-start.9 = (s32[152,128]{1,0:T(8,128)S(1)}, s32[152,128]{1,0:T(8,128)S(1)}, u32[]{:S(2)}, u32[]{:S(2)}) collective-permute-start(s32[152,128]{1,0:T(8,128)S(1)} %get-tuple-element.41), channel_id=1, source_target_pairs={{0,4},{1,5},{2,6},{3,7},{4,0},{5,1},{6,2},{7,3},{8,12},{9,13},{10,... | collective-permute-start | bytes 233480 | tf_op jit(solution)/shard_map/ppermute | solution.py:23
  52.8 6.5 %collective-permute-start.10 = (s32[152,128]{1,0:T(8,128)S(1)}, s32[152,128]{1,0:T(8,128)S(1)}, u32[]{:S(2)}, u32[]{:S(2)}) collective-permute-start(s32[152,128]{1,0:T(8,128)S(1)} %get-tuple-element.42), channel_id=1, source_target_pairs={{0,12},{1,13},{2,14},{3,15},{4,8},{5,9},{6,10},{7,11},{8,4},{9,5},... | collective-permute-start | bytes 233480 | tf_op jit(solution)/shard_map/ppermute | solution.py:23
  60.5 3.1 %collective-permute-start.13 = (f32[16,128]{1,0:T(8,128)S(1)}, f32[16,128]{1,0:T(8,128)S(1)}, u32[]{:S(2)}, u32[]{:S(2)}) collective-permute-start(f32[16,128]{1,0:T(8,128)S(1)} %get-tuple-element.45.refs_0_.refs_5_), channel_id=1, source_target_pairs={{0,3},{1,2},{2,1},{3,0},{4,7},{5,6},{6,5},{7,4},{8,11},{9,10},{10,... | collective-permute-start | bytes 24584 | tf_op jit(solution)/shard_map/ppermute | solution.py:23
  60.5 3.7 %collective-permute-start.12 = (f32[16,128]{1,0:T(8,128)S(1)}, f32[16,128]{1,0:T(8,128)S(1)}, u32[]{:S(2)}, u32[]{:S(2)}) collective-permute-start(f32[16,128]{1,0:T(8,128)S(1)} %get-tuple-element.45.refs_0_.refs_5_), channel_id=1, source_target_pairs={{0,2},{1,3},{2,0},{3,1},{4,6},{5,7},{6,4},{7,5},{8,10},{9,11},{10,... | collective-permute-start | bytes 24584 | tf_op jit(solution)/shard_map/ppermute | solution.py:23
  61.8 2.4 %collective-permute-start.11 = (f32[16,128]{1,0:T(8,128)S(1)}, f32[16,128]{1,0:T(8,128)S(1)}, u32[]{:S(2)}, u32[]{:S(2)}) collective-permute-start(f32[16,128]{1,0:T(8,128)S(1)} %get-tuple-element.45.refs_0_.refs_5_), channel_id=1, source_target_pairs={{0,1},{1,0},{2,3},{3,2},{4,5},{5,4},{6,7},{7,6},{8,9},{9,8},{10,11... | collective-permute-start | bytes 24584 | tf_op jit(solution)/shard_map/ppermute | solution.py:23
  64.3 5.5 %collective-permute-start.16 = (f32[16,128]{1,0:T(8,128)S(1)}, f32[16,128]{1,0:T(8,128)S(1)}, u32[]{:S(2)}, u32[]{:S(2)}) collective-permute-start(f32[16,128]{1,0:T(8,128)S(1)} %get-tuple-element.46.refs_0_), channel_id=1, source_target_pairs={{0,12},{1,13},{2,14},{3,15},{4,8},{5,9},{6,10},{7,11},{8,4},{9,5},... | collective-permute-start | bytes 24584 | tf_op jit(solution)/shard_map/ppermute | solution.py:23
  66.4 4.5 %collective-permute-start.15 = (f32[16,128]{1,0:T(8,128)S(1)}, f32[16,128]{1,0:T(8,128)S(1)}, u32[]{:S(2)}, u32[]{:S(2)}) collective-permute-start(f32[16,128]{1,0:T(8,128)S(1)} %get-tuple-element.46.refs_0_), channel_id=1, source_target_pairs={{0,8},{1,9},{2,10},{3,11},{4,12},{5,13},{6,14},{7,15},{8,0},{9,1},... | collective-permute-start | bytes 24584 | tf_op jit(solution)/shard_map/ppermute | solution.py:23
  67.2 3.8 %collective-permute-start.14 = (f32[16,128]{1,0:T(8,128)S(1)}, f32[16,128]{1,0:T(8,128)S(1)}, u32[]{:S(2)}, u32[]{:S(2)}) collective-permute-start(f32[16,128]{1,0:T(8,128)S(1)} %get-tuple-element.46.refs_0_), channel_id=1, source_target_pairs={{0,4},{1,5},{2,6},{3,7},{4,0},{5,1},{6,2},{7,3},{8,12},{9,13},{10,... | collective-permute-start | bytes 24584 | tf_op jit(solution)/shard_map/ppermute | solution.py:23

commit v6 on v5

--- a/solution.py
+++ b/solution.py
@@ -9,7 +9,7 @@
 
 RANK = 32
 LANES = 128
-SENT, KEPT = (6, 2), (8,)
+SENT, KEPT = (4, 2, 2), (4, 4)
 CHUNKS = ((1,), (1,))
 F32 = jnp.float32
 BITS = 18
@@ -313,6 +313,7 @@
 
 def fold_members(queries, me, refs, shift):
     members = len(refs)
+    refs = [refs[0], *refs[:0:-1]]
     tails = [ref[:, LANES - 1 : LANES] for ref in refs]
     mine = lax.rem(lax.shift_right_logical(me, shift), members)
     before = jnp.zeros_like(tails[0])
@@ -392,32 +393,39 @@
     ranks = RANK // groups
     other = lax.ppermute(own, "groups", [(i, i ^ 1) for i in range(groups)])
     flows = []
+    kinds = [columns[: len(SENT)], columns[len(SENT) :]]
     for factors, waves in zip((own, other), CHUNKS):
-        if flows:
-            factors, flows[-1][2] = lax.optimization_barrier((factors, flows[-1][2]))
         waves = [factors.shape[0] // w for w in waves]
-        sent = project(factors, bounds, columns[: len(SENT)], waves)
-        from_core = [swap(part, "loop", 1) for part in sent]
-        kept = project(factors, bounds, columns[len(SENT) :], waves)
-        to_y = [merge([k, f], [0, 0], count, 1, stay=False)[0] for k, f in zip(kept, from_core)]
+        if not flows:
+            far = [swap(part, "loop", 1) for part in project(factors, bounds, kinds[0], waves)]
+            kept = project(factors, bounds, kinds[1], waves)
+            to_y = [merge([k, f], [0, 0], count, 1, stay=False)[0] for k, f in zip(kept, far)]
+            from_y = [swap(part, "loop", 2) for part in to_y]
+            flows.extend([k, f, y, count] for k, f, y in zip(kept, far, from_y))
+            continue
+        factors, flows[-1][2] = lax.optimization_barrier((factors, flows[-1][2]))
+        far = [swap(part, "loop", 1) for part in project(factors, bounds, kinds[0][:1], waves)]
+        kept = project(factors, bounds, kinds[1][:1], waves)
+        to_y = [merge([k, f], [0, 0], count, 1, stay=False)[0] for k, f in zip(kept, far)]
         from_y = [swap(part, "loop", 2) for part in to_y]
-        flows.extend([list(flow) for flow in zip(kept, from_core, from_y)])
-        if len(flows) > 1:
-            flows[0][2], to_y[-1] = lax.optimization_barrier((flows[0][2], to_y[-1]))
+        pass
+        near = [swap(part, "loop", 1) for part in project(factors, bounds, kinds[0][1:], waves)]
+        kept = project(factors, bounds, kinds[1][1:], waves)
+        flows.extend([k, f, y, 0] for k, f, y in zip(kept, near, from_y))
+        flows[0][2], to_y[-1] = lax.optimization_barrier((flows[0][2], to_y[-1]))
     ready = []
-    for h, values in enumerate(flows):
+    for h, (*values, start) in enumerate(flows):
         if len(ready) > 1:
             values[2], ready[-2] = lax.optimization_barrier((values[2], ready[-2]))
-        starts = [count, count, None]
+        starts = [start, start, None]
         blocks = count
         bit = 4
         while bit < size:
             width = 4 if 2 * bit < size else 2
             pieces = merge(values, starts, blocks, width)
             offsets = (0, 2 * bit, bit, 3 * bit) if width == 4 else (0, bit)
-            values = [pieces[0]] + [
-                swap(piece, "loop", offset) for piece, offset in zip(pieces[1:], offsets[1:])
-            ]
+            order = (3, 1, 2) if width == 4 else (1,)
+            values = [pieces[0]] + [swap(pieces[k], "loop", offsets[k]) for k in order]
             blocks //= width
             starts = [0] + [None] * (width - 1)
             bit *= width
@@ -437,11 +445,11 @@
     shift = 0
     rounds = [[0, 1, 2, 3]] + stages
     for offsets in rounds[:-1]:
-        messages = [message] + [swap(message, "loop", offset) for offset in offsets[1:]]
+        messages = [message] + [swap(message, "loop", offset) for offset in reversed(offsets[1:])]
         before, message = fold_group(me, messages, queries, shift)
         befores.insert(0, before)
         shift += len(offsets).bit_length() - 1
-    messages = [message] + [swap(message, "loop", offset) for offset in rounds[-1][1:]]
+    messages = [message] + [swap(message, "loop", offset) for offset in reversed(rounds[-1][1:])]
     influence = pl.pallas_call(
         functools.partial(finish_kernel, queries, shift, len(messages)),
         in_specs=[pl.BlockSpec(memory_space=pltpu.SMEM)]

time: 71.9 us -> 71.8 us (level)
  waiting for transfers between devices: 27.2 us -> 25.8 us
  local copies, waits for them, and re-layouts: 4.51 us -> 5.33 us
    ppermute x16 -> x17, waiting for transfers between devices: 13.8 us -> 11.8 us  [swap(): return lax.ppermute(value, axis, [(i, i ^ offset) for i in range(size)])]
    unnamed x14 -> x18, local copies, waits for them, and re-layouts: 2.21 us -> 3.1 us
    ppermute x16 -> x17, starting transfers between devices: 17.1 us -> 17.7 us  [swap(): return lax.ppermute(value, axis, [(i, i ^ offset) for i in range(size)])]
    pallas_call x4 -> x6, Pallas kernels: 2.58 us -> 2.89 us  [project(): pl.pallas_call(functools.partial(project_kernel, depths, len(columns)), o...]
  transfers between devices with their start and end apart: 18 -> 19, of which waited for: 11 -> 11; matrix products, arithmetic and copies ran while one was open for 3% -> 2% of each run, Pallas kernels for 11% -> 13%
where the time goes in v6:
time: 71.8 us; the launch traced here: 71.5 us
  starting transfers between devices  26.6 us (37%)
  waiting for transfers between devices  25.8 us (36%)
  Pallas kernels  12.1 us (17%)
  local copies, waits for them, and re-layouts  5.33 us (7%)
  between operations  0.85 us (1%)
  other arithmetic  0.81 us (1%)
    ppermute x17, starting transfers between devices, swap(): return lax.ppermute(value, axis, [(i, i ^ offset) for i in range(size)])  17.7 us
    ppermute x17, waiting for transfers between devices, swap(): return lax.ppermute(value, axis, [(i, i ^ offset) for i in range(size)])  11.8 us
    ppermute x1, waiting for transfers between devices, local(): other = lax.ppermute(own, 'groups', [(i, i ^ 1) for i in range(groups)])  8.49 us
    all_to_all x1, starting transfers between devices, local(): lax.all_to_all(outgoing, 'loop', split_axis=0, concat_axis=0, tiled=True)  7.39 us
    all_to_all x1, waiting for transfers between devices, local(): lax.all_to_all(outgoing, 'loop', split_axis=0, concat_axis=0, tiled=True)  5.52 us
    pallas_call x1, Pallas kernels, arrange(): pl.pallas_call(arrange_kernel, in_specs=[pl.BlockSpec(memory_space=pltpu....  5.12 us
    unnamed x18, local copies, waits for them, and re-layouts  3.1 us
    pallas_call x6, Pallas kernels, project(): pl.pallas_call(functools.partial(project_kernel, depths, len(columns)), o...  2.89 us
  transfers between devices with their start and end apart: 19, of which 11 were waited for; matrix products, arithmetic and copies ran while one was open for 2% of the time, Pallas kernels for 13%

profile of v6, /device:TPU:0, one launch (start us, length us, event | category | flops | bytes accessed | tf_op | source)
XLA Modules:
  0.0 71.5 jit_solution(15172451436148505731)
XLA Ops:
  0.6 0.0 copy-start
  0.7 1.1 %copy-done = bf16[16,20480]{1,0:T(8,128)(2,1)S(1)} copy-done((bf16[16,20480]{1,0:T(8,128)(2,1)S(1)}, bf16[16,20480]{1,0:T(8,128)(2,1)}, u32[]{:S(2)}) %copy-start) | copy-done | bytes 655384
  1.7 0.9 %constant_dynamic-slice_fusion = bf16[8,5120]{1,0:T(8,128)(2,1)S(1)} fusion(bf16[16,5120]{1,0:T(8,128)(2,1)} %param.9, s32[]{:T(128)S(6)} %select_n.4), kind=kLoop, calls=%fused_computation.3 | loop fusion | bytes 163844 | tf_op jit(solution)/shard_map/dynamic_slice | solution.py:377
  2.7 0.1 reshape.17
  2.8 0.8 %pad_maximum_fusion = bf16[16,8,1600]{2,1,0:T(8,128)(2,1)} fusion(bf16[16,8,320]{2,1,0:T(8,128)(2,1)S(1)} %copy.9, bf16[16,8,1280]{2,1,0:T(8,128)(2,1)S(1)} %bitcast.15), kind=kLoop, calls=%fused_computation.1 | loop fusion | flops 819200 | bytes 819200 | tf_op jit(solution)/shard_map/concatenate | solution.py:382
  3.6 7.4 %all-to-all-start = ((bf16[16,8,1600]{2,1,0:T(8,128)(2,1)}), bf16[16,8,1600]{2,1,0:T(8,128)(2,1)S(1)}, u32[]{:S(2)}, u32[]{:S(2)}) async-start(bf16[16,8,1600]{2,1,0:T(8,128)(2,1)} %pad_maximum_fusion), calls=%async_computation | async-start | bytes 851968 | tf_op jit(solution)/shard_map/all_to_all | solution.py:385
  11.0 0.0 copy-done.7
  11.1 1.1 %gather_fusion = f32[128]{0:T(128)S(1)} fusion(f32[50688]{0:T(1024)S(1)} %copy-done.7, s32[1024]{0:T(1024)S(1)} %pad_clamp_fusion), kind=kCustom, calls=%fused_computation | custom fusion | bytes 1536 | tf_op jit(solution)/shard_map/jit(_take)/gather | solution.py:387
  12.2 5.1 %arrange.1 = (bf16[4,1600,128]{2,1,0:T(8,128)(2,1)S(1)}, bf16[2,1600,128]{2,1,0:T(8,128)(2,1)S(1)}, bf16[2,1600,128]{2,1,0:T(8,128)(2,1)S(1)}, bf16[4,1600,128]{2,1,0:T(8,128)(2,1)}, bf16[4,1600,128]{2,1,0:T(8,128)(2,1)}) custom-call(s32[1]{0:T(128)} %bitcast.3.me, bf16[320,2048]{1,0:T(8,128)(2,1)} %acts.1, bf16[1280,2048]{1,0:T(8,128)(2,1)} %grads.1), custom_call_target="tpu_custom_call" | custom-call | bytes 13107200 | tf_op jit(solution)/shard_map/arrange/pallas_call | solution.py:94
  17.3 0.0 copy-start.3
  17.3 0.9 %copy-done.3 = bf16[2,1600,128]{2,1,0:T(8,128)(2,1)} copy-done((bf16[2,1600,128]{2,1,0:T(8,128)(2,1)}, bf16[2,1600,128]{2,1,0:T(8,128)(2,1)S(1)}, u32[]{:S(2)}) %copy-start.3) | copy-done | bytes 819224
  18.2 5.5 %all-to-all-done = bf16[16,8,1600]{2,1,0:T(8,128)(2,1)S(1)} async-done(((bf16[16,8,1600]{2,1,0:T(8,128)(2,1)}), bf16[16,8,1600]{2,1,0:T(8,128)(2,1)S(1)}, u32[]{:S(2)}, u32[]{:S(2)}) %all-to-all-start) | async-done | bytes 409632 | tf_op jit(solution)/shard_map/all_to_all | solution.py:385
  23.7 1.1 %copy-done.4 = bf16[2,1600,128]{2,1,0:T(8,128)(2,1)S(1)} copy-done((bf16[2,1600,128]{2,1,0:T(8,128)(2,1)S(1)}, bf16[2,1600,128]{2,1,0:T(8,128)(2,1)}, u32[]{:S(2)}) %copy-start.4) | copy-done | bytes 819224
  24.9 0.6 project.7
  25.5 0.2 collective-permute-start
  25.7 1.5 %collective-permute-start.1 = (bf16[128,1600]{1,0:T(8,128)(2,1)S(1)}, bf16[128,1600]{1,0:T(8,128)(2,1)S(1)}, u32[]{:S(2)}, u32[]{:S(2)}) collective-permute-start(bf16[128,1600]{1,0:T(8,128)(2,1)S(1)} %bitcast.11), channel_id=1, source_target_pairs={{0,16},{16,0},{1,17},{17,1},{2,18},{18,2},{3,19},{19,3},{4,20},{20... | collective-permute-start | bytes 1228808 | tf_op jit(solution)/shard_map/ppermute | solution.py:394
  27.2 0.6 project.6.refs_0_
  27.9 0.4 collective-permute-done.refs_1_
  28.3 0.4 merge.4
  28.6 0.7 %collective-permute-start.2 = (s32[584,128]{1,0:T(8,128)S(1)}, s32[584,128]{1,0:T(8,128)S(1)}, u32[]{:S(2)}, u32[]{:S(2)}) collective-permute-start(s32[584,128]{1,0:T(8,128)S(1)} %merge.4), channel_id=1, source_target_pairs={{0,2},{1,3},{2,0},{3,1},{4,6},{5,7},{6,4},{7,5},{8,10},{9,11},{10,... | collective-permute-start | bytes 897032 | tf_op jit(solution)/shard_map/ppermute | solution.py:23
  29.4 8.5 %collective-permute-done.1.factors = bf16[128,1600]{1,0:T(8,128)(2,1)S(1)} collective-permute-done((bf16[128,1600]{1,0:T(8,128)(2,1)S(1)}, bf16[128,1600]{1,0:T(8,128)(2,1)S(1)}, u32[]{:S(2)}, u32[]{:S(2)}) %collective-permute-start.1) | collective-permute-done | bytes 409632 | tf_op jit(solution)/shard_map/ppermute | solution.py:394
  37.9 0.0 collective-permute-done.2.refs_2_
  37.9 0.4 project.9
  38.3 0.1 collective-permute-start.3
  38.4 0.4 project.11
  38.8 0.6 collective-permute-start.7
  39.3 0.4 project.8.refs_0_
  39.7 0.5 collective-permute-done.3.refs_1_
  40.3 0.4 merge.5
  40.6 0.9 %collective-permute-start.8 = (s32[584,128]{1,0:T(8,128)S(1)}, s32[584,128]{1,0:T(8,128)S(1)}, u32[]{:S(2)}, u32[]{:S(2)}) collective-permute-start(s32[584,128]{1,0:T(8,128)S(1)} %merge.5), channel_id=1, source_target_pairs={{0,2},{1,3},{2,0},{3,1},{4,6},{5,7},{6,4},{7,5},{8,10},{9,11},{10,... | collective-permute-start | bytes 897032 | tf_op jit(solution)/shard_map/ppermute | solution.py:23
  41.6 0.5 merge.6
  42.1 0.0 copy-start.6
  42.1 2.2 %collective-permute-start.4 = (s32[152,128]{1,0:T(8,128)S(1)}, s32[152,128]{1,0:T(8,128)S(1)}, u32[]{:S(2)}, u32[]{:S(2)}) collective-permute-start(s32[152,128]{1,0:T(8,128)S(1)} %get-tuple-element.44), channel_id=1, source_target_pairs={{0,12},{1,13},{2,14},{3,15},{4,8},{5,9},{6,10},{7,11},{8,4},{9,5},... | collective-permute-start | bytes 233480 | tf_op jit(solution)/shard_map/ppermute | solution.py:23
  44.3 0.4 project.10.refs_0_
  44.7 0.6 collective-permute-start.5
  45.4 1.7 %collective-permute-start.6 = (s32[152,128]{1,0:T(8,128)S(1)}, s32[152,128]{1,0:T(8,128)S(1)}, u32[]{:S(2)}, u32[]{:S(2)}) collective-permute-start(s32[152,128]{1,0:T(8,128)S(1)} %get-tuple-element.46), channel_id=1, source_target_pairs={{0,4},{1,5},{2,6},{3,7},{4,0},{5,1},{6,2},{7,3},{8,12},{9,13},{10,... | collective-permute-start | bytes 233480 | tf_op jit(solution)/shard_map/ppermute | solution.py:23
  47.0 0.0 collective-permute-done.7.refs_1_
  47.0 2.8 %collective-permute-done.8.refs_2_ = s32[584,128]{1,0:T(8,128)S(1)} collective-permute-done((s32[584,128]{1,0:T(8,128)S(1)}, s32[584,128]{1,0:T(8,128)S(1)}, u32[]{:S(2)}, u32[]{:S(2)}) %collective-permute-start.8) | collective-permute-done | bytes 299040 | tf_op jit(solution)/shard_map/ppermute | solution.py:23
  49.8 0.5 merge.7
  50.4 1.9 %collective-permute-start.10 = (s32[152,128]{1,0:T(8,128)S(1)}, s32[152,128]{1,0:T(8,128)S(1)}, u32[]{:S(2)}, u32[]{:S(2)}) collective-permute-start(s32[152,128]{1,0:T(8,128)S(1)} %get-tuple-element.49), channel_id=1, source_target_pairs={{0,8},{1,9},{2,10},{3,11},{4,12},{5,13},{6,14},{7,15},{8,0},{9,1},... | collective-permute-start | bytes 233480 | tf_op jit(solution)/shard_map/ppermute | solution.py:23
  52.3 0.3 collective-permute-start.11
  52.6 0.0 collective-permute-done.4.refs_1_
  52.6 2.2 %collective-permute-start.9 = (s32[152,128]{1,0:T(8,128)S(1)}, s32[152,128]{1,0:T(8,128)S(1)}, u32[]{:S(2)}, u32[]{:S(2)}) collective-permute-start(s32[152,128]{1,0:T(8,128)S(1)} %get-tuple-element.48), channel_id=1, source_target_pairs={{0,12},{1,13},{2,14},{3,15},{4,8},{5,9},{6,10},{7,11},{8,4},{9,5},... | collective-permute-start | bytes 233480 | tf_op jit(solution)/shard_map/ppermute | solution.py:23
  54.8 0.0 collective-permute-done.5.refs_2_
  54.8 0.0 collective-permute-done.6.refs_3_
  54.8 0.2 partial_scores.1.refs_0_
  55.1 3.0 %collective-permute-done.10.refs_3_ = s32[152,128]{1,0:T(8,128)S(1)} collective-permute-done((s32[152,128]{1,0:T(8,128)S(1)}, s32[152,128]{1,0:T(8,128)S(1)}, u32[]{:S(2)}, u32[]{:S(2)}) %collective-permute-start.10) | collective-permute-done | bytes 77856 | tf_op jit(solution)/shard_map/ppermute | solution.py:23
  58.0 0.0 collective-permute-done.11.refs_4_
  58.0 1.1 %collective-permute-done.9.refs_2_ = s32[152,128]{1,0:T(8,128)S(1)} collective-permute-done((s32[152,128]{1,0:T(8,128)S(1)}, s32[152,128]{1,0:T(8,128)S(1)}, u32[]{:S(2)}, u32[]{:S(2)}) %collective-permute-start.9) | collective-permute-done | bytes 77856 | tf_op jit(solution)/shard_map/ppermute | solution.py:23
  59.1 1.2 %tails.1 = (f32[8,128]{1,0:T(8,128)}, f32[16,128]{1,0:T(8,128)S(1)}) custom-call(f32[8,128]{1,0:T(8,128)S(1)} %partial_scores.1.refs_0_, f32[1,256,128]{2,1,0:T(8,128)S(1)} %get-tuple-element.47.refs_1_, s32[152,128]{1,0:T(8,128)S(1)} %collective-permute-done.9.refs_2_, s32[152,128]{1,0:T(8,128)S(1)} %collective-permute-done.10.refs_3_, ...), custom_call_target="tpu_custom_call" | custom-call | tf_op jit(solution)/shard_map/tails/pallas_call | solution.py:436
  60.3 0.0 collective-permute-start.12
  60.3 1.3 %collective-permute-start.13 = (f32[16,128]{1,0:T(8,128)S(1)}, f32[16,128]{1,0:T(8,128)S(1)}, u32[]{:S(2)}, u32[]{:S(2)}) collective-permute-start(f32[16,128]{1,0:T(8,128)S(1)} %get-tuple-element.53.refs_0_.refs_5_), channel_id=1, source_target_pairs={{0,2},{1,3},{2,0},{3,1},{4,6},{5,7},{6,4},{7,5},{8,10},{9,11},{10,... | collective-permute-start | bytes 24584 | tf_op jit(solution)/shard_map/ppermute | solution.py:23
  61.6 0.6 collective-permute-start.14
  62.2 1.2 %collective-permute-done.12.refs_1_ = f32[16,128]{1,0:T(8,128)S(1)} collective-permute-done((f32[16,128]{1,0:T(8,128)S(1)}, f32[16,128]{1,0:T(8,128)S(1)}, u32[]{:S(2)}, u32[]{:S(2)}) %collective-permute-start.12) | collective-permute-done | bytes 8224 | tf_op jit(solution)/shard_map/ppermute | solution.py:23
  63.4 0.6 collective-permute-done.13.refs_2_
  64.0 0.0 collective-permute-done.14.refs_3_
  64.0 0.1 fold_group.1
  64.1 2.1 %collective-permute-start.15 = (f32[16,128]{1,0:T(8,128)S(1)}, f32[16,128]{1,0:T(8,128)S(1)}, u32[]{:S(2)}, u32[]{:S(2)}) collective-permute-start(f32[16,128]{1,0:T(8,128)S(1)} %get-tuple-element.54.refs_0_), channel_id=1, source_target_pairs={{0,12},{1,13},{2,14},{3,15},{4,8},{5,9},{6,10},{7,11},{8,4},{9,5},... | collective-permute-start | bytes 24584 | tf_op jit(solution)/shard_map/ppermute | solution.py:23
  66.2 0.8 %collective-permute-start.16 = (f32[16,128]{1,0:T(8,128)S(1)}, f32[16,128]{1,0:T(8,128)S(1)}, u32[]{:S(2)}, u32[]{:S(2)}) collective-permute-start(f32[16,128]{1,0:T(8,128)S(1)} %get-tuple-element.54.refs_0_), channel_id=1, source_target_pairs={{0,8},{1,9},{2,10},{3,11},{4,12},{5,13},{6,14},{7,15},{8,0},{9,1},... | collective-permute-start | bytes 24584 | tf_op jit(solution)/shard_map/ppermute | solution.py:23
  67.0 1.5 %collective-permute-start.17 = (f32[16,128]{1,0:T(8,128)S(1)}, f32[16,128]{1,0:T(8,128)S(1)}, u32[]{:S(2)}, u32[]{:S(2)}) collective-permute-start(f32[16,128]{1,0:T(8,128)S(1)} %get-tuple-element.54.refs_0_), channel_id=1, source_target_pairs={{0,4},{1,5},{2,6},{3,7},{4,0},{5,1},{6,2},{7,3},{8,12},{9,13},{10,... | collective-permute-start | bytes 24584 | tf_op jit(solution)/shard_map/ppermute | solution.py:23
  68.5 1.1 %collective-permute-done.15.refs_1_ = f32[16,128]{1,0:T(8,128)S(1)} collective-permute-done((f32[16,128]{1,0:T(8,128)S(1)}, f32[16,128]{1,0:T(8,128)S(1)}, u32[]{:S(2)}, u32[]{:S(2)}) %collective-permute-start.15) | collective-permute-done | bytes 8224 | tf_op jit(solution)/shard_map/ppermute | solution.py:23
  69.6 1.2 %collective-permute-done.16.refs_2_ = f32[16,128]{1,0:T(8,128)S(1)} collective-permute-done((f32[16,128]{1,0:T(8,128)S(1)}, f32[16,128]{1,0:T(8,128)S(1)}, u32[]{:S(2)}, u32[]{:S(2)}) %collective-permute-start.16) | collective-permute-done | bytes 8224 | tf_op jit(solution)/shard_map/ppermute | solution.py:23
  70.8 0.0 collective-permute-done.17.refs_3_
  70.8 0.7 finish.1
  (15 shorter events, 0.1 us)
Async XLA Ops:
  0.6 1.1 %copy-start = (bf16[16,20480]{1,0:T(8,128)(2,1)S(1)}, bf16[16,20480]{1,0:T(8,128)(2,1)}, u32[]{:S(2)}) copy-start(bf16[16,20480]{1,0:T(8,128)(2,1)} %param.10) | copy-start | bytes 1966084
  0.6 10.4 %copy-start.8 = (s32[128]{0:T(128)S(1)}, s32[128]{0:T(128)}, u32[]{:S(2)}) copy-start(s32[128]{0:T(128)} %param.11) | copy-start | bytes 1540
  0.7 10.4 %copy-start.7 = (f32[50688]{0:T(1024)S(1)}, f32[50688]{0:T(1024)}, u32[]{:S(2)}) copy-start(f32[50688]{0:T(1024)} %param.13) | copy-start | bytes 608260
  3.6 20.1 %all-to-all-start = ((bf16[16,8,1600]{2,1,0:T(8,128)(2,1)}), bf16[16,8,1600]{2,1,0:T(8,128)(2,1)S(1)}, u32[]{:S(2)}, u32[]{:S(2)}) async-start(bf16[16,8,1600]{2,1,0:T(8,128)(2,1)} %pad_maximum_fusion), calls=%async_computation | async-start | bytes 851968 | tf_op jit(solution)/shard_map/all_to_all | solution.py:385
  17.3 0.9 %copy-start.3 = (bf16[2,1600,128]{2,1,0:T(8,128)(2,1)}, bf16[2,1600,128]{2,1,0:T(8,128)(2,1)S(1)}, u32[]{:S(2)}) copy-start(bf16[2,1600,128]{2,1,0:T(8,128)(2,1)S(1)} %get-tuple-element.39.rest_2_.rest_1_) | copy-start | bytes 2457604
  23.7 1.1 %copy-start.4 = (bf16[2,1600,128]{2,1,0:T(8,128)(2,1)S(1)}, bf16[2,1600,128]{2,1,0:T(8,128)(2,1)}, u32[]{:S(2)}) copy-start(bf16[2,1600,128]{2,1,0:T(8,128)(2,1)} %copy-done.3) | copy-start | bytes 2457604
  24.9 2.3 %copy-start.1 = (bf16[4,1600,128]{2,1,0:T(8,128)(2,1)S(1)}, bf16[4,1600,128]{2,1,0:T(8,128)(2,1)}, u32[]{:S(2)}) copy-start(bf16[4,1600,128]{2,1,0:T(8,128)(2,1)} %get-tuple-element.36.rest_1_.rest_0_) | copy-start | bytes 4915204
  24.9 2.3 %copy-start.2 = (bf16[4,1600,128]{2,1,0:T(8,128)(2,1)S(1)}, bf16[4,1600,128]{2,1,0:T(8,128)(2,1)}, u32[]{:S(2)}) copy-start(bf16[4,1600,128]{2,1,0:T(8,128)(2,1)} %get-tuple-element.35.rest_0_) | copy-start | bytes 4915204
  25.5 2.7 %collective-permute-start = (f32[8,256,128]{2,1,0:T(8,128)S(1)}, f32[8,256,128]{2,1,0:T(8,128)S(1)}, u32[]{:S(2)}, u32[]{:S(2)}) collective-permute-start(f32[8,256,128]{2,1,0:T(8,128)S(1)} %project.7), channel_id=1, source_target_pairs={{0,1},{1,0},{2,3},{3,2},{4,5},{5,4},{6,7},{7,6},{8,9},{9,8},{10,11... | collective-permute-start | bytes 3145736 | tf_op jit(solution)/shard_map/ppermute | solution.py:23
  25.7 12.2 %collective-permute-start.1 = (bf16[128,1600]{1,0:T(8,128)(2,1)S(1)}, bf16[128,1600]{1,0:T(8,128)(2,1)S(1)}, u32[]{:S(2)}, u32[]{:S(2)}) collective-permute-start(bf16[128,1600]{1,0:T(8,128)(2,1)S(1)} %bitcast.11), channel_id=1, source_target_pairs={{0,16},{16,0},{1,17},{17,1},{2,18},{18,2},{3,19},{19,3},{4,20},{20... | collective-permute-start | bytes 1228808 | tf_op jit(solution)/shard_map/ppermute | solution.py:394
  28.6 9.7 %copy-start.5 = (bf16[2,1600,128]{2,1,0:T(8,128)(2,1)S(1)}, bf16[2,1600,128]{2,1,0:T(8,128)(2,1)}, u32[]{:S(2)}) copy-start(bf16[2,1600,128]{2,1,0:T(8,128)(2,1)} %copy-done.3) | copy-start | bytes 2457604
  28.6 9.2 %collective-permute-start.2 = (s32[584,128]{1,0:T(8,128)S(1)}, s32[584,128]{1,0:T(8,128)S(1)}, u32[]{:S(2)}, u32[]{:S(2)}) collective-permute-start(s32[584,128]{1,0:T(8,128)S(1)} %merge.4), channel_id=1, source_target_pairs={{0,2},{1,3},{2,0},{3,1},{4,6},{5,7},{6,4},{7,5},{8,10},{9,11},{10,... | collective-permute-start | bytes 897032 | tf_op jit(solution)/shard_map/ppermute | solution.py:23
  38.3 2.0 %collective-permute-start.3 = (f32[4,256,128]{2,1,0:T(8,128)S(1)}, f32[4,256,128]{2,1,0:T(8,128)S(1)}, u32[]{:S(2)}, u32[]{:S(2)}) collective-permute-start(f32[4,256,128]{2,1,0:T(8,128)S(1)} %project.9), channel_id=1, source_target_pairs={{0,1},{1,0},{2,3},{3,2},{4,5},{5,4},{6,7},{7,6},{8,9},{9,8},{10,11... | collective-permute-start | bytes 1572872 | tf_op jit(solution)/shard_map/ppermute | solution.py:23
  38.8 8.3 %collective-permute-start.7 = (f32[4,256,128]{2,1,0:T(8,128)S(1)}, f32[4,256,128]{2,1,0:T(8,128)S(1)}, u32[]{:S(2)}, u32[]{:S(2)}) collective-permute-start(f32[4,256,128]{2,1,0:T(8,128)S(1)} %project.11), channel_id=1, source_target_pairs={{0,1},{1,0},{2,3},{3,2},{4,5},{5,4},{6,7},{7,6},{8,9},{9,8},{10,11... | collective-permute-start | bytes 1572872 | tf_op jit(solution)/shard_map/ppermute | solution.py:23
  40.6 9.2 %collective-permute-start.8 = (s32[584,128]{1,0:T(8,128)S(1)}, s32[584,128]{1,0:T(8,128)S(1)}, u32[]{:S(2)}, u32[]{:S(2)}) collective-permute-start(s32[584,128]{1,0:T(8,128)S(1)} %merge.5), channel_id=1, source_target_pairs={{0,2},{1,3},{2,0},{3,1},{4,6},{5,7},{6,4},{7,5},{8,10},{9,11},{10,... | collective-permute-start | bytes 897032 | tf_op jit(solution)/shard_map/ppermute | solution.py:23
  42.1 17.0 %copy-start.6 = (s32[128]{0:T(128)S(1)}, s32[128]{0:T(128)}, u32[]{:S(2)}) copy-start(s32[128]{0:T(128)} %param.12) | copy-start | bytes 1540
  42.1 10.5 %collective-permute-start.4 = (s32[152,128]{1,0:T(8,128)S(1)}, s32[152,128]{1,0:T(8,128)S(1)}, u32[]{:S(2)}, u32[]{:S(2)}) collective-permute-start(s32[152,128]{1,0:T(8,128)S(1)} %get-tuple-element.44), channel_id=1, source_target_pairs={{0,12},{1,13},{2,14},{3,15},{4,8},{5,9},{6,10},{7,11},{8,4},{9,5},... | collective-permute-start | bytes 233480 | tf_op jit(solution)/shard_map/ppermute | solution.py:23
  44.7 10.1 %collective-permute-start.5 = (s32[152,128]{1,0:T(8,128)S(1)}, s32[152,128]{1,0:T(8,128)S(1)}, u32[]{:S(2)}, u32[]{:S(2)}) collective-permute-start(s32[152,128]{1,0:T(8,128)S(1)} %get-tuple-element.45), channel_id=1, source_target_pairs={{0,8},{1,9},{2,10},{3,11},{4,12},{5,13},{6,14},{7,15},{8,0},{9,1},... | collective-permute-start | bytes 233480 | tf_op jit(solution)/shard_map/ppermute | solution.py:23
  45.4 9.5 %collective-permute-start.6 = (s32[152,128]{1,0:T(8,128)S(1)}, s32[152,128]{1,0:T(8,128)S(1)}, u32[]{:S(2)}, u32[]{:S(2)}) collective-permute-start(s32[152,128]{1,0:T(8,128)S(1)} %get-tuple-element.46), channel_id=1, source_target_pairs={{0,4},{1,5},{2,6},{3,7},{4,0},{5,1},{6,2},{7,3},{8,12},{9,13},{10,... | collective-permute-start | bytes 233480 | tf_op jit(solution)/shard_map/ppermute | solution.py:23
  50.4 7.7 %collective-permute-start.10 = (s32[152,128]{1,0:T(8,128)S(1)}, s32[152,128]{1,0:T(8,128)S(1)}, u32[]{:S(2)}, u32[]{:S(2)}) collective-permute-start(s32[152,128]{1,0:T(8,128)S(1)} %get-tuple-element.49), channel_id=1, source_target_pairs={{0,8},{1,9},{2,10},{3,11},{4,12},{5,13},{6,14},{7,15},{8,0},{9,1},... | collective-permute-start | bytes 233480 | tf_op jit(solution)/shard_map/ppermute | solution.py:23
  52.3 5.7 %collective-permute-start.11 = (s32[152,128]{1,0:T(8,128)S(1)}, s32[152,128]{1,0:T(8,128)S(1)}, u32[]{:S(2)}, u32[]{:S(2)}) collective-permute-start(s32[152,128]{1,0:T(8,128)S(1)} %get-tuple-element.50), channel_id=1, source_target_pairs={{0,4},{1,5},{2,6},{3,7},{4,0},{5,1},{6,2},{7,3},{8,12},{9,13},{10,... | collective-permute-start | bytes 233480 | tf_op jit(solution)/shard_map/ppermute | solution.py:23
  52.6 6.5 %collective-permute-start.9 = (s32[152,128]{1,0:T(8,128)S(1)}, s32[152,128]{1,0:T(8,128)S(1)}, u32[]{:S(2)}, u32[]{:S(2)}) collective-permute-start(s32[152,128]{1,0:T(8,128)S(1)} %get-tuple-element.48), channel_id=1, source_target_pairs={{0,12},{1,13},{2,14},{3,15},{4,8},{5,9},{6,10},{7,11},{8,4},{9,5},... | collective-permute-start | bytes 233480 | tf_op jit(solution)/shard_map/ppermute | solution.py:23
  60.3 3.1 %collective-permute-start.12 = (f32[16,128]{1,0:T(8,128)S(1)}, f32[16,128]{1,0:T(8,128)S(1)}, u32[]{:S(2)}, u32[]{:S(2)}) collective-permute-start(f32[16,128]{1,0:T(8,128)S(1)} %get-tuple-element.53.refs_0_.refs_5_), channel_id=1, source_target_pairs={{0,3},{1,2},{2,1},{3,0},{4,7},{5,6},{6,5},{7,4},{8,11},{9,10},{10,... | collective-permute-start | bytes 24584 | tf_op jit(solution)/shard_map/ppermute | solution.py:23
  60.3 3.7 %collective-permute-start.13 = (f32[16,128]{1,0:T(8,128)S(1)}, f32[16,128]{1,0:T(8,128)S(1)}, u32[]{:S(2)}, u32[]{:S(2)}) collective-permute-start(f32[16,128]{1,0:T(8,128)S(1)} %get-tuple-element.53.refs_0_.refs_5_), channel_id=1, source_target_pairs={{0,2},{1,3},{2,0},{3,1},{4,6},{5,7},{6,4},{7,5},{8,10},{9,11},{10,... | collective-permute-start | bytes 24584 | tf_op jit(solution)/shard_map/ppermute | solution.py:23
  61.6 2.4 %collective-permute-start.14 = (f32[16,128]{1,0:T(8,128)S(1)}, f32[16,128]{1,0:T(8,128)S(1)}, u32[]{:S(2)}, u32[]{:S(2)}) collective-permute-start(f32[16,128]{1,0:T(8,128)S(1)} %get-tuple-element.53.refs_0_.refs_5_), channel_id=1, source_target_pairs={{0,1},{1,0},{2,3},{3,2},{4,5},{5,4},{6,7},{7,6},{8,9},{9,8},{10,11... | collective-permute-start | bytes 24584 | tf_op jit(solution)/shard_map/ppermute | solution.py:23
  64.1 5.5 %collective-permute-start.15 = (f32[16,128]{1,0:T(8,128)S(1)}, f32[16,128]{1,0:T(8,128)S(1)}, u32[]{:S(2)}, u32[]{:S(2)}) collective-permute-start(f32[16,128]{1,0:T(8,128)S(1)} %get-tuple-element.54.refs_0_), channel_id=1, source_target_pairs={{0,12},{1,13},{2,14},{3,15},{4,8},{5,9},{6,10},{7,11},{8,4},{9,5},... | collective-permute-start | bytes 24584 | tf_op jit(solution)/shard_map/ppermute | solution.py:23
  66.2 4.5 %collective-permute-start.16 = (f32[16,128]{1,0:T(8,128)S(1)}, f32[16,128]{1,0:T(8,128)S(1)}, u32[]{:S(2)}, u32[]{:S(2)}) collective-permute-start(f32[16,128]{1,0:T(8,128)S(1)} %get-tuple-element.54.refs_0_), channel_id=1, source_target_pairs={{0,8},{1,9},{2,10},{3,11},{4,12},{5,13},{6,14},{7,15},{8,0},{9,1},... | collective-permute-start | bytes 24584 | tf_op jit(solution)/shard_map/ppermute | solution.py:23
  67.0 3.8 %collective-permute-start.17 = (f32[16,128]{1,0:T(8,128)S(1)}, f32[16,128]{1,0:T(8,128)S(1)}, u32[]{:S(2)}, u32[]{:S(2)}) collective-permute-start(f32[16,128]{1,0:T(8,128)S(1)} %get-tuple-element.54.refs_0_), channel_id=1, source_target_pairs={{0,4},{1,5},{2,6},{3,7},{4,0},{5,1},{6,2},{7,3},{8,12},{9,13},{10,... | collective-permute-start | bytes 24584 | tf_op jit(solution)/shard_map/ppermute | solution.py:23

commit v7 on v6

--- a/solution.py
+++ b/solution.py
@@ -276,9 +276,39 @@
     )(*parts)
 
 
+def docs_kernel(queries, doc_starts, same_doc, info):
+    lane = lax.broadcasted_iota(jnp.int32, (8, LANES), 1)
+    start = jnp.where(doc_starts[...] > 0, lane, -1)
+    step = 1
+    while step < LANES:
+        start = jnp.maximum(start, jnp.where(lane >= step, pltpu.roll(start, step, 1), -1))
+        step *= 2
+    start = start[0:1, :]
+    lane = lane[0:1, :]
+    earlier = lax.broadcasted_iota(jnp.int32, (LANES, LANES), 0)
+    same_doc[...] = ((earlier >= start) & (earlier <= lane)).astype(F32)
+    number = (lane - jnp.maximum(start, 0) + 1).astype(F32)
+    started = (start >= 0).astype(F32)
+    row = lax.broadcasted_iota(jnp.int32, (queries, LANES), 0)
+    rest = jnp.where(row == 2, 1.0 - started, 0.0)
+    info[...] = jnp.where(row == 0, number, jnp.where(row == 1, started, rest))
+
+
+def documents(doc_starts, queries):
+    return pl.pallas_call(
+        functools.partial(docs_kernel, queries),
+        out_shape=[
+            jax.ShapeDtypeStruct((LANES, LANES), F32),
+            jax.ShapeDtypeStruct((queries, LANES), F32),
+        ],
+        compiler_params=room(),
+        name="documents",
+    )(doc_starts[None, :])
+
+
 def tail_kernel(count, queries, ranks, *refs):
-    ready, last = refs[:count], refs[count:-4]
-    weights, doc_starts, scores, message = refs[-4:]
+    ready, last = refs[:count], refs[count:-5]
+    weights, same_doc, info, scores, message = refs[-5:]
     parts = [ref[...] for ref in ready] + [rank_sums(last, ranks)]
     value = None
     while parts:
@@ -289,26 +319,10 @@
         value = chunk if value is None else value + chunk
     value = value * weights[...]
     scores[...] = value
-    lane = lax.broadcasted_iota(jnp.int32, (8, LANES), 1)
-    start = jnp.where(doc_starts[...] > 0, lane, -1)
-    step = 1
-    while step < LANES:
-        start = jnp.maximum(start, jnp.where(lane >= step, pltpu.roll(start, step, 1), -1))
-        step *= 2
-    start = start[0:1, :]
-    lane = lane[0:1, :]
-    earlier = lax.broadcasted_iota(jnp.int32, (LANES, LANES), 0)
-    same_doc = ((earlier >= start) & (earlier <= lane)).astype(F32)
-    total = jnp.dot(
-        value, same_doc, precision=lax.Precision.HIGHEST, preferred_element_type=F32
+    message[0:queries, :] = jnp.dot(
+        value, same_doc[...], precision=lax.Precision.HIGHEST, preferred_element_type=F32
     )
-    number = (lane - jnp.maximum(start, 0) + 1).astype(F32)
-    started = (start >= 0).astype(F32)
-    message[0:queries, :] = total
-    message[queries : queries + 1, :] = number
-    message[queries + 1 : queries + 2, :] = started
-    message[queries + 2 : queries + 3, :] = 1.0 - started
-    message[queries + 3 :, :] = jnp.zeros_like(message[queries + 3 :, :])
+    message[queries:, :] = info[...]
 
 
 def fold_members(queries, me, refs, shift):
@@ -385,7 +399,10 @@
     arrived = lax.all_to_all(outgoing, "loop", split_axis=0, concat_axis=0, tiled=True)
     columns = arrange(me, activations, out_grads)
     weights = jnp.take(token_weights, token_ids, mode="clip") * RANK ** (-0.5)
-    arrived, columns, weights = lax.optimization_barrier((arrived, columns, weights))
+    same_doc, info = documents(doc_starts, queries)
+    arrived, columns, weights, same_doc, info = lax.optimization_barrier(
+        (arrived, columns, weights, same_doc, info)
+    )
     own = arrived.reshape(size * part, depth + depths[0])
     stages = later_stages(size)
     count = size // 4
@@ -438,7 +455,7 @@
         out_shape=[tile, jax.ShapeDtypeStruct((2 * queries, LANES), F32)],
         compiler_params=room(),
         name="tails",
-    )(*ready, *last, weights[None, :], doc_starts[None, :])
+    )(*ready, *last, weights[None, :], same_doc, info)
 
     own_message = message
     befores = []

time: 71.8 us -> 71.4 us (level)
  waiting for transfers between devices: 25.8 us -> 24.6 us
    all_to_all x1, waiting for transfers between devices: 5.52 us -> 4.36 us  [local(): lax.all_to_all(outgoing, 'loop', split_axis=0, concat_axis=0, tiled=True)]
    unnamed x18 -> x22, local copies, waits for them, and re-layouts: 3.1 us -> 3.74 us
where the time goes in v7:
time: 71.4 us; the launch traced here: 71.1 us
  starting transfers between devices  26.7 us (37%)
  waiting for transfers between devices  24.6 us (34%)
  Pallas kernels  12.1 us (17%)
  local copies, waits for them, and re-layouts  5.97 us (8%)
  between operations  0.87 us (1%)
  other arithmetic  0.81 us (1%)
    ppermute x17, starting transfers between devices, swap(): return lax.ppermute(value, axis, [(i, i ^ offset) for i in range(size)])  17.8 us
    ppermute x17, waiting for transfers between devices, swap(): return lax.ppermute(value, axis, [(i, i ^ offset) for i in range(size)])  11.8 us
    ppermute x1, waiting for transfers between devices, local(): other = lax.ppermute(own, 'groups', [(i, i ^ 1) for i in range(groups)])  8.44 us
    all_to_all x1, starting transfers between devices, local(): lax.all_to_all(outgoing, 'loop', split_axis=0, concat_axis=0, tiled=True)  7.39 us
    pallas_call x1, Pallas kernels, arrange(): pl.pallas_call(arrange_kernel, in_specs=[pl.BlockSpec(memory_space=pltpu....  5.12 us
    all_to_all x1, waiting for transfers between devices, local(): lax.all_to_all(outgoing, 'loop', split_axis=0, concat_axis=0, tiled=True)  4.36 us
    unnamed x22, local copies, waits for them, and re-layouts  3.74 us
    pallas_call x6, Pallas kernels, project(): pl.pallas_call(functools.partial(project_kernel, depths, len(columns)), o...  2.87 us
  transfers between devices with their start and end apart: 19, of which 11 were waited for; matrix products, arithmetic and copies ran while one was open for 2% of the time, Pallas kernels for 13%

profile of v7, /device:TPU:0, one launch (start us, length us, event | category | flops | bytes accessed | tf_op | source)
XLA Modules:
  0.0 71.1 jit_solution(1671254735835680291)
XLA Ops:
  0.6 0.0 copy-start
  0.7 1.0 %copy-done = bf16[16,20480]{1,0:T(8,128)(2,1)S(1)} copy-done((bf16[16,20480]{1,0:T(8,128)(2,1)S(1)}, bf16[16,20480]{1,0:T(8,128)(2,1)}, u32[]{:S(2)}) %copy-start) | copy-done | bytes 655384
  1.8 0.9 %constant_dynamic-slice_fusion = bf16[8,5120]{1,0:T(8,128)(2,1)S(1)} fusion(bf16[16,5120]{1,0:T(8,128)(2,1)} %param.9, s32[]{:T(128)S(6)} %select_n.4), kind=kLoop, calls=%fused_computation.3 | loop fusion | bytes 163844 | tf_op jit(solution)/shard_map/dynamic_slice | solution.py:391
  2.7 0.1 reshape.17
  2.8 0.8 %pad_maximum_fusion = bf16[16,8,1600]{2,1,0:T(8,128)(2,1)} fusion(bf16[16,8,320]{2,1,0:T(8,128)(2,1)S(1)} %copy.9, bf16[16,8,1280]{2,1,0:T(8,128)(2,1)S(1)} %bitcast.15), kind=kLoop, calls=%fused_computation.1 | loop fusion | flops 819200 | bytes 819200 | tf_op jit(solution)/shard_map/concatenate | solution.py:396
  3.6 7.4 %all-to-all-start = ((bf16[16,8,1600]{2,1,0:T(8,128)(2,1)}), bf16[16,8,1600]{2,1,0:T(8,128)(2,1)S(1)}, u32[]{:S(2)}, u32[]{:S(2)}) async-start(bf16[16,8,1600]{2,1,0:T(8,128)(2,1)} %pad_maximum_fusion), calls=%async_computation | async-start | bytes 851968 | tf_op jit(solution)/shard_map/all_to_all | solution.py:399
  11.0 0.5 documents.1
  11.5 0.6 copy-done.6
  12.2 0.0 copy-done.9
  12.2 1.1 %gather_fusion = f32[128]{0:T(128)S(1)} fusion(f32[50688]{0:T(1024)S(1)} %copy-done.9, s32[1024]{0:T(1024)S(1)} %pad_clamp_fusion), kind=kCustom, calls=%fused_computation | custom fusion | bytes 1536 | tf_op jit(solution)/shard_map/jit(_take)/gather | solution.py:401
  13.4 5.1 %arrange.1 = (bf16[4,1600,128]{2,1,0:T(8,128)(2,1)S(1)}, bf16[2,1600,128]{2,1,0:T(8,128)(2,1)S(1)}, bf16[2,1600,128]{2,1,0:T(8,128)(2,1)S(1)}, bf16[4,1600,128]{2,1,0:T(8,128)(2,1)}, bf16[4,1600,128]{2,1,0:T(8,128)(2,1)}) custom-call(s32[1]{0:T(128)} %bitcast.3.me, bf16[320,2048]{1,0:T(8,128)(2,1)} %acts.1, bf16[1280,2048]{1,0:T(8,128)(2,1)} %grads.1), custom_call_target="tpu_custom_call" | custom-call | bytes 13107200 | tf_op jit(solution)/shard_map/arrange/pallas_call | solution.py:94
  18.5 0.9 %copy-done.3 = bf16[2,1600,128]{2,1,0:T(8,128)(2,1)} copy-done((bf16[2,1600,128]{2,1,0:T(8,128)(2,1)}, bf16[2,1600,128]{2,1,0:T(8,128)(2,1)S(1)}, u32[]{:S(2)}) %copy-start.3) | copy-done | bytes 819224
  19.4 4.4 %all-to-all-done = bf16[16,8,1600]{2,1,0:T(8,128)(2,1)S(1)} async-done(((bf16[16,8,1600]{2,1,0:T(8,128)(2,1)}), bf16[16,8,1600]{2,1,0:T(8,128)(2,1)S(1)}, u32[]{:S(2)}, u32[]{:S(2)}) %all-to-all-start) | async-done | bytes 409632 | tf_op jit(solution)/shard_map/all_to_all | solution.py:399
  23.7 1.1 %copy-done.4 = bf16[2,1600,128]{2,1,0:T(8,128)(2,1)S(1)} copy-done((bf16[2,1600,128]{2,1,0:T(8,128)(2,1)S(1)}, bf16[2,1600,128]{2,1,0:T(8,128)(2,1)}, u32[]{:S(2)}) %copy-start.4) | copy-done | bytes 819224
  24.9 0.6 project.7
  25.5 0.2 collective-permute-start
  25.7 1.5 %collective-permute-start.1 = (bf16[128,1600]{1,0:T(8,128)(2,1)S(1)}, bf16[128,1600]{1,0:T(8,128)(2,1)S(1)}, u32[]{:S(2)}, u32[]{:S(2)}) collective-permute-start(bf16[128,1600]{1,0:T(8,128)(2,1)S(1)} %bitcast.11), channel_id=1, source_target_pairs={{0,16},{16,0},{1,17},{17,1},{2,18},{18,2},{3,19},{19,3},{4,20},{20... | collective-permute-start | bytes 1228808 | tf_op jit(solution)/shard_map/ppermute | solution.py:411
  27.2 0.6 project.6.refs_0_
  27.9 0.4 collective-permute-done.refs_1_
  28.3 0.4 merge.4
  28.6 0.8 %collective-permute-start.2 = (s32[584,128]{1,0:T(8,128)S(1)}, s32[584,128]{1,0:T(8,128)S(1)}, u32[]{:S(2)}, u32[]{:S(2)}) collective-permute-start(s32[584,128]{1,0:T(8,128)S(1)} %merge.4), channel_id=1, source_target_pairs={{0,2},{1,3},{2,0},{3,1},{4,6},{5,7},{6,4},{7,5},{8,10},{9,11},{10,... | collective-permute-start | bytes 897032 | tf_op jit(solution)/shard_map/ppermute | solution.py:23
  29.4 8.4 %collective-permute-done.1.factors = bf16[128,1600]{1,0:T(8,128)(2,1)S(1)} collective-permute-done((bf16[128,1600]{1,0:T(8,128)(2,1)S(1)}, bf16[128,1600]{1,0:T(8,128)(2,1)S(1)}, u32[]{:S(2)}, u32[]{:S(2)}) %collective-permute-start.1) | collective-permute-done | bytes 409632 | tf_op jit(solution)/shard_map/ppermute | solution.py:411
  37.8 0.0 collective-permute-done.2.refs_2_
  37.8 0.4 project.9
  38.2 0.1 collective-permute-start.3
  38.3 0.4 project.11
  38.7 0.6 collective-permute-start.7
  39.3 0.4 project.8.refs_0_
  39.7 0.5 collective-permute-done.3.refs_1_
  40.2 0.4 merge.5
  40.6 1.0 %collective-permute-start.8 = (s32[584,128]{1,0:T(8,128)S(1)}, s32[584,128]{1,0:T(8,128)S(1)}, u32[]{:S(2)}, u32[]{:S(2)}) collective-permute-start(s32[584,128]{1,0:T(8,128)S(1)} %merge.5), channel_id=1, source_target_pairs={{0,2},{1,3},{2,0},{3,1},{4,6},{5,7},{6,4},{7,5},{8,10},{9,11},{10,... | collective-permute-start | bytes 897032 | tf_op jit(solution)/shard_map/ppermute | solution.py:23
  41.6 0.5 merge.6
  42.1 2.2 %collective-permute-start.4 = (s32[152,128]{1,0:T(8,128)S(1)}, s32[152,128]{1,0:T(8,128)S(1)}, u32[]{:S(2)}, u32[]{:S(2)}) collective-permute-start(s32[152,128]{1,0:T(8,128)S(1)} %get-tuple-element.50), channel_id=1, source_target_pairs={{0,12},{1,13},{2,14},{3,15},{4,8},{5,9},{6,10},{7,11},{8,4},{9,5},... | collective-permute-start | bytes 233480 | tf_op jit(solution)/shard_map/ppermute | solution.py:23
  44.3 0.4 project.10.refs_0_
  44.7 0.6 collective-permute-start.5
  45.4 1.7 %collective-permute-start.6 = (s32[152,128]{1,0:T(8,128)S(1)}, s32[152,128]{1,0:T(8,128)S(1)}, u32[]{:S(2)}, u32[]{:S(2)}) collective-permute-start(s32[152,128]{1,0:T(8,128)S(1)} %get-tuple-element.52), channel_id=1, source_target_pairs={{0,4},{1,5},{2,6},{3,7},{4,0},{5,1},{6,2},{7,3},{8,12},{9,13},{10,... | collective-permute-start | bytes 233480 | tf_op jit(solution)/shard_map/ppermute | solution.py:23
  47.0 0.0 collective-permute-done.7.refs_1_
  47.1 2.7 %collective-permute-done.8.refs_2_ = s32[584,128]{1,0:T(8,128)S(1)} collective-permute-done((s32[584,128]{1,0:T(8,128)S(1)}, s32[584,128]{1,0:T(8,128)S(1)}, u32[]{:S(2)}, u32[]{:S(2)}) %collective-permute-start.8) | collective-permute-done | bytes 299040 | tf_op jit(solution)/shard_map/ppermute | solution.py:23
  49.8 0.5 merge.7
  50.3 2.0 %collective-permute-start.10 = (s32[152,128]{1,0:T(8,128)S(1)}, s32[152,128]{1,0:T(8,128)S(1)}, u32[]{:S(2)}, u32[]{:S(2)}) collective-permute-start(s32[152,128]{1,0:T(8,128)S(1)} %get-tuple-element.55), channel_id=1, source_target_pairs={{0,8},{1,9},{2,10},{3,11},{4,12},{5,13},{6,14},{7,15},{8,0},{9,1},... | collective-permute-start | bytes 233480 | tf_op jit(solution)/shard_map/ppermute | solution.py:23
  52.3 0.3 collective-permute-start.11
  52.6 0.0 collective-permute-done.4.refs_1_
  52.6 2.2 %collective-permute-start.9 = (s32[152,128]{1,0:T(8,128)S(1)}, s32[152,128]{1,0:T(8,128)S(1)}, u32[]{:S(2)}, u32[]{:S(2)}) collective-permute-start(s32[152,128]{1,0:T(8,128)S(1)} %get-tuple-element.54), channel_id=1, source_target_pairs={{0,12},{1,13},{2,14},{3,15},{4,8},{5,9},{6,10},{7,11},{8,4},{9,5},... | collective-permute-start | bytes 233480 | tf_op jit(solution)/shard_map/ppermute | solution.py:23
  54.8 0.0 collective-permute-done.5.refs_2_
  54.8 0.0 collective-permute-done.6.refs_3_
  54.8 0.2 partial_scores.1.refs_0_
  55.0 2.9 %collective-permute-done.10.refs_3_ = s32[152,128]{1,0:T(8,128)S(1)} collective-permute-done((s32[152,128]{1,0:T(8,128)S(1)}, s32[152,128]{1,0:T(8,128)S(1)}, u32[]{:S(2)}, u32[]{:S(2)}) %collective-permute-start.10) | collective-permute-done | bytes 77856 | tf_op jit(solution)/shard_map/ppermute | solution.py:23
  58.0 0.0 collective-permute-done.11.refs_4_
  58.0 1.1 %collective-permute-done.9.refs_2_ = s32[152,128]{1,0:T(8,128)S(1)} collective-permute-done((s32[152,128]{1,0:T(8,128)S(1)}, s32[152,128]{1,0:T(8,128)S(1)}, u32[]{:S(2)}, u32[]{:S(2)}) %collective-permute-start.9) | collective-permute-done | bytes 77856 | tf_op jit(solution)/shard_map/ppermute | solution.py:23
  59.1 0.8 %tails.1 = (f32[8,128]{1,0:T(8,128)}, f32[16,128]{1,0:T(8,128)S(1)}) custom-call(f32[8,128]{1,0:T(8,128)S(1)} %partial_scores.1.refs_0_, f32[1,256,128]{2,1,0:T(8,128)S(1)} %get-tuple-element.53.refs_1_, s32[152,128]{1,0:T(8,128)S(1)} %collective-permute-done.9.refs_2_, s32[152,128]{1,0:T(8,128)S(1)} %collective-permute-done.10.refs_3_, ...), custom_call_target="tpu_custom_call" | custom-call | tf_op jit(solution)/shard_map/tails/pallas_call | solution.py:453
  59.9 0.0 collective-permute-start.12
  59.9 1.3 %collective-permute-start.13 = (f32[16,128]{1,0:T(8,128)S(1)}, f32[16,128]{1,0:T(8,128)S(1)}, u32[]{:S(2)}, u32[]{:S(2)}) collective-permute-start(f32[16,128]{1,0:T(8,128)S(1)} %get-tuple-element.61.refs_0_.refs_5_), channel_id=1, source_target_pairs={{0,2},{1,3},{2,0},{3,1},{4,6},{5,7},{6,4},{7,5},{8,10},{9,11},{10,... | collective-permute-start | bytes 24584 | tf_op jit(solution)/shard_map/ppermute | solution.py:23
  61.2 0.6 collective-permute-start.14
  61.8 1.2 %collective-permute-done.12.refs_1_ = f32[16,128]{1,0:T(8,128)S(1)} collective-permute-done((f32[16,128]{1,0:T(8,128)S(1)}, f32[16,128]{1,0:T(8,128)S(1)}, u32[]{:S(2)}, u32[]{:S(2)}) %collective-permute-start.12) | collective-permute-done | bytes 8224 | tf_op jit(solution)/shard_map/ppermute | solution.py:23
  63.0 0.6 collective-permute-done.13.refs_2_
  63.6 0.0 collective-permute-done.14.refs_3_
  63.6 0.1 fold_group.1
  63.7 2.1 %collective-permute-start.15 = (f32[16,128]{1,0:T(8,128)S(1)}, f32[16,128]{1,0:T(8,128)S(1)}, u32[]{:S(2)}, u32[]{:S(2)}) collective-permute-start(f32[16,128]{1,0:T(8,128)S(1)} %get-tuple-element.62.refs_0_), channel_id=1, source_target_pairs={{0,12},{1,13},{2,14},{3,15},{4,8},{5,9},{6,10},{7,11},{8,4},{9,5},... | collective-permute-start | bytes 24584 | tf_op jit(solution)/shard_map/ppermute | solution.py:23
  65.8 0.7 %collective-permute-start.16 = (f32[16,128]{1,0:T(8,128)S(1)}, f32[16,128]{1,0:T(8,128)S(1)}, u32[]{:S(2)}, u32[]{:S(2)}) collective-permute-start(f32[16,128]{1,0:T(8,128)S(1)} %get-tuple-element.62.refs_0_), channel_id=1, source_target_pairs={{0,8},{1,9},{2,10},{3,11},{4,12},{5,13},{6,14},{7,15},{8,0},{9,1},... | collective-permute-start | bytes 24584 | tf_op jit(solution)/shard_map/ppermute | solution.py:23
  66.6 1.5 %collective-permute-start.17 = (f32[16,128]{1,0:T(8,128)S(1)}, f32[16,128]{1,0:T(8,128)S(1)}, u32[]{:S(2)}, u32[]{:S(2)}) collective-permute-start(f32[16,128]{1,0:T(8,128)S(1)} %get-tuple-element.62.refs_0_), channel_id=1, source_target_pairs={{0,4},{1,5},{2,6},{3,7},{4,0},{5,1},{6,2},{7,3},{8,12},{9,13},{10,... | collective-permute-start | bytes 24584 | tf_op jit(solution)/shard_map/ppermute | solution.py:23
  68.1 1.1 %collective-permute-done.15.refs_1_ = f32[16,128]{1,0:T(8,128)S(1)} collective-permute-done((f32[16,128]{1,0:T(8,128)S(1)}, f32[16,128]{1,0:T(8,128)S(1)}, u32[]{:S(2)}, u32[]{:S(2)}) %collective-permute-start.15) | collective-permute-done | bytes 8224 | tf_op jit(solution)/shard_map/ppermute | solution.py:23
  69.2 1.2 %collective-permute-done.16.refs_2_ = f32[16,128]{1,0:T(8,128)S(1)} collective-permute-done((f32[16,128]{1,0:T(8,128)S(1)}, f32[16,128]{1,0:T(8,128)S(1)}, u32[]{:S(2)}, u32[]{:S(2)}) %collective-permute-start.16) | collective-permute-done | bytes 8224 | tf_op jit(solution)/shard_map/ppermute | solution.py:23
  70.4 0.0 collective-permute-done.17.refs_3_
  70.4 0.7 finish.1
  (20 shorter events, 0.1 us)
Async XLA Ops:
  0.6 1.1 %copy-start = (bf16[16,20480]{1,0:T(8,128)(2,1)S(1)}, bf16[16,20480]{1,0:T(8,128)(2,1)}, u32[]{:S(2)}) copy-start(bf16[16,20480]{1,0:T(8,128)(2,1)} %param.10) | copy-start | bytes 1966084
  0.6 10.4 %copy-start.8 = (s32[128]{0:T(128)S(1)}, s32[128]{0:T(128)}, u32[]{:S(2)}) copy-start(s32[128]{0:T(128)} %param.12) | copy-start | bytes 1540
  0.7 11.5 %copy-start.10 = (s32[128]{0:T(128)S(1)}, s32[128]{0:T(128)}, u32[]{:S(2)}) copy-start(s32[128]{0:T(128)} %param.11) | copy-start | bytes 1540
  0.7 11.5 %copy-start.9 = (f32[50688]{0:T(1024)S(1)}, f32[50688]{0:T(1024)}, u32[]{:S(2)}) copy-start(f32[50688]{0:T(1024)} %param.13) | copy-start | bytes 608260
  3.6 20.1 %all-to-all-start = ((bf16[16,8,1600]{2,1,0:T(8,128)(2,1)}), bf16[16,8,1600]{2,1,0:T(8,128)(2,1)S(1)}, u32[]{:S(2)}, u32[]{:S(2)}) async-start(bf16[16,8,1600]{2,1,0:T(8,128)(2,1)} %pad_maximum_fusion), calls=%async_computation | async-start | bytes 851968 | tf_op jit(solution)/shard_map/all_to_all | solution.py:399
  11.5 0.6 copy-start.6
  18.5 0.9 %copy-start.3 = (bf16[2,1600,128]{2,1,0:T(8,128)(2,1)}, bf16[2,1600,128]{2,1,0:T(8,128)(2,1)S(1)}, u32[]{:S(2)}) copy-start(bf16[2,1600,128]{2,1,0:T(8,128)(2,1)S(1)} %get-tuple-element.45.rest_2_.rest_1_) | copy-start | bytes 2457604
  23.7 1.1 %copy-start.4 = (bf16[2,1600,128]{2,1,0:T(8,128)(2,1)S(1)}, bf16[2,1600,128]{2,1,0:T(8,128)(2,1)}, u32[]{:S(2)}) copy-start(bf16[2,1600,128]{2,1,0:T(8,128)(2,1)} %copy-done.3) | copy-start | bytes 2457604
  24.9 2.3 %copy-start.1 = (bf16[4,1600,128]{2,1,0:T(8,128)(2,1)S(1)}, bf16[4,1600,128]{2,1,0:T(8,128)(2,1)}, u32[]{:S(2)}) copy-start(bf16[4,1600,128]{2,1,0:T(8,128)(2,1)} %get-tuple-element.42.rest_1_.rest_0_) | copy-start | bytes 4915204
  24.9 2.3 %copy-start.2 = (bf16[4,1600,128]{2,1,0:T(8,128)(2,1)S(1)}, bf16[4,1600,128]{2,1,0:T(8,128)(2,1)}, u32[]{:S(2)}) copy-start(bf16[4,1600,128]{2,1,0:T(8,128)(2,1)} %get-tuple-element.41.rest_0_) | copy-start | bytes 4915204
  25.5 2.7 %collective-permute-start = (f32[8,256,128]{2,1,0:T(8,128)S(1)}, f32[8,256,128]{2,1,0:T(8,128)S(1)}, u32[]{:S(2)}, u32[]{:S(2)}) collective-permute-start(f32[8,256,128]{2,1,0:T(8,128)S(1)} %project.7), channel_id=1, source_target_pairs={{0,1},{1,0},{2,3},{3,2},{4,5},{5,4},{6,7},{7,6},{8,9},{9,8},{10,11... | collective-permute-start | bytes 3145736 | tf_op jit(solution)/shard_map/ppermute | solution.py:23
  25.7 12.1 %collective-permute-start.1 = (bf16[128,1600]{1,0:T(8,128)(2,1)S(1)}, bf16[128,1600]{1,0:T(8,128)(2,1)S(1)}, u32[]{:S(2)}, u32[]{:S(2)}) collective-permute-start(bf16[128,1600]{1,0:T(8,128)(2,1)S(1)} %bitcast.11), channel_id=1, source_target_pairs={{0,16},{16,0},{1,17},{17,1},{2,18},{18,2},{3,19},{19,3},{4,20},{20... | collective-permute-start | bytes 1228808 | tf_op jit(solution)/shard_map/ppermute | solution.py:411
  28.6 9.7 %copy-start.5 = (bf16[2,1600,128]{2,1,0:T(8,128)(2,1)S(1)}, bf16[2,1600,128]{2,1,0:T(8,128)(2,1)}, u32[]{:S(2)}) copy-start(bf16[2,1600,128]{2,1,0:T(8,128)(2,1)} %copy-done.3) | copy-start | bytes 2457604
  28.6 9.2 %collective-permute-start.2 = (s32[584,128]{1,0:T(8,128)S(1)}, s32[584,128]{1,0:T(8,128)S(1)}, u32[]{:S(2)}, u32[]{:S(2)}) collective-permute-start(s32[584,128]{1,0:T(8,128)S(1)} %merge.4), channel_id=1, source_target_pairs={{0,2},{1,3},{2,0},{3,1},{4,6},{5,7},{6,4},{7,5},{8,10},{9,11},{10,... | collective-permute-start | bytes 897032 | tf_op jit(solution)/shard_map/ppermute | solution.py:23
  38.2 2.0 %collective-permute-start.3 = (f32[4,256,128]{2,1,0:T(8,128)S(1)}, f32[4,256,128]{2,1,0:T(8,128)S(1)}, u32[]{:S(2)}, u32[]{:S(2)}) collective-permute-start(f32[4,256,128]{2,1,0:T(8,128)S(1)} %project.9), channel_id=1, source_target_pairs={{0,1},{1,0},{2,3},{3,2},{4,5},{5,4},{6,7},{7,6},{8,9},{9,8},{10,11... | collective-permute-start | bytes 1572872 | tf_op jit(solution)/shard_map/ppermute | solution.py:23
  38.7 8.3 %collective-permute-start.7 = (f32[4,256,128]{2,1,0:T(8,128)S(1)}, f32[4,256,128]{2,1,0:T(8,128)S(1)}, u32[]{:S(2)}, u32[]{:S(2)}) collective-permute-start(f32[4,256,128]{2,1,0:T(8,128)S(1)} %project.11), channel_id=1, source_target_pairs={{0,1},{1,0},{2,3},{3,2},{4,5},{5,4},{6,7},{7,6},{8,9},{9,8},{10,11... | collective-permute-start | bytes 1572872 | tf_op jit(solution)/shard_map/ppermute | solution.py:23
  40.6 9.2 %collective-permute-start.8 = (s32[584,128]{1,0:T(8,128)S(1)}, s32[584,128]{1,0:T(8,128)S(1)}, u32[]{:S(2)}, u32[]{:S(2)}) collective-permute-start(s32[584,128]{1,0:T(8,128)S(1)} %merge.5), channel_id=1, source_target_pairs={{0,2},{1,3},{2,0},{3,1},{4,6},{5,7},{6,4},{7,5},{8,10},{9,11},{10,... | collective-permute-start | bytes 897032 | tf_op jit(solution)/shard_map/ppermute | solution.py:23
  42.1 17.0 %copy-start.7 = (f32[128,128]{1,0:T(8,128)S(1)}, f32[128,128]{1,0:T(8,128)}, u32[]{:S(2)}) copy-start(f32[128,128]{1,0:T(8,128)} %copy-done.6) | copy-start | bytes 196612
  42.1 10.5 %collective-permute-start.4 = (s32[152,128]{1,0:T(8,128)S(1)}, s32[152,128]{1,0:T(8,128)S(1)}, u32[]{:S(2)}, u32[]{:S(2)}) collective-permute-start(s32[152,128]{1,0:T(8,128)S(1)} %get-tuple-element.50), channel_id=1, source_target_pairs={{0,12},{1,13},{2,14},{3,15},{4,8},{5,9},{6,10},{7,11},{8,4},{9,5},... | collective-permute-start | bytes 233480 | tf_op jit(solution)/shard_map/ppermute | solution.py:23
  44.7 10.1 %collective-permute-start.5 = (s32[152,128]{1,0:T(8,128)S(1)}, s32[152,128]{1,0:T(8,128)S(1)}, u32[]{:S(2)}, u32[]{:S(2)}) collective-permute-start(s32[152,128]{1,0:T(8,128)S(1)} %get-tuple-element.51), channel_id=1, source_target_pairs={{0,8},{1,9},{2,10},{3,11},{4,12},{5,13},{6,14},{7,15},{8,0},{9,1},... | collective-permute-start | bytes 233480 | tf_op jit(solution)/shard_map/ppermute | solution.py:23
  45.4 9.4 %collective-permute-start.6 = (s32[152,128]{1,0:T(8,128)S(1)}, s32[152,128]{1,0:T(8,128)S(1)}, u32[]{:S(2)}, u32[]{:S(2)}) collective-permute-start(s32[152,128]{1,0:T(8,128)S(1)} %get-tuple-element.52), channel_id=1, source_target_pairs={{0,4},{1,5},{2,6},{3,7},{4,0},{5,1},{6,2},{7,3},{8,12},{9,13},{10,... | collective-permute-start | bytes 233480 | tf_op jit(solution)/shard_map/ppermute | solution.py:23
  50.3 7.6 %collective-permute-start.10 = (s32[152,128]{1,0:T(8,128)S(1)}, s32[152,128]{1,0:T(8,128)S(1)}, u32[]{:S(2)}, u32[]{:S(2)}) collective-permute-start(s32[152,128]{1,0:T(8,128)S(1)} %get-tuple-element.55), channel_id=1, source_target_pairs={{0,8},{1,9},{2,10},{3,11},{4,12},{5,13},{6,14},{7,15},{8,0},{9,1},... | collective-permute-start | bytes 233480 | tf_op jit(solution)/shard_map/ppermute | solution.py:23
  52.3 5.6 %collective-permute-start.11 = (s32[152,128]{1,0:T(8,128)S(1)}, s32[152,128]{1,0:T(8,128)S(1)}, u32[]{:S(2)}, u32[]{:S(2)}) collective-permute-start(s32[152,128]{1,0:T(8,128)S(1)} %get-tuple-element.56), channel_id=1, source_target_pairs={{0,4},{1,5},{2,6},{3,7},{4,0},{5,1},{6,2},{7,3},{8,12},{9,13},{10,... | collective-permute-start | bytes 233480 | tf_op jit(solution)/shard_map/ppermute | solution.py:23
  52.6 6.5 %collective-permute-start.9 = (s32[152,128]{1,0:T(8,128)S(1)}, s32[152,128]{1,0:T(8,128)S(1)}, u32[]{:S(2)}, u32[]{:S(2)}) collective-permute-start(s32[152,128]{1,0:T(8,128)S(1)} %get-tuple-element.54), channel_id=1, source_target_pairs={{0,12},{1,13},{2,14},{3,15},{4,8},{5,9},{6,10},{7,11},{8,4},{9,5},... | collective-permute-start | bytes 233480 | tf_op jit(solution)/shard_map/ppermute | solution.py:23
  59.9 3.1 %collective-permute-start.12 = (f32[16,128]{1,0:T(8,128)S(1)}, f32[16,128]{1,0:T(8,128)S(1)}, u32[]{:S(2)}, u32[]{:S(2)}) collective-permute-start(f32[16,128]{1,0:T(8,128)S(1)} %get-tuple-element.61.refs_0_.refs_5_), channel_id=1, source_target_pairs={{0,3},{1,2},{2,1},{3,0},{4,7},{5,6},{6,5},{7,4},{8,11},{9,10},{10,... | collective-permute-start | bytes 24584 | tf_op jit(solution)/shard_map/ppermute | solution.py:23
  59.9 3.7 %collective-permute-start.13 = (f32[16,128]{1,0:T(8,128)S(1)}, f32[16,128]{1,0:T(8,128)S(1)}, u32[]{:S(2)}, u32[]{:S(2)}) collective-permute-start(f32[16,128]{1,0:T(8,128)S(1)} %get-tuple-element.61.refs_0_.refs_5_), channel_id=1, source_target_pairs={{0,2},{1,3},{2,0},{3,1},{4,6},{5,7},{6,4},{7,5},{8,10},{9,11},{10,... | collective-permute-start | bytes 24584 | tf_op jit(solution)/shard_map/ppermute | solution.py:23
  61.2 2.4 %collective-permute-start.14 = (f32[16,128]{1,0:T(8,128)S(1)}, f32[16,128]{1,0:T(8,128)S(1)}, u32[]{:S(2)}, u32[]{:S(2)}) collective-permute-start(f32[16,128]{1,0:T(8,128)S(1)} %get-tuple-element.61.refs_0_.refs_5_), channel_id=1, source_target_pairs={{0,1},{1,0},{2,3},{3,2},{4,5},{5,4},{6,7},{7,6},{8,9},{9,8},{10,11... | collective-permute-start | bytes 24584 | tf_op jit(solution)/shard_map/ppermute | solution.py:23
  63.7 5.5 %collective-permute-start.15 = (f32[16,128]{1,0:T(8,128)S(1)}, f32[16,128]{1,0:T(8,128)S(1)}, u32[]{:S(2)}, u32[]{:S(2)}) collective-permute-start(f32[16,128]{1,0:T(8,128)S(1)} %get-tuple-element.62.refs_0_), channel_id=1, source_target_pairs={{0,12},{1,13},{2,14},{3,15},{4,8},{5,9},{6,10},{7,11},{8,4},{9,5},... | collective-permute-start | bytes 24584 | tf_op jit(solution)/shard_map/ppermute | solution.py:23
  65.8 4.5 %collective-permute-start.16 = (f32[16,128]{1,0:T(8,128)S(1)}, f32[16,128]{1,0:T(8,128)S(1)}, u32[]{:S(2)}, u32[]{:S(2)}) collective-permute-start(f32[16,128]{1,0:T(8,128)S(1)} %get-tuple-element.62.refs_0_), channel_id=1, source_target_pairs={{0,8},{1,9},{2,10},{3,11},{4,12},{5,13},{6,14},{7,15},{8,0},{9,1},... | collective-permute-start | bytes 24584 | tf_op jit(solution)/shard_map/ppermute | solution.py:23
  66.6 3.8 %collective-permute-start.17 = (f32[16,128]{1,0:T(8,128)S(1)}, f32[16,128]{1,0:T(8,128)S(1)}, u32[]{:S(2)}, u32[]{:S(2)}) collective-permute-start(f32[16,128]{1,0:T(8,128)S(1)} %get-tuple-element.62.refs_0_), channel_id=1, source_target_pairs={{0,4},{1,5},{2,6},{3,7},{4,0},{5,1},{6,2},{7,3},{8,12},{9,13},{10,... | collective-permute-start | bytes 24584 | tf_op jit(solution)/shard_map/ppermute | solution.py:23
